TPU v7x, 32 devices: a whole 2x2x4 slice. The times are simulated.
32 devices in a mesh: tm: 4 (over y, x), sta: 8 (over z, core).
Axes of the slice: x: 2, y: 2, z: 4, core: 2. Of those that a mesh axis runs over, the one named last changes fastest.
Arguments:
- templates: bfloat16 [4, 256, 8, 3, 600], P('tm', None, 'sta'), may hold values from -6 to 6
- channel_mask: int32 [4, 256, 8], P('tm', None, 'sta'), may hold values 0 or 1
- waveforms: bfloat16 [8, 3, 3584], P('sta', None, 'tm'), may hold values from -60 to 60
- waveform_tail: bfloat16 [8, 3, 599], P('sta'), may hold values from -6 to 6
Outputs:
- detections: float32 [4, 256, 3584], P(None, 'sta', 'tm')
All inputs are finite; a program needn't handle non-finite values. No bound on the sum of `channel_mask` on one device may be relied on, other than what follows from the above.
Results may differ from a plain program's by a relative error of at most 0.0044.
Values may be sent and summed in bfloat16 or wider, within the bound.
No kernel may reach another device: no remote copies, remote signals or barrier semaphores. Data moves between devices by JAX's collectives and lax.ppermute only.
A program may use at most 128 MiB of HBM per device.

v0:
```python
import jax
import jax.numpy as jnp
from jax import lax
from jax.sharding import PartitionSpec as P


def from_behind(x, axis, by):
    size = lax.axis_size(axis)
    pairs = [(i, i + by) for i in range(size) if 0 <= i + by < size]
    return lax.ppermute(x, axis, pairs)


def from_behind_2(x, axis, by):
    size = lax.axis_size(axis)
    return lax.ppermute(x, axis, [(i, (i + by) % size) for i in range(size)])


def normalize(templates, channel_mask):
    values = templates.astype(jnp.float32)
    centred = values - jnp.mean(values, axis=-1, keepdims=True)
    energy = jnp.sum(centred * centred, axis=-1, keepdims=True)
    weighted = (
        centred * lax.rsqrt(energy + 1e-05) * channel_mask.astype(jnp.float32)[..., None, None]
    )
    return weighted.astype(jnp.bfloat16)


def windows(extended, length, sample_count):
    values = extended.astype(jnp.float32)
    zero_col = jnp.zeros(values.shape[:-1] + (1,), jnp.float32)
    prefix_one = jnp.concatenate([zero_col, jnp.cumsum(values, axis=-1)], axis=-1)
    prefix_two = jnp.concatenate([zero_col, jnp.cumsum(values * values, axis=-1)], axis=-1)
    window_sum = prefix_one[..., length : length + sample_count] - prefix_one[..., :sample_count]
    window_square = prefix_two[..., length : length + sample_count] - prefix_two[..., :sample_count]
    inverse = lax.rsqrt(window_square - window_sum * window_sum / length + 1e-05)
    span = extended.shape[-1]
    leading = extended.shape[:-1]
    copies = jnp.broadcast_to(extended[..., None, :], leading + (length + 1, span))
    flat = copies.reshape(leading + ((length + 1) * span,))
    hankel = flat[..., : length * (span + 1)].reshape(leading + (length, span + 1))[
        ..., :sample_count
    ]
    return (hankel.astype(jnp.float32) * inverse[..., None, :]).astype(jnp.bfloat16)


def stacked(tpl_block, scaled):
    return lax.psum_scatter(
        jnp.dot(tpl_block, scaled, preferred_element_type=jnp.float32),
        "sta",
        scatter_dimension=0,
        tiled=True,
    )


def per_device(templates, channel_mask, waveforms, waveform_tail):
    length = templates.shape[-1]
    sample_count = waveforms.shape[-1]
    tm_count = lax.axis_size("tm")
    sta_count = lax.axis_size("sta")
    tm_index = lax.axis_index("tm")
    normed = normalize(templates, channel_mask)[0]
    tpl_rows = normed.shape[0]
    tpl_flat = normed.reshape(tpl_rows, -1)
    own_rows = tpl_rows // sta_count
    following = from_behind(waveforms[:, :, : length - 1], "tm", -1)
    following = jnp.where(tm_index == tm_count - 1, waveform_tail, following)
    extended = jnp.concatenate([waveforms, following], axis=-1)
    scaled = windows(extended, length, sample_count).reshape(-1, sample_count)
    result = jnp.zeros((tm_count, own_rows, sample_count), jnp.float32)
    tpl_block = tpl_flat
    for turn_index in range(tm_count):
        if turn_index > 0:
            tpl_block = from_behind_2(tpl_block, "tm", 1)
        anchor = (tm_index - turn_index) % tm_count
        result = lax.dynamic_update_index_in_dim(result, stacked(tpl_block, scaled), anchor, 0)
    return result


def solution(mesh):
    placed = (
        P("tm", None, "sta", None, None),
        P("tm", None, "sta"),
        P("sta", None, "tm"),
        P("sta", None, None),
    )
    return jax.shard_map(
        per_device, mesh=mesh, in_specs=placed, out_specs=P(None, "sta", "tm"), check_vma=False
    )
```

profile of v0, /device:TPU:0, one launch (start us, length us, event | category | flops | bytes accessed | tf_op | source)
XLA Modules:
  0.0 224.0 jit_solution(4949666293945741692)
XLA Ops:
  6.5 0.8 slice.41
  7.3 1.3 collective-permute-start
  8.6 1.3 convert_reduce_fusion
  9.9 1.4 fusion.2
  11.4 0.7 convert_element_type.31
  12.1 2.4 %fusion.4 = bf16[1,256,1,3,600]{1,4,3,2,0:T(8,128)(2,1)} fusion(bf16[1,256,1,3,600]{1,4,3,2,0:T(8,128)(2,1)} %param.4, f32[256]{0:T(256)S(1)} %bitcast.51, f32[256,3]{0,1:T(4,128)S(1)} %add_rsqrt_fusion.1, f32[256,3]{0,1:T(4,128)S(1)} %broadcast_multiply_fusion), kind=kLoop, calls=%fused_computation.7 | loop fusion | flops 2304000 | bytes 1850368 | tf_op jit(solution)/shard_map/convert_element_type | solution.py:25
  14.5 0.9 reduce-window.16
  15.4 0.2 slice_reduce_fusion
  15.7 0.9 reduce-window.14
  16.5 0.2 slice_reduce_fusion.1
  16.7 0.6 reduce-window.19
  17.3 0.1 broadcast.49
  17.4 0.6 reduce-window.15
  18.0 0.1 broadcast.48
  18.2 0.2 add_rsqrt_fusion
  18.3 2.8 %broadcast_in_dim.32 = bf16[3,601,1495]{2,1,0:T(8,128)(2,1)} broadcast(bf16[3,1495]{1,0:T(4,128)(2,1)S(1)} %get-tuple-element.6), dimensions={0,2} | broadcast | bytes 5399940 | tf_op jit(solution)/shard_map/broadcast_in_dim | solution.py:38
  21.2 16.4 %reshape.173 = bf16[2695485]{0:T(1024)(128)(2,1)} reshape(bf16[3,601,1495]{2,1,0:T(8,128)(2,1)} %broadcast_in_dim.32) | data formatting | bytes 10781940
  37.6 8.8 %broadcast_in_dim.33 = bf16[1,3,898495]{2,1,0:T(4,128)(2,1)} reshape(bf16[2695485]{0:T(1024)(128)(2,1)} %reshape.173) | data formatting | bytes 10781940 | tf_op jit(solution)/shard_map/broadcast_in_dim | solution.py:38
  46.3 7.3 %slice.54 = bf16[1,3,897600]{2,1,0:T(4,128)(2,1)} slice(bf16[1,3,898495]{2,1,0:T(4,128)(2,1)} %broadcast_in_dim.33), slice={[0:1], [0:3], [0:897600]} | slice | bytes 10771200 | tf_op jit(solution)/shard_map/slice | solution.py:40
  53.7 12.4 %reshape.175 = bf16[2692800]{0:T(1024)(128)(2,1)} reshape(bf16[1,3,897600]{2,1,0:T(4,128)(2,1)} %slice.54) | data formatting | bytes 10771200
  66.0 11.8 %reshape.157 = bf16[1,3,600,1496]{3,2,1,0:T(8,128)(2,1)} reshape(bf16[2692800]{0:T(1024)(128)(2,1)} %reshape.175) | data formatting | bytes 10771200 | tf_op jit(solution)/shard_map/reshape | solution.py:40
  77.8 2.6 %multiply_convert_fusion = bf16[1,3,600,896]{3,2,1,0:T(8,128)(2,1)S(1)} fusion(bf16[1,3,600,1496]{3,2,1,0:T(8,128)(2,1)} %reshape.157, f32[3,896]{1,0:T(4,128)S(1)} %bitcast.46), kind=kLoop, calls=%fused_computation | loop fusion | flops 4838400 | bytes 6461952 | tf_op jit(solution)/shard_map/convert_element_type | solution.py:43
  80.5 2.2 %fusion.11 = f32[256,896]{1,0:T(8,128)} fusion(bf16[256,1800]{0,1:T(8,128)(2,1)S(1)} %bitcast.41, bf16[1800,896]{1,0:T(8,128)(2,1)S(1)} %bitcast.36), kind=kOutput, calls=%fused_computation.31 | convolution fusion | flops 825753600 | bytes 5064704 | tf_op jit(solution)/shard_map/dot_general | solution.py:48
  82.7 0.0 reduce-scatter.5.cloned.1.call-update
  82.7 0.0 reduce-scatter.7.cloned.1.call-start
  82.8 3.6 %collective-permute-start.1 = (bf16[256,1800]{0,1:T(8,128)(2,1)}, bf16[256,1800]{0,1:T(8,128)(2,1)S(1)}, u32[]{:S(2)}, u32[]{:S(2)}) collective-permute-start(bf16[256,1800]{0,1:T(8,128)(2,1)} %bitcast.40), channel_id=1, source_target_pairs={{0,8},{8,16},{16,24},{24,0},{1,9},{9,17},{17,25},{25,1},{2,10},{10... | collective-permute-start | bytes 2764808 | tf_op jit(solution)/shard_map/ppermute | solution.py:15
  86.4 21.8 %collective-permute-done.1 = bf16[256,1800]{0,1:T(8,128)(2,1)S(1)} collective-permute-done((bf16[256,1800]{0,1:T(8,128)(2,1)}, bf16[256,1800]{0,1:T(8,128)(2,1)S(1)}, u32[]{:S(2)}, u32[]{:S(2)}) %collective-permute-start.1) | collective-permute-done | bytes 921632 | tf_op jit(solution)/shard_map/ppermute | solution.py:15
  108.2 0.9 copy-done.4
  109.2 2.2 fusion.12
  111.4 0.0 reduce-scatter.7.cloned.1.call-update
  111.4 0.0 reduce-scatter.9.cloned.1.call-start
  111.5 0.9 collective-permute-start.2
  112.3 21.6 %collective-permute-done.2 = bf16[256,1800]{0,1:T(8,128)(2,1)S(1)} collective-permute-done((bf16[256,1800]{0,1:T(8,128)(2,1)}, bf16[256,1800]{0,1:T(8,128)(2,1)S(1)}, u32[]{:S(2)}, u32[]{:S(2)}) %collective-permute-start.2) | collective-permute-done | bytes 921632 | tf_op jit(solution)/shard_map/ppermute | solution.py:15
  133.9 0.9 copy-done.5
  134.8 2.2 fusion.13
  137.0 0.0 reduce-scatter.9.cloned.1.call-update
  137.1 0.0 reduce-scatter.11.cloned.1.call-start
  137.1 0.5 collective-permute-start.3
  137.7 21.0 %collective-permute-done.3 = bf16[256,1800]{0,1:T(8,128)(2,1)S(1)} collective-permute-done((bf16[256,1800]{0,1:T(8,128)(2,1)}, bf16[256,1800]{0,1:T(8,128)(2,1)S(1)}, u32[]{:S(2)}, u32[]{:S(2)}) %collective-permute-start.3) | collective-permute-done | bytes 921632 | tf_op jit(solution)/shard_map/ppermute | solution.py:15
  158.7 2.2 fusion.14
  160.9 0.0 reduce-scatter.5.cloned.1.call-done
  161.0 0.9 bitcast_dynamic-update-slice_fusion.3
  161.9 0.0 reduce-scatter.7.cloned.1.call-done
  162.0 0.9 bitcast_dynamic-update-slice_fusion.2
  162.9 20.6 %reduce-scatter.9.cloned.1.call-done = f32[32,896]{1,0:T(8,128)} async-done(((f32[256,896]{1,0:T(8,128)}), f32[32,896]{1,0:T(8,128)}) %reduce-scatter.9.cloned.1.call-update) | async-done | bytes 114704 | tf_op jit(solution)/shard_map/reduce_scatter | solution.py:47
  183.5 0.9 bitcast_dynamic-update-slice_fusion.1
  184.4 31.5 %reduce-scatter.11.cloned.1.call-done = f32[32,896]{1,0:T(8,128)} async-done(((f32[256,896]{1,0:T(8,128)}), f32[32,896]{1,0:T(8,128)}) %reduce-scatter.11.cloned.1.call-update) | async-done | bytes 114704 | tf_op jit(solution)/shard_map/reduce_scatter | solution.py:47
  215.9 1.6 bitcast_dynamic-update-slice_fusion
  (34 shorter events, 0.3 us)
Async XLA Ops:
  6.5 7.9 %copy-start.2 = (bf16[1,3,896]{2,1,0:T(4,128)(2,1)S(1)}, bf16[1,3,896]{2,1,0:T(4,128)(2,1)}, u32[]{:S(2)}) copy-start(bf16[1,3,896]{2,1,0:T(4,128)(2,1)} %param.6) | copy-start | bytes 16132
  6.5 7.9 %copy-start.3 = (bf16[1,3,599]{2,1,0:T(4,128)(2,1)S(1)}, bf16[1,3,599]{2,1,0:T(4,128)(2,1)}, u32[]{:S(2)}) copy-start(bf16[1,3,599]{2,1,0:T(4,128)(2,1)} %param.7) | copy-start | bytes 10786
  6.5 154.4 %reduce-scatter.5.cloned.1.call-start = ((), (), s32[]{:S(2)}) async-start(), calls=%async_computation.4 | async-start | bytes 1032192 | tf_op jit(solution)/shard_map/reduce_scatter | solution.py:47
  7.3 7.2 %collective-permute-start = (bf16[1,3,599]{2,1,0:T(4,128)(2,1)S(1)}, bf16[1,3,599]{2,1,0:T(4,128)(2,1)S(1)}, u32[]{:S(2)}, u32[]{:S(2)}) collective-permute-start(bf16[1,3,599]{2,1,0:T(4,128)(2,1)S(1)} %slice.41), channel_id=1, source_target_pairs={{8,0},{16,8},{24,16},{9,1},{17,9},{25,17},{10,2},{18,10},{26,18},{... | collective-permute-start | bytes 10790 | tf_op jit(solution)/shard_map/ppermute | solution.py:10
  77.8 2.6 %copy-start = (bf16[1,256,1,3,600]{1,4,3,2,0:T(8,128)(2,1)S(1)}, bf16[1,256,1,3,600]{1,4,3,2,0:T(8,128)(2,1)}, u32[]{:S(2)}) copy-start(bf16[1,256,1,3,600]{1,4,3,2,0:T(8,128)(2,1)} %fusion.4) | copy-start | bytes 2764804
  82.7 79.2 %reduce-scatter.7.cloned.1.call-start = ((), (), s32[]{:S(2)}) async-start(), calls=%async_computation.5 | async-start | bytes 1032192 | tf_op jit(solution)/shard_map/reduce_scatter | solution.py:47
  82.8 25.5 %collective-permute-start.1 = (bf16[256,1800]{0,1:T(8,128)(2,1)}, bf16[256,1800]{0,1:T(8,128)(2,1)S(1)}, u32[]{:S(2)}, u32[]{:S(2)}) collective-permute-start(bf16[256,1800]{0,1:T(8,128)(2,1)} %bitcast.40), channel_id=1, source_target_pairs={{0,8},{8,16},{16,24},{24,0},{1,9},{9,17},{17,25},{25,1},{2,10},{10... | collective-permute-start | bytes 2764808 | tf_op jit(solution)/shard_map/ppermute | solution.py:15
  108.2 0.9 copy-start.4
  111.4 72.1 %reduce-scatter.9.cloned.1.call-start = ((), (), s32[]{:S(2)}) async-start(), calls=%async_computation.6 | async-start | bytes 1032192 | tf_op jit(solution)/shard_map/reduce_scatter | solution.py:47
  111.5 22.5 %collective-permute-start.2 = (bf16[256,1800]{0,1:T(8,128)(2,1)}, bf16[256,1800]{0,1:T(8,128)(2,1)S(1)}, u32[]{:S(2)}, u32[]{:S(2)}) collective-permute-start(bf16[256,1800]{0,1:T(8,128)(2,1)} %copy-done.4), channel_id=1, source_target_pairs={{0,8},{8,16},{16,24},{24,0},{1,9},{9,17},{17,25},{25,1},{2,10},{10... | collective-permute-start | bytes 2764808 | tf_op jit(solution)/shard_map/ppermute | solution.py:15
  133.9 0.9 copy-start.5
  137.1 78.8 %reduce-scatter.11.cloned.1.call-start = ((), (), s32[]{:S(2)}) async-start(), calls=%async_computation.7 | async-start | bytes 1032192 | tf_op jit(solution)/shard_map/reduce_scatter | solution.py:47
  137.1 21.5 %collective-permute-start.3 = (bf16[256,1800]{0,1:T(8,128)(2,1)}, bf16[256,1800]{0,1:T(8,128)(2,1)S(1)}, u32[]{:S(2)}, u32[]{:S(2)}) collective-permute-start(bf16[256,1800]{0,1:T(8,128)(2,1)} %copy-done.5), channel_id=1, source_target_pairs={{0,8},{8,16},{16,24},{24,0},{1,9},{9,17},{17,25},{25,1},{2,10},{10... | collective-permute-start | bytes 2764808 | tf_op jit(solution)/shard_map/ppermute | solution.py:15
  184.4 31.5 %copy-start.1 = (f32[4,32,896]{2,1,0:T(8,128)}, f32[4,32,896]{2,1,0:T(8,128)S(1)}, u32[]{:S(2)}) copy-start(f32[4,32,896]{2,1,0:T(8,128)S(1)} %bitcast_dynamic-update-slice_fusion.1) | copy-start | bytes 1376260
Sparse Core Ops, SparseCore 0:
  82.8 35.6 reduce-scatter.4
  120.9 29.9 reduce-scatter.6
  153.2 30.2 reduce-scatter.8
  185.8 30.1 reduce-scatter.10
where the time goes:
time: 225 us; the launch traced here: 224 us
  waiting for transfers between devices  117 us (52%)
  local copies, waits for them, and re-layouts  67 us (30%)
  between operations  13.4 us (6%)
  other arithmetic  11.6 us (5%)
  matrix products  8.86 us (4%)
  starting transfers between devices  6.41 us (3%)
    ppermute x3, waiting for transfers between devices, from_behind_2(): return lax.ppermute(x, axis, [(i, (i + by) % size) for i in range(size)])  64.4 us
    reduce_scatter x4, waiting for transfers between devices, stacked(): lax.psum_scatter(jnp.dot(tpl_block, scaled, preferred_element_type=jnp.fl...  52.1 us
    unnamed x17, local copies, waits for them, and re-layouts  30.6 us
    reshape x1, local copies, waits for them, and re-layouts, windows(): flat[..., :length * (span + 1)].reshape(leading + (length, span + 1))  11.8 us
    broadcast_in_dim x2, local copies, waits for them, and re-layouts, windows(): jnp.broadcast_to(extended[..., None, :], leading + (length + 1, span))  11.6 us
    dot_general x4, matrix products, stacked(): jnp.dot(tpl_block, scaled, preferred_element_type=jnp.float32)  8.86 us
    slice x1, local copies, waits for them, and re-layouts, windows(): flat[..., :length * (span + 1)].reshape(leading + (length, span + 1))  7.33 us
    ppermute x3, starting transfers between devices, from_behind_2(): return lax.ppermute(x, axis, [(i, (i + by) % size) for i in range(size)])  5.01 us
  transfers between devices with their start and end apart: 8, of which 5 were waited for; matrix products, arithmetic and copies ran while one was open for 7% of the time, Pallas kernels for 0%

commit v1 on v0

v1 whole, which is shorter than its diff:
```python
import functools
import jax
import jax.numpy as jnp
from jax import lax
from jax.experimental import pallas as pl
from jax.experimental.pallas import tpu as pltpu
from jax.sharding import PartitionSpec as P

F32 = jnp.float32
BF16 = jnp.bfloat16
LANES = 128
VMEM = pl.BlockSpec(memory_space=pltpu.VMEM)
SMEM = pl.BlockSpec(memory_space=pltpu.SMEM)


def params(limit_mib):
    return pltpu.CompilerParams(vmem_limit_bytes=limit_mib << 20)


def up(value, multiple):
    return (value + multiple - 1) // multiple * multiple


def swap_with(x, axis, offset):
    size = lax.axis_size(axis)
    return lax.ppermute(x, axis, [(i, i ^ offset) for i in range(size)])


def pack_kernel(chips, rows, length, place_ref, tpl_ref, mask_ref, wave_ref, tail_ref, *out_refs):
    tpl_outs, wave_out = out_refs[:chips], out_refs[chips]
    folds = LANES // rows
    fold_lags = tpl_outs[0].shape[1]
    samples = wave_ref.shape[-1]
    wave_out[...] = jnp.zeros_like(wave_out)
    wave_out[:, :samples] = wave_ref[...]
    wave_out[:, samples : samples + tail_ref.shape[-1]] = tail_ref[...]
    lane = lax.broadcasted_iota(jnp.int32, (1, LANES), 1)
    for offset in range(chips):
        target = place_ref[0] ^ offset
        tile = pl.multiple_of((target * rows) // LANES * LANES, LANES)
        start = (target * rows) % LANES
        mask = mask_ref[:, pl.ds(tile, LANES)].astype(F32)
        for comp in range(tpl_ref.shape[0]):
            values = tpl_ref[comp, :, pl.ds(tile, LANES)].astype(F32) * mask
            folded = jnp.zeros((fold_lags, LANES), F32)
            for fold in range(folds):
                piece = values[fold * fold_lags : min((fold + 1) * fold_lags, length)]
                if piece.shape[0] == 0:
                    continue
                if piece.shape[0] < fold_lags:
                    piece = jnp.concatenate(
                        [piece, jnp.zeros((fold_lags - piece.shape[0], LANES), F32)], axis=0
                    )
                turned = pltpu.roll(piece, (fold * rows - start + LANES) % LANES, 1)
                here = (lane >= fold * rows) & (lane < (fold + 1) * rows)
                folded = jnp.where(here, turned, folded)
            tpl_outs[offset][comp] = folded.astype(BF16)


def pack(place, tpl, mask, wave, tail, chips):
    comps, length, all_rows = tpl.shape
    rows = all_rows // chips
    fold_lags = up(-(-length // (LANES // rows)), 16)
    shapes = [jax.ShapeDtypeStruct((comps, fold_lags, LANES), BF16)] * chips
    shapes.append(jax.ShapeDtypeStruct((comps, up(wave.shape[-1] + tail.shape[-1], LANES)), BF16))
    return pl.pallas_call(
        functools.partial(pack_kernel, chips, rows, length),
        out_shape=shapes,
        in_specs=[SMEM] + [VMEM] * 4,
        out_specs=[VMEM] * len(shapes),
        compiler_params=params(16),
    )(place, tpl, mask, wave, tail)


def wave_kernel(shards, chips, length, halo, place_ref, *refs):
    shard_refs, tail_refs = refs[:shards], refs[shards : shards + chips]
    ext_ref, inv_ref = refs[shards + chips :]
    comps, samples = shard_refs[0].shape[1:]
    total = inv_ref.shape[-1]
    width = ext_ref.shape[-1]
    ext_ref[...] = jnp.zeros_like(ext_ref)
    for chip in range(chips):
        for offset in range(shards):
            at = pl.multiple_of((place_ref[1] ^ offset) * samples, LANES)
            ext_ref[chip * comps : (chip + 1) * comps, pl.ds(at, samples)] = shard_refs[offset][chip].astype(F32)
        ext_ref[chip * comps : (chip + 1) * comps, total : total + halo] = tail_refs[chip][
            :, samples : samples + halo
        ].astype(F32)

    def window(values):
        result, done, span, doubled = None, 0, 1, values
        while span <= length:
            if length & span:
                part = doubled if done == 0 else pltpu.roll(doubled, width - done, 1)
                result = part if result is None else result + part
                done += span
            span *= 2
            if span <= length:
                doubled = doubled + pltpu.roll(doubled, width - span // 2, 1)
        return result[:, :total]

    values = ext_ref[...]
    window_sum = window(values)
    window_square = window(values * values)
    inv_ref[...] = lax.rsqrt(window_square - window_sum * window_sum / length + 1e-05)


def wave_windows(place, shards, tails, length, halo):
    chips, comps, samples = shards[0].shape
    total = samples * len(shards)
    width = total + up(length, LANES)
    return pl.pallas_call(
        functools.partial(wave_kernel, len(shards), chips, length, halo),
        out_shape=[
            jax.ShapeDtypeStruct((chips * comps, width), F32),
            jax.ShapeDtypeStruct((chips * comps, total), F32),
        ],
        in_specs=[SMEM] + [VMEM] * (len(shards) + chips),
        out_specs=[VMEM] * 2,
        compiler_params=params(24),
    )(place, *shards, *tails)


def normed_rows(values, rows, length):
    fold_lags = values.shape[0]
    folds = LANES // rows

    def over_folds(total):
        span = rows
        while span < LANES:
            total = total + pltpu.roll(total, span, 1)
            span *= 2
        return total

    lane = lax.broadcasted_iota(jnp.int32, values.shape, 1)
    lag = lax.broadcasted_iota(jnp.int32, values.shape, 0) + lane // rows * fold_lags
    mean = over_folds(jnp.sum(values, axis=0, keepdims=True)) / length
    centred = jnp.where(lag < length, values - mean, 0.0)
    energy = over_folds(jnp.sum(centred * centred, axis=0, keepdims=True))
    weighted = centred * lax.rsqrt(energy + 1e-05)
    parts = [weighted] + [pltpu.roll(weighted, LANES - fold * rows, 1) for fold in range(1, folds)]
    return jnp.concatenate(parts, axis=0)


def piece_kernel(index, rows, length, tpl_ref, ext_ref, inv_ref, *refs):
    acc_ref, (out_ref, lags_ref, hankel_ref) = (refs[0] if len(refs) == 4 else None), refs[-3:]
    comps = tpl_ref.shape[0]
    width, total = ext_ref.shape[-1], inv_ref.shape[-1]
    blocks = up(-(-length // LANES), 2)
    flip = (
        lax.broadcasted_iota(jnp.int32, (LANES, LANES), 0)
        + lax.broadcasted_iota(jnp.int32, (LANES, LANES), 1)
        == LANES - 1
    ).astype(BF16)
    for comp in range(comps):
        spread = normed_rows(tpl_ref[comp].astype(F32), rows, length)[: blocks * LANES].astype(BF16)
        if spread.shape[0] < blocks * LANES:
            lags_ref[spread.shape[0] :, :] = jnp.zeros((blocks * LANES - spread.shape[0], LANES), BF16)
        lags_ref[: spread.shape[0], :] = spread
        turned = [
            lax.dot_general(
                lags_ref[block * LANES : (block + 1) * LANES, :],
                flip,
                (((0,), (0,)), ((), ())),
                preferred_element_type=F32,
            )[:rows].astype(BF16)
            for block in range(blocks)
        ]
        lhs = jnp.concatenate(
            [jnp.concatenate(turned[block : block + 2], axis=1) for block in range(0, blocks, 2)], axis=0
        )
        at = index * comps + comp
        row = jnp.broadcast_to(ext_ref[at : at + 1, :].astype(BF16), (LANES, width))
        hankel_ref[:, :width] = pltpu.roll(row, width - (LANES - 1), 1, stride=1, stride_axis=0)
        reach = total + (blocks - 2) * LANES
        rhs = jnp.concatenate([hankel_ref[:, :reach], hankel_ref[:, LANES : LANES + reach]], axis=0)
        product = jnp.dot(lhs, rhs, preferred_element_type=F32)
        gathered = product[:rows, :total]
        for split in range(1, blocks // 2):
            shift = split * 2 * LANES
            gathered = gathered + product[split * rows : (split + 1) * rows, shift : shift + total]
        gathered = gathered * inv_ref[at : at + 1, :]
        if comp == 0 and acc_ref is None:
            out_ref[...] = gathered
        elif comp == 0:
            out_ref[...] = acc_ref[...] + gathered
        else:
            out_ref[...] += gathered


def piece(index, rows, length, tpl, ext, inv, acc):
    total, width = inv.shape[-1], ext.shape[-1]
    blocks = up(-(-length // LANES), 2)
    inputs = [tpl, ext, inv] + ([] if acc is None else [acc])
    return pl.pallas_call(
        functools.partial(piece_kernel, index, rows, length),
        out_shape=jax.ShapeDtypeStruct((rows, total), F32),
        in_specs=[VMEM] * len(inputs),
        out_specs=VMEM,
        scratch_shapes=[
            pltpu.VMEM((blocks * LANES, LANES), BF16),
            pltpu.VMEM((LANES, up(width, LANES) + LANES), BF16),
        ],
        compiler_params=params(32),
        cost_estimate=pl.CostEstimate(
            flops=2 * rows * total * length * tpl.shape[0] * 3, bytes_accessed=tpl.size * 2, transcendentals=0
        ),
    )(*inputs)


def split_kernel(place_ref, acc_ref, keep_ref, send_ref):
    own = keep_ref.shape[0]
    at = pl.multiple_of(place_ref[2] * own, own)
    other = pl.multiple_of((1 - place_ref[2]) * own, own)
    keep_ref[...] = acc_ref[pl.ds(at, own), :]
    send_ref[...] = acc_ref[pl.ds(other, own), :].astype(BF16)


def split(place, acc):
    rows, total = acc.shape
    return pl.pallas_call(
        split_kernel,
        out_shape=[jax.ShapeDtypeStruct((rows // 2, total), F32), jax.ShapeDtypeStruct((rows // 2, total), BF16)],
        in_specs=[SMEM, VMEM],
        out_specs=[VMEM] * 2,
        compiler_params=params(16),
    )(place, acc)


def shard_kernel(place_ref, keep_ref, came_ref, own_ref, *send_refs):
    samples = own_ref.shape[-1]
    for offset, ref in enumerate((own_ref,) + send_refs):
        at = pl.multiple_of((place_ref[1] ^ offset) * samples, LANES)
        total = keep_ref[:, pl.ds(at, samples)] + came_ref[:, pl.ds(at, samples)].astype(F32)
        ref[...] = total.astype(ref.dtype)


def shard(place, keep, came, count):
    own, total = keep.shape
    samples = total // count
    return pl.pallas_call(
        shard_kernel,
        out_shape=[jax.ShapeDtypeStruct((own, samples), F32)]
        + [jax.ShapeDtypeStruct((own, samples), BF16)] * (count - 1),
        in_specs=[SMEM, VMEM, VMEM],
        out_specs=[VMEM] * count,
        compiler_params=params(16),
    )(place, keep, came)


def gather_kernel(place_ref, *refs):
    out_ref = refs[-1]
    for offset, ref in enumerate(refs[:-1]):
        out_ref[place_ref[1] ^ offset] = ref[...].astype(F32)


def gather(place, parts):
    own, samples = parts[0].shape
    return pl.pallas_call(
        gather_kernel,
        out_shape=jax.ShapeDtypeStruct((len(parts), own, samples), F32),
        in_specs=[SMEM] + [VMEM] * len(parts),
        out_specs=VMEM,
        compiler_params=params(16),
    )(place, *parts)


def per_device(templates, channel_mask, waveforms, waveform_tail):
    length = templates.shape[-1]
    samples = waveforms.shape[-1]
    halo = waveform_tail.shape[-1]
    tm_count = lax.axis_size("tm")
    chips = lax.axis_size("sta") // 2
    tm_index, sta_index = lax.axis_index("tm"), lax.axis_index("sta")
    place = jnp.stack([sta_index // 2, tm_index, sta_index % 2]).astype(jnp.int32)
    tpl = jnp.transpose(templates[0, :, 0], (1, 2, 0))
    mask = channel_mask[..., 0]
    rows = tpl.shape[-1] // chips
    packed = pack(place, tpl, mask, waveforms[0], waveform_tail[0], chips)
    messages, wave = packed[:chips], packed[chips]
    waves = [wave] + [swap_with(wave, "sta", 2 * offset) for offset in range(1, chips)]
    pieces = [messages[0]] + [swap_with(messages[offset], "sta", 2 * offset) for offset in range(1, chips)]
    stacked = jnp.stack([part[:, :samples] for part in waves])
    shards = [stacked] + [swap_with(stacked, "tm", offset) for offset in range(1, tm_count)]
    ext, inv = wave_windows(place, shards, waves, length, halo)
    acc = None
    for offset in range(chips):
        acc = piece(offset, rows, length, pieces[offset], ext, inv, acc)
    keep, send = split(place, acc)
    parts = shard(place, keep, swap_with(send, "sta", 1), tm_count)
    parts = [parts[0]] + [swap_with(parts[offset], "tm", offset) for offset in range(1, tm_count)]
    return gather(place, parts)


def solution(mesh):
    placed = (
        P("tm", None, "sta", None, None),
        P("tm", None, "sta"),
        P("sta", None, "tm"),
        P("sta", None, None),
    )
    return jax.shard_map(
        per_device, mesh=mesh, in_specs=placed, out_specs=P(None, "sta", "tm"), check_vma=False
    )
```

time: 225 us -> 56.2 us (0.25)
  waiting for transfers between devices: 117 us -> 19.9 us
  local copies, waits for them, and re-layouts: 67 us -> 1.89 us
  Pallas kernels: 0 us -> 17.6 us
  between operations: 13.4 us -> 0.11 us
  other arithmetic: 11.6 us -> 0.1 us
  starting transfers between devices: 6.41 us -> 16.4 us
  matrix products: 8.86 us -> 0 us
    reduce_scatter x4 -> x0, waiting for transfers between devices: 52.1 us -> none  [stacked(): lax.psum_scatter(jnp.dot(tpl_block, scaled, preferred_element_type=jnp.fl...]
    ppermute x4 -> x13, waiting for transfers between devices: 64.4 us -> 19.9 us  [swap_with(): return lax.ppermute(x, axis, [(i, i ^ offset) for i in range(size)])]
    unnamed x17 -> x8, local copies, waits for them, and re-layouts: 30.6 us -> 1.86 us
    pallas_call x0 -> x9, Pallas kernels: none -> 17.6 us  [the longest x4 11.8 us: piece(): pl.pallas_call(functools.partial(piece_kernel, index, rows, length), out_...]
    reshape x2 -> x0, local copies, waits for them, and re-layouts: 11.8 us -> none  [the longest x1 11.8 us: windows(): flat[..., :length * (span + 1)].reshape(leading + (length, span + 1))]
    broadcast_in_dim x3 -> x0, local copies, waits for them, and re-layouts: 11.6 us -> none  [the longest x2 11.6 us: windows(): jnp.broadcast_to(extended[..., None, :], leading + (length + 1, span))]
    ppermute x4 -> x13, starting transfers between devices: 6.29 us -> 16.4 us  [swap_with(): return lax.ppermute(x, axis, [(i, i ^ offset) for i in range(size)])]
    dot_general x4 -> x0, matrix products: 8.86 us -> none  [stacked(): jnp.dot(tpl_block, scaled, preferred_element_type=jnp.float32)]
  transfers between devices with their start and end apart: 8 -> 13, of which waited for: 5 -> 8; matrix products, arithmetic and copies ran while one was open for 7% -> 0% of each run, Pallas kernels for 0% -> 20%
where the time goes in v1:
time: 56.2 us; the launch traced here: 56.1 us
  waiting for transfers between devices  19.9 us (35%)
  Pallas kernels  17.6 us (31%)
  starting transfers between devices  16.4 us (29%)
  local copies, waits for them, and re-layouts  1.89 us (3%)
    ppermute x13, waiting for transfers between devices, swap_with(): return lax.ppermute(x, axis, [(i, i ^ offset) for i in range(size)])  19.9 us
    ppermute x13, starting transfers between devices, swap_with(): return lax.ppermute(x, axis, [(i, i ^ offset) for i in range(size)])  16.4 us
    pallas_call x4, Pallas kernels, piece(): pl.pallas_call(functools.partial(piece_kernel, index, rows, length), out_...  11.8 us
    pallas_call x1, Pallas kernels, wave_windows(): pl.pallas_call(functools.partial(wave_kernel, len(shards), chips, length,...  2.06 us
    unnamed x8, local copies, waits for them, and re-layouts  1.86 us
    pallas_call x1, Pallas kernels, gather(): pl.pallas_call(gather_kernel, out_shape=jax.ShapeDtypeStruct((len(parts),...  1.34 us
    pallas_call x1, Pallas kernels, pack(): pl.pallas_call(functools.partial(pack_kernel, chips, rows, length), out_s...  1.16 us
  transfers between devices with their start and end apart: 13, of which 8 were waited for; matrix products, arithmetic and copies ran while one was open for 0% of the time, Pallas kernels for 20%

profile of v1, /device:TPU:0, one launch (start us, length us, event | category | flops | bytes accessed | tf_op | source)
XLA Modules:
  0.0 56.1 jit_solution(14296815992056770211)
XLA Ops:
  0.0 0.0 copy-start.1
  0.0 0.0 copy-start.2
  0.0 0.1 pad_add_fusion.place_ref
  0.1 0.0 copy-start.3
  0.1 0.6 %copy-done.1 = bf16[1,3,896]{2,1,0:T(4,128)(2,1)S(1)} copy-done((bf16[1,3,896]{2,1,0:T(4,128)(2,1)S(1)}, bf16[1,3,896]{2,1,0:T(4,128)(2,1)}, u32[]{:S(2)}) %copy-start.1) | copy-done | bytes 5400
  0.7 0.0 copy-done.2
  0.7 0.1 copy-done.3
  0.8 0.0 copy-start
  0.8 1.2 %copy-done = bf16[1,256,1,3,600]{1,4,3,2,0:T(8,128)(2,1)S(1)} copy-done((bf16[1,256,1,3,600]{1,4,3,2,0:T(8,128)(2,1)S(1)}, bf16[1,256,1,3,600]{1,4,3,2,0:T(8,128)(2,1)}, u32[]{:S(2)}) %copy-start) | copy-done | bytes 921624
  1.9 1.2 %shard_map.46 = (bf16[3,304,128]{2,1,0:T(8,128)(2,1)S(1)}, bf16[3,304,128]{2,1,0:T(8,128)(2,1)S(1)}, bf16[3,304,128]{2,1,0:T(8,128)(2,1)S(1)}, bf16[3,304,128]{2,1,0:T(8,128)(2,1)S(1)}, bf16[3,1536]{1,0:T(4,128)(2,1)S(1)}) custom-call(s32[3]{0:T(128)S(1)} %pad_add_fusion.place_ref, bf16[3,600,256]{2,1,0:T(8,128)(2,1)S(1)} %bitcast.17, ...), custom_call_target="tpu_custom_call" | custom-call | tf_op jit(solution)/shard_map/pallas_call | solution.py:66
  3.1 5.1 %collective-permute-start.3 = (bf16[3,1536]{1,0:T(4,128)(2,1)S(1)}, bf16[3,1536]{1,0:T(4,128)(2,1)S(1)}, u32[]{:S(2)}, u32[]{:S(2)}) collective-permute-start(bf16[3,1536]{1,0:T(4,128)(2,1)S(1)} %get-tuple-element.19.refs_4_), channel_id=1, source_target_pairs={{0,6},{1,7},{2,4},{3,5},{4,2},{5,3},{6,0},{7,1},{8,14},{9,15},{10,... | collective-permute-start | bytes 27656 | tf_op jit(solution)/shard_map/ppermute | solution.py:26
  8.2 0.0 collective-permute-start.2
  8.2 0.6 %collective-permute-start.1 = (bf16[3,1536]{1,0:T(4,128)(2,1)S(1)}, bf16[3,1536]{1,0:T(4,128)(2,1)S(1)}, u32[]{:S(2)}, u32[]{:S(2)}) collective-permute-start(bf16[3,1536]{1,0:T(4,128)(2,1)S(1)} %get-tuple-element.19.refs_4_), channel_id=1, source_target_pairs={{0,2},{1,3},{2,0},{3,1},{4,6},{5,7},{6,4},{7,5},{8,10},{9,11},{10,... | collective-permute-start | bytes 27656 | tf_op jit(solution)/shard_map/ppermute | solution.py:26
  8.9 1.0 %collective-permute-done.3.refs_7_ = bf16[3,1536]{1,0:T(4,128)(2,1)S(1)} collective-permute-done((bf16[3,1536]{1,0:T(4,128)(2,1)S(1)}, bf16[3,1536]{1,0:T(4,128)(2,1)S(1)}, u32[]{:S(2)}, u32[]{:S(2)}) %collective-permute-start.3) | collective-permute-done | bytes 9248 | tf_op jit(solution)/shard_map/ppermute | solution.py:26
  9.9 2.9 %collective-permute-done.2.refs_6_ = bf16[3,1536]{1,0:T(4,128)(2,1)S(1)} collective-permute-done((bf16[3,1536]{1,0:T(4,128)(2,1)S(1)}, bf16[3,1536]{1,0:T(4,128)(2,1)S(1)}, u32[]{:S(2)}, u32[]{:S(2)}) %collective-permute-start.2) | collective-permute-done | bytes 9248 | tf_op jit(solution)/shard_map/ppermute | solution.py:26
  12.8 0.0 collective-permute-done.1.refs_5_
  12.9 2.5 %collective-permute-start.6 = (bf16[4,3,896]{2,1,0:T(4,128)(2,1)S(1)}, bf16[4,3,896]{2,1,0:T(4,128)(2,1)S(1)}, u32[]{:S(2)}, u32[]{:S(2)}) collective-permute-start(bf16[4,3,896]{2,1,0:T(4,128)(2,1)S(1)} %pad_maximum_fusion.refs_0_), channel_id=1, source_target_pairs={{0,24},{8,16},{16,8},{24,0},{1,25},{9,17},{17,9},{25,1},{2,26},{10... | collective-permute-start | bytes 64520 | tf_op jit(solution)/shard_map/ppermute | solution.py:26
  15.4 0.5 collective-permute-start.5
  15.9 0.5 collective-permute-start.4
  16.4 0.0 collective-permute-start.8
  16.4 3.5 %collective-permute-start = (bf16[3,304,128]{2,1,0:T(8,128)(2,1)S(1)}, bf16[3,304,128]{2,1,0:T(8,128)(2,1)S(1)}, u32[]{:S(2)}, u32[]{:S(2)}) collective-permute-start(bf16[3,304,128]{2,1,0:T(8,128)(2,1)S(1)} %get-tuple-element.18), channel_id=1, source_target_pairs={{0,6},{1,7},{2,4},{3,5},{4,2},{5,3},{6,0},{7,1},{8,14},{9,15},{10,... | collective-permute-start | bytes 700424 | tf_op jit(solution)/shard_map/ppermute | solution.py:26
  19.9 0.0 collective-permute-done.6.refs_3_
  19.9 0.0 collective-permute-start.7
  19.9 0.0 collective-permute-done.5.refs_2_
  19.9 0.0 collective-permute-done.4.refs_1_
  19.9 2.1 %shard_map.47 = (f32[12,4224]{1,0:T(8,128)S(1)}, f32[12,3584]{1,0:T(8,128)S(1)}) custom-call(s32[3]{0:T(128)S(1)} %pad_add_fusion.place_ref, bf16[4,3,896]{2,1,0:T(4,128)(2,1)S(1)} %pad_maximum_fusion.refs_0_, bf16[4,3,896]{2,1,0:T(4,128)(2,1)S(1)} %collective-permute-done.4.refs_1_, bf16[4,3,896]{2,1,0:T(4,128)(2,1)S(1)} %collective-permute-done.5.refs_2_, ...), custom_call_target="tpu_custom_call" | custom-call | tf_op jit(solution)/shard_map/pallas_call | solution.py:112
  22.0 2.9 %shard_map.48.refs_0_ = f32[64,3584]{1,0:T(8,128)S(1)} custom-call(bf16[3,304,128]{2,1,0:T(8,128)(2,1)S(1)} %get-tuple-element.24.tpl_ref, f32[12,4224]{1,0:T(8,128)S(1)} %get-tuple-element.20.ext_ref, f32[12,3584]{1,0:T(8,128)S(1)} %get-tuple-element.21.inv_ref), custom_call_target="tpu_custom_call" | custom-call | flops 2477260800 | bytes 233472 | tf_op jit(solution)/shard_map/pallas_call | solution.py:195
  25.0 1.4 %collective-permute-done.8.tpl_ref = bf16[3,304,128]{2,1,0:T(8,128)(2,1)S(1)} collective-permute-done((bf16[3,304,128]{2,1,0:T(8,128)(2,1)S(1)}, bf16[3,304,128]{2,1,0:T(8,128)(2,1)S(1)}, u32[]{:S(2)}, u32[]{:S(2)}) %collective-permute-start.8) | collective-permute-done | bytes 233504 | tf_op jit(solution)/shard_map/ppermute | solution.py:26
  26.4 3.0 %shard_map.49.refs_0_ = f32[64,3584]{1,0:T(8,128)S(1)} custom-call(bf16[3,304,128]{2,1,0:T(8,128)(2,1)S(1)} %collective-permute-done.8.tpl_ref, f32[12,4224]{1,0:T(8,128)S(1)} %get-tuple-element.20.ext_ref, f32[12,3584]{1,0:T(8,128)S(1)} %get-tuple-element.21.inv_ref, f32[64,3584]{1,0:T(8,128)S(1)} %shard_map.48.refs_0_), custom_call_target="tpu_custom_call" | custom-call | flops 2477260800 | bytes 233472 | tf_op jit(solution)/shard_map/pallas_call | solution.py:195
  29.3 8.5 %collective-permute-done.7.tpl_ref = bf16[3,304,128]{2,1,0:T(8,128)(2,1)S(1)} collective-permute-done((bf16[3,304,128]{2,1,0:T(8,128)(2,1)S(1)}, bf16[3,304,128]{2,1,0:T(8,128)(2,1)S(1)}, u32[]{:S(2)}, u32[]{:S(2)}) %collective-permute-start.7) | collective-permute-done | bytes 233504 | tf_op jit(solution)/shard_map/ppermute | solution.py:26
  37.8 3.0 %shard_map.50.refs_0_ = f32[64,3584]{1,0:T(8,128)S(1)} custom-call(bf16[3,304,128]{2,1,0:T(8,128)(2,1)S(1)} %collective-permute-done.7.tpl_ref, f32[12,4224]{1,0:T(8,128)S(1)} %get-tuple-element.20.ext_ref, f32[12,3584]{1,0:T(8,128)S(1)} %get-tuple-element.21.inv_ref, f32[64,3584]{1,0:T(8,128)S(1)} %shard_map.49.refs_0_), custom_call_target="tpu_custom_call" | custom-call | flops 2477260800 | bytes 233472 | tf_op jit(solution)/shard_map/pallas_call | solution.py:195
  40.8 0.0 collective-permute-done.tpl_ref
  40.8 3.0 %shard_map.51.acc_ref = f32[64,3584]{1,0:T(8,128)S(1)} custom-call(bf16[3,304,128]{2,1,0:T(8,128)(2,1)S(1)} %collective-permute-done.tpl_ref, f32[12,4224]{1,0:T(8,128)S(1)} %get-tuple-element.20.ext_ref, f32[12,3584]{1,0:T(8,128)S(1)} %get-tuple-element.21.inv_ref, f32[64,3584]{1,0:T(8,128)S(1)} %shard_map.50.refs_0_), custom_call_target="tpu_custom_call" | custom-call | flops 2477260800 | bytes 233472 | tf_op jit(solution)/shard_map/pallas_call | solution.py:195
  43.8 0.6 %shard_map.52 = (f32[32,3584]{1,0:T(8,128)S(1)}, bf16[32,3584]{1,0:T(8,128)(2,1)S(1)}) custom-call(s32[3]{0:T(128)S(1)} %pad_add_fusion.place_ref, f32[64,3584]{1,0:T(8,128)S(1)} %shard_map.51.acc_ref), custom_call_target="tpu_custom_call" | custom-call | tf_op jit(solution)/shard_map/pallas_call | solution.py:221
  44.4 0.1 collective-permute-start.9
  44.5 1.5 %collective-permute-done.9.came_ref = bf16[32,3584]{1,0:T(8,128)(2,1)S(1)} collective-permute-done((bf16[32,3584]{1,0:T(8,128)(2,1)S(1)}, bf16[32,3584]{1,0:T(8,128)(2,1)S(1)}, u32[]{:S(2)}, u32[]{:S(2)}) %collective-permute-start.9) | collective-permute-done | bytes 229408 | tf_op jit(solution)/shard_map/ppermute | solution.py:26
  46.0 0.6 %shard_map.53 = (f32[32,896]{1,0:T(8,128)S(1)}, bf16[32,896]{1,0:T(8,128)(2,1)S(1)}, bf16[32,896]{1,0:T(8,128)(2,1)S(1)}, bf16[32,896]{1,0:T(8,128)(2,1)S(1)}) custom-call(s32[3]{0:T(128)S(1)} %pad_add_fusion.place_ref, f32[32,3584]{1,0:T(8,128)S(1)} %get-tuple-element.25.keep_ref, bf16[32,3584]{1,0:T(8,128)(2,1)S(1)} %collective-permute-done.9.came_ref), custom_call_target="tpu_custom_call" | custom-call | tf_op jit(solution)/shard_map/pallas_call | solution.py:241
  46.6 1.6 %collective-permute-start.10 = (bf16[32,896]{1,0:T(8,128)(2,1)S(1)}, bf16[32,896]{1,0:T(8,128)(2,1)S(1)}, u32[]{:S(2)}, u32[]{:S(2)}) collective-permute-start(bf16[32,896]{1,0:T(8,128)(2,1)S(1)} %get-tuple-element.28), channel_id=1, source_target_pairs={{0,8},{8,0},{16,24},{24,16},{1,9},{9,1},{17,25},{25,17},{2,10},{10... | collective-permute-start | bytes 172040 | tf_op jit(solution)/shard_map/ppermute | solution.py:26
  48.1 1.5 %collective-permute-start.11 = (bf16[32,896]{1,0:T(8,128)(2,1)S(1)}, bf16[32,896]{1,0:T(8,128)(2,1)S(1)}, u32[]{:S(2)}, u32[]{:S(2)}) collective-permute-start(bf16[32,896]{1,0:T(8,128)(2,1)S(1)} %get-tuple-element.29), channel_id=1, source_target_pairs={{0,16},{8,24},{16,0},{24,8},{1,17},{9,25},{17,1},{25,9},{2,18},{10... | collective-permute-start | bytes 172040 | tf_op jit(solution)/shard_map/ppermute | solution.py:26
  49.6 0.5 collective-permute-start.12
  50.1 0.7 %collective-permute-done.10.refs_1_ = bf16[32,896]{1,0:T(8,128)(2,1)S(1)} collective-permute-done((bf16[32,896]{1,0:T(8,128)(2,1)S(1)}, bf16[32,896]{1,0:T(8,128)(2,1)S(1)}, u32[]{:S(2)}, u32[]{:S(2)}) %collective-permute-start.10) | collective-permute-done | bytes 57376 | tf_op jit(solution)/shard_map/ppermute | solution.py:26
  50.8 1.5 %collective-permute-done.11.refs_2_ = bf16[32,896]{1,0:T(8,128)(2,1)S(1)} collective-permute-done((bf16[32,896]{1,0:T(8,128)(2,1)S(1)}, bf16[32,896]{1,0:T(8,128)(2,1)S(1)}, u32[]{:S(2)}, u32[]{:S(2)}) %collective-permute-start.11) | collective-permute-done | bytes 57376 | tf_op jit(solution)/shard_map/ppermute | solution.py:26
  52.3 2.4 %collective-permute-done.12.refs_3_ = bf16[32,896]{1,0:T(8,128)(2,1)S(1)} collective-permute-done((bf16[32,896]{1,0:T(8,128)(2,1)S(1)}, bf16[32,896]{1,0:T(8,128)(2,1)S(1)}, u32[]{:S(2)}, u32[]{:S(2)}) %collective-permute-start.12) | collective-permute-done | bytes 57376 | tf_op jit(solution)/shard_map/ppermute | solution.py:26
  54.7 1.3 %shard_map.54 = f32[4,32,896]{2,1,0:T(8,128)} custom-call(s32[3]{0:T(128)S(1)} %pad_add_fusion.place_ref, f32[32,896]{1,0:T(8,128)S(1)} %get-tuple-element.27.refs_0_, bf16[32,896]{1,0:T(8,128)(2,1)S(1)} %collective-permute-done.10.refs_1_, bf16[32,896]{1,0:T(8,128)(2,1)S(1)} %collective-permute-done.11.refs_2_, ...), custom_call_target="tpu_custom_call" | custom-call | tf_op jit(solution)/shard_map/pallas_call | solution.py:259
  (5 shorter events, 0.1 us)
Async XLA Ops:
  0.0 0.7 %copy-start.1 = (bf16[1,3,896]{2,1,0:T(4,128)(2,1)S(1)}, bf16[1,3,896]{2,1,0:T(4,128)(2,1)}, u32[]{:S(2)}) copy-start(bf16[1,3,896]{2,1,0:T(4,128)(2,1)} %param.6) | copy-start | bytes 16132
  0.0 0.7 %copy-start.2 = (bf16[1,3,599]{2,1,0:T(4,128)(2,1)S(1)}, bf16[1,3,599]{2,1,0:T(4,128)(2,1)}, u32[]{:S(2)}) copy-start(bf16[1,3,599]{2,1,0:T(4,128)(2,1)} %param.7) | copy-start | bytes 10786
  0.1 0.7 %copy-start.3 = (s32[1,256,1]{1,2,0:T(1,128)S(1)}, s32[1,256,1]{1,2,0:T(1,128)}, u32[]{:S(2)}) copy-start(s32[1,256,1]{1,2,0:T(1,128)} %param.5) | copy-start | bytes 3076
  0.8 1.2 %copy-start = (bf16[1,256,1,3,600]{1,4,3,2,0:T(8,128)(2,1)S(1)}, bf16[1,256,1,3,600]{1,4,3,2,0:T(8,128)(2,1)}, u32[]{:S(2)}) copy-start(bf16[1,256,1,3,600]{1,4,3,2,0:T(8,128)(2,1)} %param.4) | copy-start | bytes 2764804
  3.1 6.8 %collective-permute-start.3 = (bf16[3,1536]{1,0:T(4,128)(2,1)S(1)}, bf16[3,1536]{1,0:T(4,128)(2,1)S(1)}, u32[]{:S(2)}, u32[]{:S(2)}) collective-permute-start(bf16[3,1536]{1,0:T(4,128)(2,1)S(1)} %get-tuple-element.19.refs_4_), channel_id=1, source_target_pairs={{0,6},{1,7},{2,4},{3,5},{4,2},{5,3},{6,0},{7,1},{8,14},{9,15},{10,... | collective-permute-start | bytes 27656 | tf_op jit(solution)/shard_map/ppermute | solution.py:26
  8.2 4.6 %collective-permute-start.2 = (bf16[3,1536]{1,0:T(4,128)(2,1)S(1)}, bf16[3,1536]{1,0:T(4,128)(2,1)S(1)}, u32[]{:S(2)}, u32[]{:S(2)}) collective-permute-start(bf16[3,1536]{1,0:T(4,128)(2,1)S(1)} %get-tuple-element.19.refs_4_), channel_id=1, source_target_pairs={{0,4},{1,5},{2,6},{3,7},{4,0},{5,1},{6,2},{7,3},{8,12},{9,13},{10,... | collective-permute-start | bytes 27656 | tf_op jit(solution)/shard_map/ppermute | solution.py:26
  8.2 4.6 %collective-permute-start.1 = (bf16[3,1536]{1,0:T(4,128)(2,1)S(1)}, bf16[3,1536]{1,0:T(4,128)(2,1)S(1)}, u32[]{:S(2)}, u32[]{:S(2)}) collective-permute-start(bf16[3,1536]{1,0:T(4,128)(2,1)S(1)} %get-tuple-element.19.refs_4_), channel_id=1, source_target_pairs={{0,2},{1,3},{2,0},{3,1},{4,6},{5,7},{6,4},{7,5},{8,10},{9,11},{10,... | collective-permute-start | bytes 27656 | tf_op jit(solution)/shard_map/ppermute | solution.py:26
  12.9 7.0 %collective-permute-start.6 = (bf16[4,3,896]{2,1,0:T(4,128)(2,1)S(1)}, bf16[4,3,896]{2,1,0:T(4,128)(2,1)S(1)}, u32[]{:S(2)}, u32[]{:S(2)}) collective-permute-start(bf16[4,3,896]{2,1,0:T(4,128)(2,1)S(1)} %pad_maximum_fusion.refs_0_), channel_id=1, source_target_pairs={{0,24},{8,16},{16,8},{24,0},{1,25},{9,17},{17,9},{25,1},{2,26},{10... | collective-permute-start | bytes 64520 | tf_op jit(solution)/shard_map/ppermute | solution.py:26
  15.4 4.5 %collective-permute-start.5 = (bf16[4,3,896]{2,1,0:T(4,128)(2,1)S(1)}, bf16[4,3,896]{2,1,0:T(4,128)(2,1)S(1)}, u32[]{:S(2)}, u32[]{:S(2)}) collective-permute-start(bf16[4,3,896]{2,1,0:T(4,128)(2,1)S(1)} %pad_maximum_fusion.refs_0_), channel_id=1, source_target_pairs={{0,16},{8,24},{16,0},{24,8},{1,17},{9,25},{17,1},{25,9},{2,18},{10... | collective-permute-start | bytes 64520 | tf_op jit(solution)/shard_map/ppermute | solution.py:26
  15.9 4.0 %collective-permute-start.4 = (bf16[4,3,896]{2,1,0:T(4,128)(2,1)S(1)}, bf16[4,3,896]{2,1,0:T(4,128)(2,1)S(1)}, u32[]{:S(2)}, u32[]{:S(2)}) collective-permute-start(bf16[4,3,896]{2,1,0:T(4,128)(2,1)S(1)} %pad_maximum_fusion.refs_0_), channel_id=1, source_target_pairs={{0,8},{8,0},{16,24},{24,16},{1,9},{9,1},{17,25},{25,17},{2,10},{10... | collective-permute-start | bytes 64520 | tf_op jit(solution)/shard_map/ppermute | solution.py:26
  16.4 9.9 %collective-permute-start.8 = (bf16[3,304,128]{2,1,0:T(8,128)(2,1)S(1)}, bf16[3,304,128]{2,1,0:T(8,128)(2,1)S(1)}, u32[]{:S(2)}, u32[]{:S(2)}) collective-permute-start(bf16[3,304,128]{2,1,0:T(8,128)(2,1)S(1)} %get-tuple-element.23), channel_id=1, source_target_pairs={{0,2},{1,3},{2,0},{3,1},{4,6},{5,7},{6,4},{7,5},{8,10},{9,11},{10,... | collective-permute-start | bytes 700424 | tf_op jit(solution)/shard_map/ppermute | solution.py:26
  16.4 24.4 %collective-permute-start = (bf16[3,304,128]{2,1,0:T(8,128)(2,1)S(1)}, bf16[3,304,128]{2,1,0:T(8,128)(2,1)S(1)}, u32[]{:S(2)}, u32[]{:S(2)}) collective-permute-start(bf16[3,304,128]{2,1,0:T(8,128)(2,1)S(1)} %get-tuple-element.18), channel_id=1, source_target_pairs={{0,6},{1,7},{2,4},{3,5},{4,2},{5,3},{6,0},{7,1},{8,14},{9,15},{10,... | collective-permute-start | bytes 700424 | tf_op jit(solution)/shard_map/ppermute | solution.py:26
  19.9 17.9 %collective-permute-start.7 = (bf16[3,304,128]{2,1,0:T(8,128)(2,1)S(1)}, bf16[3,304,128]{2,1,0:T(8,128)(2,1)S(1)}, u32[]{:S(2)}, u32[]{:S(2)}) collective-permute-start(bf16[3,304,128]{2,1,0:T(8,128)(2,1)S(1)} %get-tuple-element.22), channel_id=1, source_target_pairs={{0,4},{1,5},{2,6},{3,7},{4,0},{5,1},{6,2},{7,3},{8,12},{9,13},{10,... | collective-permute-start | bytes 700424 | tf_op jit(solution)/shard_map/ppermute | solution.py:26
  44.4 1.6 %collective-permute-start.9 = (bf16[32,3584]{1,0:T(8,128)(2,1)S(1)}, bf16[32,3584]{1,0:T(8,128)(2,1)S(1)}, u32[]{:S(2)}, u32[]{:S(2)}) collective-permute-start(bf16[32,3584]{1,0:T(8,128)(2,1)S(1)} %get-tuple-element.26), channel_id=1, source_target_pairs={{0,1},{1,0},{2,3},{3,2},{4,5},{5,4},{6,7},{7,6},{8,9},{9,8},{10,11... | collective-permute-start | bytes 688136 | tf_op jit(solution)/shard_map/ppermute | solution.py:26
  46.6 4.2 %collective-permute-start.10 = (bf16[32,896]{1,0:T(8,128)(2,1)S(1)}, bf16[32,896]{1,0:T(8,128)(2,1)S(1)}, u32[]{:S(2)}, u32[]{:S(2)}) collective-permute-start(bf16[32,896]{1,0:T(8,128)(2,1)S(1)} %get-tuple-element.28), channel_id=1, source_target_pairs={{0,8},{8,0},{16,24},{24,16},{1,9},{9,1},{17,25},{25,17},{2,10},{10... | collective-permute-start | bytes 172040 | tf_op jit(solution)/shard_map/ppermute | solution.py:26
  48.1 4.2 %collective-permute-start.11 = (bf16[32,896]{1,0:T(8,128)(2,1)S(1)}, bf16[32,896]{1,0:T(8,128)(2,1)S(1)}, u32[]{:S(2)}, u32[]{:S(2)}) collective-permute-start(bf16[32,896]{1,0:T(8,128)(2,1)S(1)} %get-tuple-element.29), channel_id=1, source_target_pairs={{0,16},{8,24},{16,0},{24,8},{1,17},{9,25},{17,1},{25,9},{2,18},{10... | collective-permute-start | bytes 172040 | tf_op jit(solution)/shard_map/ppermute | solution.py:26
  49.6 5.1 %collective-permute-start.12 = (bf16[32,896]{1,0:T(8,128)(2,1)S(1)}, bf16[32,896]{1,0:T(8,128)(2,1)S(1)}, u32[]{:S(2)}, u32[]{:S(2)}) collective-permute-start(bf16[32,896]{1,0:T(8,128)(2,1)S(1)} %get-tuple-element.30), channel_id=1, source_target_pairs={{0,24},{8,16},{16,8},{24,0},{1,25},{9,17},{17,9},{25,1},{2,26},{10... | collective-permute-start | bytes 172040 | tf_op jit(solution)/shard_map/ppermute | solution.py:26

commit v2 on v1

v2 whole, which is shorter than its diff:
```python
import functools
import jax
import jax.numpy as jnp
from jax import lax
from jax.experimental import pallas as pl
from jax.experimental.pallas import tpu as pltpu
from jax.sharding import PartitionSpec as P

F32 = jnp.float32
BF16 = jnp.bfloat16
LANES = 128
CHUNK = 512
VMEM = pl.BlockSpec(memory_space=pltpu.VMEM)
SMEM = pl.BlockSpec(memory_space=pltpu.SMEM)
HBM = pl.BlockSpec(memory_space=pltpu.HBM)
CHEAP = pl.CostEstimate(flops=1, bytes_accessed=1, transcendentals=0)


def params(limit_mib):
    return pltpu.CompilerParams(vmem_limit_bytes=limit_mib << 20)


def up(value, multiple):
    return (value + multiple - 1) // multiple * multiple


def swap_with(x, axis, offset):
    size = lax.axis_size(axis)
    return lax.ppermute(x, axis, [(i, i ^ offset) for i in range(size)])


def join_kernel(wave_ref, tail_ref, out_ref, wave_held, tail_held, arrived):
    copies = [
        pltpu.make_async_copy(wave_ref, wave_held, arrived.at[0]),
        pltpu.make_async_copy(tail_ref, tail_held, arrived.at[1]),
    ]
    for copy in copies:
        copy.start()
    for copy in copies:
        copy.wait()
    samples = wave_held.shape[-1]
    out_ref[...] = jnp.zeros_like(out_ref)
    out_ref[:, :samples] = wave_held[...]
    out_ref[:, samples : samples + tail_held.shape[-1]] = tail_held[...]


def join(wave, tail):
    return pl.pallas_call(
        join_kernel,
        out_shape=jax.ShapeDtypeStruct((wave.shape[0], up(wave.shape[-1] + tail.shape[-1], LANES)), BF16),
        in_specs=[HBM] * 2,
        out_specs=VMEM,
        scratch_shapes=[pltpu.VMEM(x.shape, x.dtype) for x in (wave, tail)] + [pltpu.SemaphoreType.DMA((2,))],
        compiler_params=params(16),
        cost_estimate=CHEAP,
    )(*[pltpu.with_memory_space_constraint(x, pltpu.HBM) for x in (wave, tail)])


def pack_kernel(chips, rows, length, place_ref, tpl_ref, mask_ref, *refs):
    tpl_outs, (held_ref, mask_held, arrived) = refs[:chips], refs[chips:]
    comps = tpl_ref.shape[0]
    copies = [pltpu.make_async_copy(mask_ref, mask_held, arrived.at[comps])]
    copies += [pltpu.make_async_copy(tpl_ref.at[c], held_ref.at[c], arrived.at[c]) for c in range(comps)]
    for copy in copies:
        copy.start()
    copies[0].wait()
    folds = LANES // rows
    fold_lags = tpl_outs[0].shape[1]
    lane = lax.broadcasted_iota(jnp.int32, (1, LANES), 1)
    for comp in range(comps):
        copies[1 + comp].wait()
        for offset in range(chips):
            target = place_ref[0] ^ offset
            tile = pl.multiple_of((target * rows) // LANES * LANES, LANES)
            start = (target * rows) % LANES
            mask = mask_held[:, pl.ds(tile, LANES)].astype(F32)
            values = held_ref[comp, :, pl.ds(tile, LANES)].astype(F32) * mask
            folded = jnp.zeros((fold_lags, LANES), F32)
            for fold in range(folds):
                piece = values[fold * fold_lags : min((fold + 1) * fold_lags, length)]
                if piece.shape[0] == 0:
                    continue
                if piece.shape[0] < fold_lags:
                    piece = jnp.concatenate(
                        [piece, jnp.zeros((fold_lags - piece.shape[0], LANES), F32)], axis=0
                    )
                turned = pltpu.roll(piece, (fold * rows - start + LANES) % LANES, 1)
                here = (lane >= fold * rows) & (lane < (fold + 1) * rows)
                folded = jnp.where(here, turned, folded)
            tpl_outs[offset][comp] = folded.astype(BF16)


def pack(place, tpl, mask, chips):
    comps, length, all_rows = tpl.shape
    rows = all_rows // chips
    fold_lags = up(-(-length // (LANES // rows)), 16)
    return pl.pallas_call(
        functools.partial(pack_kernel, chips, rows, length),
        out_shape=[jax.ShapeDtypeStruct((comps, fold_lags, LANES), BF16)] * chips,
        in_specs=[SMEM] + [HBM] * 2,
        out_specs=[VMEM] * chips,
        scratch_shapes=[pltpu.VMEM(x.shape, x.dtype) for x in (tpl, mask)]
        + [pltpu.SemaphoreType.DMA((comps + 1,))],
        compiler_params=params(16),
        cost_estimate=CHEAP,
    )(place, *[pltpu.with_memory_space_constraint(x, pltpu.HBM) for x in (tpl, mask)])


def wave_kernel(shards, chips, length, halo, place_ref, *refs):
    shard_refs, tail_refs = refs[:shards], refs[shards : shards + chips]
    ext_ref, inv_ref = refs[shards + chips :]
    comps, samples = shard_refs[0].shape[1:]
    total = inv_ref.shape[-1]
    width = ext_ref.shape[-1]
    ext_ref[...] = jnp.zeros_like(ext_ref)
    for chip in range(chips):
        for offset in range(shards):
            at = pl.multiple_of((place_ref[1] ^ offset) * samples, LANES)
            ext_ref[chip * comps : (chip + 1) * comps, pl.ds(at, samples)] = shard_refs[offset][chip].astype(F32)
        ext_ref[chip * comps : (chip + 1) * comps, total : total + halo] = tail_refs[chip][
            :, samples : samples + halo
        ].astype(F32)

    def window(values):
        result, done, span, doubled = None, 0, 1, values
        while span <= length:
            if length & span:
                part = doubled if done == 0 else pltpu.roll(doubled, width - done, 1)
                result = part if result is None else result + part
                done += span
            span *= 2
            if span <= length:
                doubled = doubled + pltpu.roll(doubled, width - span // 2, 1)
        return result[:, :total]

    values = ext_ref[...]
    window_sum = window(values)
    window_square = window(values * values)
    inv_ref[...] = lax.rsqrt(window_square - window_sum * window_sum / length + 1e-05)


def wave_windows(place, shards, tails, length, halo):
    chips, comps, samples = shards[0].shape
    total = samples * len(shards)
    width = total + up(length, LANES)
    return pl.pallas_call(
        functools.partial(wave_kernel, len(shards), chips, length, halo),
        out_shape=[
            jax.ShapeDtypeStruct((chips * comps, width), F32),
            jax.ShapeDtypeStruct((chips * comps, total), F32),
        ],
        in_specs=[SMEM] + [VMEM] * (len(shards) + chips),
        out_specs=[VMEM] * 2,
        compiler_params=params(16),
        cost_estimate=CHEAP,
    )(place, *shards, *tails)


def lag_rows(values, rows, length):
    fold_lags = values.shape[0]
    folds = LANES // rows
    splits = -(-length // (2 * LANES))

    def over_folds(total):
        span = rows
        while span < LANES:
            total = total + pltpu.roll(total, span, 1)
            span *= 2
        return total

    lane = lax.broadcasted_iota(jnp.int32, values.shape, 1)
    lag = lax.broadcasted_iota(jnp.int32, values.shape, 0) + lane // rows * fold_lags
    mean = over_folds(jnp.sum(values, axis=0, keepdims=True)) / length
    centred = jnp.where(lag < length, values - mean, 0.0)
    energy = over_folds(jnp.sum(centred * centred, axis=0, keepdims=True))
    weighted = centred * lax.rsqrt(energy + 1e-05)
    parts = [weighted] + [pltpu.roll(weighted, LANES - fold * rows, 1) for fold in range(1, folds)]
    wanted = splits * 2 * LANES
    if folds * fold_lags < wanted:
        parts.append(jnp.zeros((wanted - folds * fold_lags, LANES), F32))
    spread = jnp.concatenate(parts, axis=0)
    low = lax.broadcasted_iota(jnp.int32, (LANES, LANES), 1) < LANES // 2
    flip = (
        lax.broadcasted_iota(jnp.int32, (LANES, LANES), 0)
        + lax.broadcasted_iota(jnp.int32, (LANES, LANES), 1)
        == LANES - 1
    ).astype(BF16)
    result = []
    for split in range(splits):
        at = split * 2 * LANES
        both = jnp.where(low, spread[at : at + LANES], pltpu.roll(spread[at + LANES : at + 2 * LANES], LANES // 2, 1))
        turned = lax.dot_general(
            both.astype(BF16), flip, (((0,), (0,)), ((), ())), preferred_element_type=F32
        ).astype(BF16)
        result.append(jnp.concatenate([turned[:rows], turned[LANES // 2 : LANES // 2 + rows]], axis=1))
    return jnp.concatenate(result, axis=0)


def fill_hankel(row, out_ref):
    width = row.shape[-1]
    spread = jnp.broadcast_to(row.astype(BF16), (LANES, width))
    out_ref[...] = pltpu.roll(spread, width - (LANES - 1), 1, stride=1, stride_axis=0)


def hankel_kernel(index, ext_ref, out_ref):
    comps = out_ref.shape[0]
    for comp in range(comps):
        at = index * comps + comp
        fill_hankel(ext_ref[at : at + 1, :], out_ref.at[comp])


def hankel(index, comps, ext):
    return pl.pallas_call(
        functools.partial(hankel_kernel, index),
        out_shape=jax.ShapeDtypeStruct((comps, LANES, ext.shape[-1]), BF16),
        in_specs=[VMEM],
        out_specs=VMEM,
        compiler_params=params(16),
        cost_estimate=CHEAP,
    )(ext)


def piece_kernel(index, rows, length, last, place_ref, tpl_ref, ext_ref, inv_ref, *refs):
    refs = list(refs)
    acc_ref = None if index == 0 else refs.pop(0)
    given_ref = refs.pop(0) if last else None
    out_refs = [refs.pop(0) for _ in range(2 if last else 1)]
    hankel_ref, product_ref, sum_ref = refs
    sum_ref = sum_ref if last else out_refs[0]
    comps = tpl_ref.shape[0]
    total = inv_ref.shape[-1]
    reach = product_ref.shape[-1]
    splits = product_ref.shape[1] // rows
    if last:
        hankel_ref = given_ref
    else:
        for comp in range(comps):
            at = index * comps + comp
            fill_hankel(ext_ref[at : at + 1, :], hankel_ref.at[comp])
    lhs = [lag_rows(tpl_ref[comp].astype(F32), rows, length) for comp in range(comps)]
    for comp in range(comps):
        rhs = jnp.concatenate(
            [hankel_ref[comp, :, :reach], hankel_ref[comp, :, LANES : LANES + reach]], axis=0
        )
        product_ref[comp] = jnp.dot(lhs[comp], rhs, preferred_element_type=F32)
    for start in range(0, total, CHUNK):
        stop = min(start + CHUNK, total)
        chunk = None if acc_ref is None else acc_ref[:, start:stop]
        for comp in range(comps):
            at = index * comps + comp
            part = product_ref[comp, :rows, start:stop]
            for split in range(1, splits):
                shift = split * 2 * LANES
                part = part + product_ref[comp, split * rows : (split + 1) * rows, shift + start : shift + stop]
            part = part * inv_ref[at : at + 1, start:stop]
            chunk = part if chunk is None else chunk + part
        sum_ref[:, start:stop] = chunk
    if last:
        keep_ref, send_ref = out_refs
        own = rows // 2
        at = pl.multiple_of(place_ref[2] * own, own)
        other = pl.multiple_of((1 - place_ref[2]) * own, own)
        keep_ref[...] = sum_ref[pl.ds(at, own), :]
        send_ref[...] = sum_ref[pl.ds(other, own), :].astype(BF16)


def piece(place, index, rows, length, last, tpl, ext, inv, acc, given):
    total, width = inv.shape[-1], ext.shape[-1]
    comps = tpl.shape[0]
    splits = -(-length // (2 * LANES))
    reach = total + (splits - 1) * 2 * LANES
    inputs = [place, tpl, ext, inv] + [part for part in (acc, given) if part is not None]
    out_shape = [jax.ShapeDtypeStruct((rows, total), F32)]
    if last:
        half = (rows // 2, total)
        out_shape = [jax.ShapeDtypeStruct(half, F32), jax.ShapeDtypeStruct(half, BF16)]
    return pl.pallas_call(
        functools.partial(piece_kernel, index, rows, length, last),
        out_shape=out_shape,
        in_specs=[SMEM] + [VMEM] * (len(inputs) - 1),
        out_specs=[VMEM] * len(out_shape),
        scratch_shapes=[
            pltpu.VMEM((1, LANES, LANES) if last else (comps, LANES, width), BF16),
            pltpu.VMEM((comps, splits * rows, reach), F32),
            pltpu.VMEM((rows, total) if last else (8, LANES), F32),
        ],
        compiler_params=params(24),
        cost_estimate=CHEAP,
    )(*inputs)


def shard_kernel(place_ref, keep_ref, came_ref, own_ref, *send_refs):
    samples = own_ref.shape[-1]
    for offset, ref in enumerate((own_ref,) + send_refs):
        at = pl.multiple_of((place_ref[1] ^ offset) * samples, LANES)
        total = keep_ref[:, pl.ds(at, samples)] + came_ref[:, pl.ds(at, samples)].astype(F32)
        ref[...] = total.astype(ref.dtype)


def shard(place, keep, came, count):
    own, total = keep.shape
    samples = total // count
    return pl.pallas_call(
        shard_kernel,
        out_shape=[jax.ShapeDtypeStruct((own, samples), F32)]
        + [jax.ShapeDtypeStruct((own, samples), BF16)] * (count - 1),
        in_specs=[SMEM, VMEM, VMEM],
        out_specs=[VMEM] * count,
        compiler_params=params(16),
        cost_estimate=CHEAP,
    )(place, keep, came)


def gather_kernel(place_ref, *refs):
    out_ref = refs[-1]
    for offset, ref in enumerate(refs[:-1]):
        out_ref[place_ref[1] ^ offset] = ref[...].astype(F32)


def gather(place, parts):
    own, samples = parts[0].shape
    return pl.pallas_call(
        gather_kernel,
        out_shape=jax.ShapeDtypeStruct((len(parts), own, samples), F32),
        in_specs=[SMEM] + [VMEM] * len(parts),
        out_specs=VMEM,
        compiler_params=params(16),
    )(place, *parts)


def per_device(templates, channel_mask, waveforms, waveform_tail):
    length = templates.shape[-1]
    samples = waveforms.shape[-1]
    halo = waveform_tail.shape[-1]
    tm_count = lax.axis_size("tm")
    chips = lax.axis_size("sta") // 2
    tm_index, sta_index = lax.axis_index("tm"), lax.axis_index("sta")
    place = jnp.stack([sta_index // 2, tm_index, sta_index % 2]).astype(jnp.int32)
    tpl = jnp.transpose(templates[0, :, 0], (1, 2, 0))
    mask = channel_mask[..., 0]
    rows = tpl.shape[-1] // chips
    wave = join(waveforms[0], waveform_tail[0])
    waves = [wave] + [swap_with(wave, "sta", 2 * offset) for offset in range(1, chips)]
    messages = pack(place, tpl, mask, chips)
    messages, waves = lax.optimization_barrier((messages, waves))
    pieces = {offset: swap_with(messages[offset], "sta", 2 * offset) for offset in range(2, chips)}
    stacked = jnp.stack([part[:, :samples] for part in waves])
    shards = [stacked] + [swap_with(stacked, "tm", offset) for offset in range(1, tm_count)]
    near, shards = lax.optimization_barrier((messages[1], shards))
    pieces[0], pieces[1] = messages[0], swap_with(near, "sta", 2)
    ext, inv = wave_windows(place, shards, waves, length, halo)
    acc = None
    order = [0] + list(range(chips - 1, 2, -1)) + [1, 2]
    given = hankel(order[-1], waveforms.shape[1], ext)
    for offset in order:
        last = offset == order[-1]
        *done, acc = piece(
            place, offset, rows, length, last, pieces[offset], ext, inv, acc, given if last else None
        )
    keep, send = done[0], acc
    parts = shard(place, keep, swap_with(send, "sta", 1), tm_count)
    parts = [parts[0]] + [swap_with(parts[offset], "tm", offset) for offset in range(1, tm_count)]
    return gather(place, parts)


def solution(mesh):
    placed = (
        P("tm", None, "sta", None, None),
        P("tm", None, "sta"),
        P("sta", None, "tm"),
        P("sta", None, None),
    )
    return jax.shard_map(
        per_device, mesh=mesh, in_specs=placed, out_specs=P(None, "sta", "tm"), check_vma=False
    )
```

time: 56.2 us -> 48.9 us (0.87)
  waiting for transfers between devices: 19.9 us -> 12.2 us
  local copies, waits for them, and re-layouts: 1.89 us -> 0.02 us
  starting transfers between devices: 16.4 us -> 17.9 us
  Pallas kernels: 17.6 us -> 18.3 us
    ppermute x13, waiting for transfers between devices: 19.9 us -> 12.2 us  [swap_with(): return lax.ppermute(x, axis, [(i, i ^ offset) for i in range(size)])]
    unnamed x8 -> x0, local copies, waits for them, and re-layouts: 1.86 us -> none
    ppermute x13, starting transfers between devices: 16.4 us -> 17.9 us  [swap_with(): return lax.ppermute(x, axis, [(i, i ^ offset) for i in range(size)])]
    pallas_call x1, Pallas kernels: 1.16 us -> 2.29 us  [pack(): pl.pallas_call(functools.partial(pack_kernel, chips, rows, length), out_s...]
    pallas_call x5 -> x6, Pallas kernels: 12.4 us -> 12 us  [the longest x4 10.4 us: piece(): pl.pallas_call(functools.partial(piece_kernel, index, rows, length, last)...]
  transfers between devices with their start and end apart: 13 -> 13, of which waited for: 8 -> 8; matrix products, arithmetic and copies ran while one was open for 0% -> 0% of each run, Pallas kernels for 20% -> 27%
where the time goes in v2:
time: 48.9 us; the launch traced here: 48.7 us
  Pallas kernels  18.3 us (37%)
  starting transfers between devices  17.9 us (37%)
  waiting for transfers between devices  12.2 us (25%)
    ppermute x13, starting transfers between devices, swap_with(): return lax.ppermute(x, axis, [(i, i ^ offset) for i in range(size)])  17.9 us
    ppermute x13, waiting for transfers between devices, swap_with(): return lax.ppermute(x, axis, [(i, i ^ offset) for i in range(size)])  12.2 us
    pallas_call x4, Pallas kernels, piece(): pl.pallas_call(functools.partial(piece_kernel, index, rows, length, last)...  10.4 us
    pallas_call x1, Pallas kernels, pack(): pl.pallas_call(functools.partial(pack_kernel, chips, rows, length), out_s...  2.29 us
    pallas_call x1, Pallas kernels, wave_windows(): pl.pallas_call(functools.partial(wave_kernel, len(shards), chips, length,...  2.06 us
    pallas_call x1, Pallas kernels, gather(): pl.pallas_call(gather_kernel, out_shape=jax.ShapeDtypeStruct((len(parts),...  1.34 us
  transfers between devices with their start and end apart: 13, of which 8 were waited for; matrix products, arithmetic and copies ran while one was open for 0% of the time, Pallas kernels for 27%

profile of v2, /device:TPU:0, one launch (start us, length us, event | category | flops | bytes accessed | tf_op | source)
XLA Modules:
  0.0 48.7 jit_solution(13484819829527565374)
XLA Ops:
  0.0 0.7 %shard_map.47.refs_4_ = bf16[3,1536]{1,0:T(4,128)(2,1)S(1)} custom-call(bf16[3,896]{1,0:T(4,128)(2,1)} %bitcast.18, bf16[3,599]{1,0:T(4,128)(2,1)} %bitcast.19), custom_call_target="tpu_custom_call" | custom-call | flops 1 | bytes 1 | tf_op jit(solution)/shard_map/pallas_call | solution.py:48
  0.7 5.1 %collective-permute-start.2 = (bf16[3,1536]{1,0:T(4,128)(2,1)S(1)}, bf16[3,1536]{1,0:T(4,128)(2,1)S(1)}, u32[]{:S(2)}, u32[]{:S(2)}) collective-permute-start(bf16[3,1536]{1,0:T(4,128)(2,1)S(1)} %shard_map.47.refs_4_), channel_id=1, source_target_pairs={{0,6},{1,7},{2,4},{3,5},{4,2},{5,3},{6,0},{7,1},{8,14},{9,15},{10,... | collective-permute-start | bytes 27656 | tf_op jit(solution)/shard_map/ppermute | solution.py:29
  5.9 0.0 collective-permute-start.1
  5.9 0.6 %collective-permute-start = (bf16[3,1536]{1,0:T(4,128)(2,1)S(1)}, bf16[3,1536]{1,0:T(4,128)(2,1)S(1)}, u32[]{:S(2)}, u32[]{:S(2)}) collective-permute-start(bf16[3,1536]{1,0:T(4,128)(2,1)S(1)} %shard_map.47.refs_4_), channel_id=1, source_target_pairs={{0,2},{1,3},{2,0},{3,1},{4,6},{5,7},{6,4},{7,5},{8,10},{9,11},{10,... | collective-permute-start | bytes 27656 | tf_op jit(solution)/shard_map/ppermute | solution.py:29
  6.5 0.1 pad_add_fusion.place_ref
  6.6 2.3 %shard_map.46 = (bf16[3,304,128]{2,1,0:T(8,128)(2,1)S(1)}, bf16[3,304,128]{2,1,0:T(8,128)(2,1)S(1)}, bf16[3,304,128]{2,1,0:T(8,128)(2,1)S(1)}, bf16[3,304,128]{2,1,0:T(8,128)(2,1)S(1)}) custom-call(s32[3]{0:T(128)S(1)} %pad_add_fusion.place_ref, bf16[3,600,256]{2,1,0:T(8,128)(2,1)} %bitcast.17, s32[1,256]{1,0:T(1,128)} %bitcast.20), custom_call_target="tpu_custom_call" | custom-call | flops 1 | bytes 1 | tf_op jit(solution)/shard_map/pallas_call | solution.py:97
  8.9 0.0 collective-permute-done.2.refs_7_
  8.9 1.6 %collective-permute-done.1.refs_6_ = bf16[3,1536]{1,0:T(4,128)(2,1)S(1)} collective-permute-done((bf16[3,1536]{1,0:T(4,128)(2,1)S(1)}, bf16[3,1536]{1,0:T(4,128)(2,1)S(1)}, u32[]{:S(2)}, u32[]{:S(2)}) %collective-permute-start.1) | collective-permute-done | bytes 9248 | tf_op jit(solution)/shard_map/ppermute | solution.py:29
  10.5 0.0 collective-permute-done.refs_5_
  10.5 2.5 %collective-permute-start.6 = (bf16[4,3,896]{2,1,0:T(4,128)(2,1)S(1)}, bf16[4,3,896]{2,1,0:T(4,128)(2,1)S(1)}, u32[]{:S(2)}, u32[]{:S(2)}) collective-permute-start(bf16[4,3,896]{2,1,0:T(4,128)(2,1)S(1)} %pad_maximum_fusion.refs_0_), channel_id=1, source_target_pairs={{0,24},{8,16},{16,8},{24,0},{1,25},{9,17},{17,9},{25,1},{2,26},{10... | collective-permute-start | bytes 64520 | tf_op jit(solution)/shard_map/ppermute | solution.py:29
  13.0 0.5 %collective-permute-start.5 = (bf16[4,3,896]{2,1,0:T(4,128)(2,1)S(1)}, bf16[4,3,896]{2,1,0:T(4,128)(2,1)S(1)}, u32[]{:S(2)}, u32[]{:S(2)}) collective-permute-start(bf16[4,3,896]{2,1,0:T(4,128)(2,1)S(1)} %pad_maximum_fusion.refs_0_), channel_id=1, source_target_pairs={{0,16},{8,24},{16,0},{24,8},{1,17},{9,25},{17,1},{25,9},{2,18},{10... | collective-permute-start | bytes 64520 | tf_op jit(solution)/shard_map/ppermute | solution.py:29
  13.5 0.5 %collective-permute-start.4 = (bf16[4,3,896]{2,1,0:T(4,128)(2,1)S(1)}, bf16[4,3,896]{2,1,0:T(4,128)(2,1)S(1)}, u32[]{:S(2)}, u32[]{:S(2)}) collective-permute-start(bf16[4,3,896]{2,1,0:T(4,128)(2,1)S(1)} %pad_maximum_fusion.refs_0_), channel_id=1, source_target_pairs={{0,8},{8,0},{16,24},{24,16},{1,9},{9,1},{17,25},{25,17},{2,10},{10... | collective-permute-start | bytes 64520 | tf_op jit(solution)/shard_map/ppermute | solution.py:29
  14.1 2.2 %collective-permute-start.8 = (bf16[3,304,128]{2,1,0:T(8,128)(2,1)S(1)}, bf16[3,304,128]{2,1,0:T(8,128)(2,1)S(1)}, u32[]{:S(2)}, u32[]{:S(2)}) collective-permute-start(bf16[3,304,128]{2,1,0:T(8,128)(2,1)S(1)} %get-tuple-element.47), channel_id=1, source_target_pairs={{0,6},{1,7},{2,4},{3,5},{4,2},{5,3},{6,0},{7,1},{8,14},{9,15},{10,... | collective-permute-start | bytes 700424 | tf_op jit(solution)/shard_map/ppermute | solution.py:29
  16.3 0.0 collective-permute-done.6.refs_3_
  16.3 0.6 %collective-permute-done.5.refs_2_ = bf16[4,3,896]{2,1,0:T(4,128)(2,1)S(1)} collective-permute-done((bf16[4,3,896]{2,1,0:T(4,128)(2,1)S(1)}, bf16[4,3,896]{2,1,0:T(4,128)(2,1)S(1)}, u32[]{:S(2)}, u32[]{:S(2)}) %collective-permute-start.5) | collective-permute-done | bytes 21536 | tf_op jit(solution)/shard_map/ppermute | solution.py:29
  16.9 0.5 %collective-permute-done.4.refs_1_ = bf16[4,3,896]{2,1,0:T(4,128)(2,1)S(1)} collective-permute-done((bf16[4,3,896]{2,1,0:T(4,128)(2,1)S(1)}, bf16[4,3,896]{2,1,0:T(4,128)(2,1)S(1)}, u32[]{:S(2)}, u32[]{:S(2)}) %collective-permute-start.4) | collective-permute-done | bytes 21536 | tf_op jit(solution)/shard_map/ppermute | solution.py:29
  17.4 0.0 collective-permute-start.7
  17.4 2.8 %collective-permute-start.3 = (bf16[3,304,128]{2,1,0:T(8,128)(2,1)S(1)}, bf16[3,304,128]{2,1,0:T(8,128)(2,1)S(1)}, u32[]{:S(2)}, u32[]{:S(2)}) collective-permute-start(bf16[3,304,128]{2,1,0:T(8,128)(2,1)S(1)} %get-tuple-element.34), channel_id=1, source_target_pairs={{0,4},{1,5},{2,6},{3,7},{4,0},{5,1},{6,2},{7,3},{8,12},{9,13},{10,... | collective-permute-start | bytes 700424 | tf_op jit(solution)/shard_map/ppermute | solution.py:29
  20.2 2.1 %shard_map.48 = (f32[12,4224]{1,0:T(8,128)S(1)}, f32[12,3584]{1,0:T(8,128)S(1)}) custom-call(s32[3]{0:T(128)S(1)} %pad_add_fusion.place_ref, bf16[4,3,896]{2,1,0:T(4,128)(2,1)S(1)} %pad_maximum_fusion.refs_0_, bf16[4,3,896]{2,1,0:T(4,128)(2,1)S(1)} %collective-permute-done.4.refs_1_, bf16[4,3,896]{2,1,0:T(4,128)(2,1)S(1)} %collective-permute-done.5.refs_2_, ...), custom_call_target="tpu_custom_call" | custom-call | flops 1 | bytes 1 | tf_op jit(solution)/shard_map/pallas_call | solution.py:146
  22.2 0.9 %shard_map.52.refs_1_ = bf16[3,128,4224]{2,1,0:T(8,128)(2,1)S(1)} custom-call(f32[12,4224]{1,0:T(8,128)S(1)} %get-tuple-element.44.ext_ref), custom_call_target="tpu_custom_call" | custom-call | flops 1 | bytes 1 | tf_op jit(solution)/shard_map/pallas_call | solution.py:213
  23.1 2.6 %shard_map.49.refs_0_ = f32[64,3584]{1,0:T(8,128)S(1)} custom-call(s32[3]{0:T(128)S(1)} %pad_add_fusion.place_ref, bf16[3,304,128]{2,1,0:T(8,128)(2,1)S(1)} %get-tuple-element.48.tpl_ref, f32[12,4224]{1,0:T(8,128)S(1)} %get-tuple-element.44.ext_ref, f32[12,3584]{1,0:T(8,128)S(1)} %get-tuple-element.45.inv_ref), custom_call_target="tpu_custom_call" | custom-call | flops 1 | bytes 1 | tf_op jit(solution)/shard_map/pallas_call | solution.py:277
  25.7 0.0 collective-permute-done.8.tpl_ref
  25.7 2.6 %shard_map.50.refs_0_ = f32[64,3584]{1,0:T(8,128)S(1)} custom-call(s32[3]{0:T(128)S(1)} %pad_add_fusion.place_ref, bf16[3,304,128]{2,1,0:T(8,128)(2,1)S(1)} %collective-permute-done.8.tpl_ref, f32[12,4224]{1,0:T(8,128)S(1)} %get-tuple-element.44.ext_ref, f32[12,3584]{1,0:T(8,128)S(1)} %get-tuple-element.45.inv_ref, f32[64,3584]{1,0:T(8,128)S(1)} %shard_map.49.refs_0_), custom_call_target="tpu_custom_call" | custom-call | flops 1 | bytes 1 | tf_op jit(solution)/shard_map/pallas_call | solution.py:277
  28.3 0.0 collective-permute-done.7.tpl_ref
  28.3 2.6 %shard_map.51.refs_0_ = f32[64,3584]{1,0:T(8,128)S(1)} custom-call(s32[3]{0:T(128)S(1)} %pad_add_fusion.place_ref, bf16[3,304,128]{2,1,0:T(8,128)(2,1)S(1)} %collective-permute-done.7.tpl_ref, f32[12,4224]{1,0:T(8,128)S(1)} %get-tuple-element.44.ext_ref, f32[12,3584]{1,0:T(8,128)S(1)} %get-tuple-element.45.inv_ref, f32[64,3584]{1,0:T(8,128)S(1)} %shard_map.50.refs_0_), custom_call_target="tpu_custom_call" | custom-call | flops 1 | bytes 1 | tf_op jit(solution)/shard_map/pallas_call | solution.py:277
  30.9 3.5 %collective-permute-done.3.tpl_ref = bf16[3,304,128]{2,1,0:T(8,128)(2,1)S(1)} collective-permute-done((bf16[3,304,128]{2,1,0:T(8,128)(2,1)S(1)}, bf16[3,304,128]{2,1,0:T(8,128)(2,1)S(1)}, u32[]{:S(2)}, u32[]{:S(2)}) %collective-permute-start.3) | collective-permute-done | bytes 233504 | tf_op jit(solution)/shard_map/ppermute | solution.py:29
  34.4 2.6 %shard_map.53 = (f32[32,3584]{1,0:T(8,128)S(1)}, bf16[32,3584]{1,0:T(8,128)(2,1)S(1)}) custom-call(s32[3]{0:T(128)S(1)} %pad_add_fusion.place_ref, bf16[3,304,128]{2,1,0:T(8,128)(2,1)S(1)} %collective-permute-done.3.tpl_ref, f32[12,4224]{1,0:T(8,128)S(1)} %get-tuple-element.44.ext_ref, f32[12,3584]{1,0:T(8,128)S(1)} %get-tuple-element.45.inv_ref, ...), custom_call_target="tpu_custom_call" | custom-call | flops 1 | bytes 1 | tf_op jit(solution)/shard_map/pallas_call | solution.py:277
  37.0 0.1 collective-permute-start.9
  37.1 1.5 %collective-permute-done.9.came_ref = bf16[32,3584]{1,0:T(8,128)(2,1)S(1)} collective-permute-done((bf16[32,3584]{1,0:T(8,128)(2,1)S(1)}, bf16[32,3584]{1,0:T(8,128)(2,1)S(1)}, u32[]{:S(2)}, u32[]{:S(2)}) %collective-permute-start.9) | collective-permute-done | bytes 229408 | tf_op jit(solution)/shard_map/ppermute | solution.py:29
  38.6 0.6 %shard_map.54 = (f32[32,896]{1,0:T(8,128)S(1)}, bf16[32,896]{1,0:T(8,128)(2,1)S(1)}, bf16[32,896]{1,0:T(8,128)(2,1)S(1)}, bf16[32,896]{1,0:T(8,128)(2,1)S(1)}) custom-call(s32[3]{0:T(128)S(1)} %pad_add_fusion.place_ref, f32[32,3584]{1,0:T(8,128)S(1)} %get-tuple-element.49.keep_ref, bf16[32,3584]{1,0:T(8,128)(2,1)S(1)} %collective-permute-done.9.came_ref), custom_call_target="tpu_custom_call" | custom-call | flops 1 | bytes 1 | tf_op jit(solution)/shard_map/pallas_call | solution.py:303
  39.2 1.6 %collective-permute-start.10 = (bf16[32,896]{1,0:T(8,128)(2,1)S(1)}, bf16[32,896]{1,0:T(8,128)(2,1)S(1)}, u32[]{:S(2)}, u32[]{:S(2)}) collective-permute-start(bf16[32,896]{1,0:T(8,128)(2,1)S(1)} %get-tuple-element.52), channel_id=1, source_target_pairs={{0,8},{8,0},{16,24},{24,16},{1,9},{9,1},{17,25},{25,17},{2,10},{10... | collective-permute-start | bytes 172040 | tf_op jit(solution)/shard_map/ppermute | solution.py:29
  40.7 1.5 %collective-permute-start.11 = (bf16[32,896]{1,0:T(8,128)(2,1)S(1)}, bf16[32,896]{1,0:T(8,128)(2,1)S(1)}, u32[]{:S(2)}, u32[]{:S(2)}) collective-permute-start(bf16[32,896]{1,0:T(8,128)(2,1)S(1)} %get-tuple-element.53), channel_id=1, source_target_pairs={{0,16},{8,24},{16,0},{24,8},{1,17},{9,25},{17,1},{25,9},{2,18},{10... | collective-permute-start | bytes 172040 | tf_op jit(solution)/shard_map/ppermute | solution.py:29
  42.2 0.5 collective-permute-start.12
  42.7 0.7 %collective-permute-done.10.refs_1_ = bf16[32,896]{1,0:T(8,128)(2,1)S(1)} collective-permute-done((bf16[32,896]{1,0:T(8,128)(2,1)S(1)}, bf16[32,896]{1,0:T(8,128)(2,1)S(1)}, u32[]{:S(2)}, u32[]{:S(2)}) %collective-permute-start.10) | collective-permute-done | bytes 57376 | tf_op jit(solution)/shard_map/ppermute | solution.py:29
  43.4 1.5 %collective-permute-done.11.refs_2_ = bf16[32,896]{1,0:T(8,128)(2,1)S(1)} collective-permute-done((bf16[32,896]{1,0:T(8,128)(2,1)S(1)}, bf16[32,896]{1,0:T(8,128)(2,1)S(1)}, u32[]{:S(2)}, u32[]{:S(2)}) %collective-permute-start.11) | collective-permute-done | bytes 57376 | tf_op jit(solution)/shard_map/ppermute | solution.py:29
  44.9 2.4 %collective-permute-done.12.refs_3_ = bf16[32,896]{1,0:T(8,128)(2,1)S(1)} collective-permute-done((bf16[32,896]{1,0:T(8,128)(2,1)S(1)}, bf16[32,896]{1,0:T(8,128)(2,1)S(1)}, u32[]{:S(2)}, u32[]{:S(2)}) %collective-permute-start.12) | collective-permute-done | bytes 57376 | tf_op jit(solution)/shard_map/ppermute | solution.py:29
  47.3 1.3 %shard_map.55 = f32[4,32,896]{2,1,0:T(8,128)} custom-call(s32[3]{0:T(128)S(1)} %pad_add_fusion.place_ref, f32[32,896]{1,0:T(8,128)S(1)} %get-tuple-element.51.refs_0_, bf16[32,896]{1,0:T(8,128)(2,1)S(1)} %collective-permute-done.10.refs_1_, bf16[32,896]{1,0:T(8,128)(2,1)S(1)} %collective-permute-done.11.refs_2_, ...), custom_call_target="tpu_custom_call" | custom-call | tf_op jit(solution)/shard_map/pallas_call | solution.py:322
  (3 shorter events, 0.0 us)
Async XLA Ops:
  0.7 8.1 %collective-permute-start.2 = (bf16[3,1536]{1,0:T(4,128)(2,1)S(1)}, bf16[3,1536]{1,0:T(4,128)(2,1)S(1)}, u32[]{:S(2)}, u32[]{:S(2)}) collective-permute-start(bf16[3,1536]{1,0:T(4,128)(2,1)S(1)} %shard_map.47.refs_4_), channel_id=1, source_target_pairs={{0,6},{1,7},{2,4},{3,5},{4,2},{5,3},{6,0},{7,1},{8,14},{9,15},{10,... | collective-permute-start | bytes 27656 | tf_op jit(solution)/shard_map/ppermute | solution.py:29
  5.9 4.6 %collective-permute-start.1 = (bf16[3,1536]{1,0:T(4,128)(2,1)S(1)}, bf16[3,1536]{1,0:T(4,128)(2,1)S(1)}, u32[]{:S(2)}, u32[]{:S(2)}) collective-permute-start(bf16[3,1536]{1,0:T(4,128)(2,1)S(1)} %shard_map.47.refs_4_), channel_id=1, source_target_pairs={{0,4},{1,5},{2,6},{3,7},{4,0},{5,1},{6,2},{7,3},{8,12},{9,13},{10,... | collective-permute-start | bytes 27656 | tf_op jit(solution)/shard_map/ppermute | solution.py:29
  5.9 4.6 %collective-permute-start = (bf16[3,1536]{1,0:T(4,128)(2,1)S(1)}, bf16[3,1536]{1,0:T(4,128)(2,1)S(1)}, u32[]{:S(2)}, u32[]{:S(2)}) collective-permute-start(bf16[3,1536]{1,0:T(4,128)(2,1)S(1)} %shard_map.47.refs_4_), channel_id=1, source_target_pairs={{0,2},{1,3},{2,0},{3,1},{4,6},{5,7},{6,4},{7,5},{8,10},{9,11},{10,... | collective-permute-start | bytes 27656 | tf_op jit(solution)/shard_map/ppermute | solution.py:29
  10.5 5.8 %collective-permute-start.6 = (bf16[4,3,896]{2,1,0:T(4,128)(2,1)S(1)}, bf16[4,3,896]{2,1,0:T(4,128)(2,1)S(1)}, u32[]{:S(2)}, u32[]{:S(2)}) collective-permute-start(bf16[4,3,896]{2,1,0:T(4,128)(2,1)S(1)} %pad_maximum_fusion.refs_0_), channel_id=1, source_target_pairs={{0,24},{8,16},{16,8},{24,0},{1,25},{9,17},{17,9},{25,1},{2,26},{10... | collective-permute-start | bytes 64520 | tf_op jit(solution)/shard_map/ppermute | solution.py:29
  13.0 3.9 %collective-permute-start.5 = (bf16[4,3,896]{2,1,0:T(4,128)(2,1)S(1)}, bf16[4,3,896]{2,1,0:T(4,128)(2,1)S(1)}, u32[]{:S(2)}, u32[]{:S(2)}) collective-permute-start(bf16[4,3,896]{2,1,0:T(4,128)(2,1)S(1)} %pad_maximum_fusion.refs_0_), channel_id=1, source_target_pairs={{0,16},{8,24},{16,0},{24,8},{1,17},{9,25},{17,1},{25,9},{2,18},{10... | collective-permute-start | bytes 64520 | tf_op jit(solution)/shard_map/ppermute | solution.py:29
  13.5 3.9 %collective-permute-start.4 = (bf16[4,3,896]{2,1,0:T(4,128)(2,1)S(1)}, bf16[4,3,896]{2,1,0:T(4,128)(2,1)S(1)}, u32[]{:S(2)}, u32[]{:S(2)}) collective-permute-start(bf16[4,3,896]{2,1,0:T(4,128)(2,1)S(1)} %pad_maximum_fusion.refs_0_), channel_id=1, source_target_pairs={{0,8},{8,0},{16,24},{24,16},{1,9},{9,1},{17,25},{25,17},{2,10},{10... | collective-permute-start | bytes 64520 | tf_op jit(solution)/shard_map/ppermute | solution.py:29
  14.1 11.7 %collective-permute-start.8 = (bf16[3,304,128]{2,1,0:T(8,128)(2,1)S(1)}, bf16[3,304,128]{2,1,0:T(8,128)(2,1)S(1)}, u32[]{:S(2)}, u32[]{:S(2)}) collective-permute-start(bf16[3,304,128]{2,1,0:T(8,128)(2,1)S(1)} %get-tuple-element.47), channel_id=1, source_target_pairs={{0,6},{1,7},{2,4},{3,5},{4,2},{5,3},{6,0},{7,1},{8,14},{9,15},{10,... | collective-permute-start | bytes 700424 | tf_op jit(solution)/shard_map/ppermute | solution.py:29
  17.4 10.9 %collective-permute-start.7 = (bf16[3,304,128]{2,1,0:T(8,128)(2,1)S(1)}, bf16[3,304,128]{2,1,0:T(8,128)(2,1)S(1)}, u32[]{:S(2)}, u32[]{:S(2)}) collective-permute-start(bf16[3,304,128]{2,1,0:T(8,128)(2,1)S(1)} %get-tuple-element.46), channel_id=1, source_target_pairs={{0,2},{1,3},{2,0},{3,1},{4,6},{5,7},{6,4},{7,5},{8,10},{9,11},{10,... | collective-permute-start | bytes 700424 | tf_op jit(solution)/shard_map/ppermute | solution.py:29
  17.4 17.0 %collective-permute-start.3 = (bf16[3,304,128]{2,1,0:T(8,128)(2,1)S(1)}, bf16[3,304,128]{2,1,0:T(8,128)(2,1)S(1)}, u32[]{:S(2)}, u32[]{:S(2)}) collective-permute-start(bf16[3,304,128]{2,1,0:T(8,128)(2,1)S(1)} %get-tuple-element.34), channel_id=1, source_target_pairs={{0,4},{1,5},{2,6},{3,7},{4,0},{5,1},{6,2},{7,3},{8,12},{9,13},{10,... | collective-permute-start | bytes 700424 | tf_op jit(solution)/shard_map/ppermute | solution.py:29
  37.0 1.6 %collective-permute-start.9 = (bf16[32,3584]{1,0:T(8,128)(2,1)S(1)}, bf16[32,3584]{1,0:T(8,128)(2,1)S(1)}, u32[]{:S(2)}, u32[]{:S(2)}) collective-permute-start(bf16[32,3584]{1,0:T(8,128)(2,1)S(1)} %get-tuple-element.50), channel_id=1, source_target_pairs={{0,1},{1,0},{2,3},{3,2},{4,5},{5,4},{6,7},{7,6},{8,9},{9,8},{10,11... | collective-permute-start | bytes 688136 | tf_op jit(solution)/shard_map/ppermute | solution.py:29
  39.2 4.2 %collective-permute-start.10 = (bf16[32,896]{1,0:T(8,128)(2,1)S(1)}, bf16[32,896]{1,0:T(8,128)(2,1)S(1)}, u32[]{:S(2)}, u32[]{:S(2)}) collective-permute-start(bf16[32,896]{1,0:T(8,128)(2,1)S(1)} %get-tuple-element.52), channel_id=1, source_target_pairs={{0,8},{8,0},{16,24},{24,16},{1,9},{9,1},{17,25},{25,17},{2,10},{10... | collective-permute-start | bytes 172040 | tf_op jit(solution)/shard_map/ppermute | solution.py:29
  40.7 4.2 %collective-permute-start.11 = (bf16[32,896]{1,0:T(8,128)(2,1)S(1)}, bf16[32,896]{1,0:T(8,128)(2,1)S(1)}, u32[]{:S(2)}, u32[]{:S(2)}) collective-permute-start(bf16[32,896]{1,0:T(8,128)(2,1)S(1)} %get-tuple-element.53), channel_id=1, source_target_pairs={{0,16},{8,24},{16,0},{24,8},{1,17},{9,25},{17,1},{25,9},{2,18},{10... | collective-permute-start | bytes 172040 | tf_op jit(solution)/shard_map/ppermute | solution.py:29
  42.2 5.1 %collective-permute-start.12 = (bf16[32,896]{1,0:T(8,128)(2,1)S(1)}, bf16[32,896]{1,0:T(8,128)(2,1)S(1)}, u32[]{:S(2)}, u32[]{:S(2)}) collective-permute-start(bf16[32,896]{1,0:T(8,128)(2,1)S(1)} %get-tuple-element.54), channel_id=1, source_target_pairs={{0,24},{8,16},{16,8},{24,0},{1,25},{9,17},{17,9},{25,1},{2,26},{10... | collective-permute-start | bytes 172040 | tf_op jit(solution)/shard_map/ppermute | solution.py:29

commit v3 on v2

v3 whole, which is shorter than its diff:
```python
import functools
import jax
import jax.numpy as jnp
from jax import lax
from jax.experimental import pallas as pl
from jax.experimental.pallas import tpu as pltpu
from jax.sharding import PartitionSpec as P

F32 = jnp.float32
BF16 = jnp.bfloat16
LANES = 128
CHUNK = 512
EXTRA = 8
VMEM = pl.BlockSpec(memory_space=pltpu.VMEM)
SMEM = pl.BlockSpec(memory_space=pltpu.SMEM)
HBM = pl.BlockSpec(memory_space=pltpu.HBM)
COSTS = (500000000, 1, 500000000)
CHEAP = pl.CostEstimate(flops=1, bytes_accessed=1, transcendentals=0)


def params(limit_mib):
    return pltpu.CompilerParams(vmem_limit_bytes=limit_mib << 20)


def up(value, multiple):
    return (value + multiple - 1) // multiple * multiple


def swap_with(x, axis, offset):
    size = lax.axis_size(axis)
    return lax.ppermute(x, axis, [(i, i ^ offset) for i in range(size)])


def join_kernel(wave_ref, tail_ref, out_ref, wave_held, tail_held, arrived):
    copies = [
        pltpu.make_async_copy(wave_ref, wave_held, arrived.at[0]),
        pltpu.make_async_copy(tail_ref, tail_held, arrived.at[1]),
    ]
    for copy in copies:
        copy.start()
    for copy in copies:
        copy.wait()
    samples = wave_held.shape[-1]
    out_ref[...] = jnp.zeros_like(out_ref)
    out_ref[:, :samples] = wave_held[...]
    out_ref[:, samples : samples + tail_held.shape[-1]] = tail_held[...]


def join(wave, tail):
    return pl.pallas_call(
        join_kernel,
        out_shape=jax.ShapeDtypeStruct((wave.shape[0], up(wave.shape[-1] + tail.shape[-1], LANES)), BF16),
        in_specs=[HBM] * 2,
        out_specs=VMEM,
        scratch_shapes=[pltpu.VMEM(x.shape, x.dtype) for x in (wave, tail)] + [pltpu.SemaphoreType.DMA((2,))],
        compiler_params=params(16),
        cost_estimate=CHEAP,
    )(*[pltpu.with_memory_space_constraint(x, pltpu.HBM) for x in (wave, tail)])


def fold_lags(rows, length):
    return up(-(-length // (LANES // rows)), 8)


def pack_kernel(parts, rows, length, starts_ref, tpl_ref, mask_ref, *refs):
    tpl_outs, (held_ref, mask_held, arrived) = refs[: len(parts)], refs[len(parts) :]
    lags = fold_lags(rows, length)
    comps = tpl_ref.shape[0]
    copies = [pltpu.make_async_copy(mask_ref, mask_held, arrived.at[comps])]
    copies += [pltpu.make_async_copy(tpl_ref.at[c], held_ref.at[c], arrived.at[c]) for c in range(comps)]
    for copy in copies:
        copy.start()
    copies[0].wait()
    lane = lax.broadcasted_iota(jnp.int32, (1, LANES), 1)
    for comp in range(comps):
        copies[1 + comp].wait()
        for index, (low, high) in enumerate(parts):
            if not low <= comp < high:
                continue
            row = starts_ref[index]
            tile = pl.multiple_of(row // LANES * LANES, LANES)
            mask = mask_held[:, pl.ds(tile, LANES)].astype(F32)
            values = held_ref[comp, :, pl.ds(tile, LANES)].astype(F32) * mask
            folded = jnp.zeros((lags, LANES), F32)
            for fold in range(LANES // rows):
                piece = values[fold * lags : min((fold + 1) * lags, length)]
                if piece.shape[0] == 0:
                    continue
                if piece.shape[0] < lags:
                    piece = jnp.concatenate([piece, jnp.zeros((lags - piece.shape[0], LANES), F32)], axis=0)
                turned = pltpu.roll(piece, (fold * rows - row % LANES + LANES) % LANES, 1)
                here = (lane >= fold * rows) & (lane < (fold + 1) * rows)
                folded = jnp.where(here, turned, folded)
            tpl_outs[index][comp - low] = folded.astype(BF16)


def pack(starts, parts, rows, tpl, mask):
    comps, length, _ = tpl.shape
    lags = fold_lags(rows, length)
    return pl.pallas_call(
        functools.partial(pack_kernel, parts, rows, length),
        out_shape=[jax.ShapeDtypeStruct((high - low, lags, LANES), BF16) for low, high in parts],
        in_specs=[SMEM] + [HBM] * 2,
        out_specs=[VMEM] * len(parts),
        scratch_shapes=[pltpu.VMEM(x.shape, x.dtype) for x in (tpl, mask)]
        + [pltpu.SemaphoreType.DMA((comps + 1,))],
        compiler_params=params(16),
        cost_estimate=CHEAP,
    )(starts, *[pltpu.with_memory_space_constraint(x, pltpu.HBM) for x in (tpl, mask)])


def fill_samples(halo, tm_index, shard_refs, tail_refs, ext_ref):
    chips, comps, samples = shard_refs[0].shape
    total = samples * len(shard_refs)
    ext_ref[...] = jnp.zeros_like(ext_ref)
    for chip in range(chips):
        at = chip * comps
        for offset, ref in enumerate(shard_refs):
            start = pl.multiple_of((tm_index ^ offset) * samples, LANES)
            ext_ref[at : at + comps, pl.ds(start, samples)] = ref[chip].astype(F32)
        ext_ref[at : at + comps, total : total + halo] = tail_refs[chip][:, samples : samples + halo].astype(F32)


def fill_inverse(length, ext_ref, both_ref, inv_ref):
    count, width = ext_ref.shape
    total = inv_ref.shape[-1]
    both_ref[:count, :] = ext_ref[...]
    both_ref[count : 2 * count, :] = ext_ref[...] * ext_ref[...]
    result, done, span, doubled = None, 0, 1, both_ref[: 2 * count, :]
    while span <= length:
        if length & span:
            part = doubled if done == 0 else pltpu.roll(doubled, width - done, 1)
            result = part if result is None else result + part
            done += span
        span *= 2
        if span <= length:
            doubled = doubled + pltpu.roll(doubled, width - span // 2, 1)
    both_ref[: 2 * count, :] = result
    window_sum = both_ref[:count, :total]
    window_square = both_ref[count : 2 * count, :total]
    inv_ref[...] = lax.rsqrt(window_square - window_sum * window_sum / length + 1e-05)


def lag_rows(values, rows, length):
    lags = values.shape[0]
    folds = LANES // rows
    splits = -(-length // (2 * LANES))

    def over_folds(total):
        span = rows
        while span < LANES:
            total = total + pltpu.roll(total, span, 1)
            span *= 2
        return total

    lane = lax.broadcasted_iota(jnp.int32, values.shape, 1)
    lag = lax.broadcasted_iota(jnp.int32, values.shape, 0) + lane // rows * lags
    mean = over_folds(jnp.sum(values, axis=0, keepdims=True)) / length
    centred = jnp.where(lag < length, values - mean, 0.0)
    energy = over_folds(jnp.sum(centred * centred, axis=0, keepdims=True))
    weighted = centred * lax.rsqrt(energy + 1e-05)
    parts = [weighted] + [pltpu.roll(weighted, LANES - fold * rows, 1) for fold in range(1, folds)]
    wanted = splits * 2 * LANES
    if folds * lags < wanted:
        parts.append(jnp.zeros((wanted - folds * lags, LANES), F32))
    spread = jnp.concatenate(parts, axis=0)
    low = lax.broadcasted_iota(jnp.int32, (LANES, LANES), 1) < LANES // 2
    flip = (
        lax.broadcasted_iota(jnp.int32, (LANES, LANES), 0)
        + lax.broadcasted_iota(jnp.int32, (LANES, LANES), 1)
        == LANES - 1
    ).astype(BF16)
    result = []
    for split in range(splits):
        at = split * 2 * LANES
        both = jnp.where(low, spread[at : at + LANES], pltpu.roll(spread[at + LANES : at + 2 * LANES], LANES // 2, 1))
        turned = lax.dot_general(
            both.astype(BF16), flip, (((0,), (0,)), ((), ())), preferred_element_type=F32
        )
        result.append(jnp.concatenate([turned[:rows], turned[LANES // 2 : LANES // 2 + rows]], axis=1))
    return jnp.concatenate(result, axis=0).astype(BF16)


def fill_hankel(row, out_ref):
    width = row.shape[-1]
    spread = jnp.broadcast_to(row.astype(BF16), (LANES, width))
    out_ref[...] = pltpu.roll(spread, width - (LANES - 1), 1, stride=1, stride_axis=0)


def multiply(ext_at, rows, length, tpl_ref, ext_ref, work_refs):
    hankel_ref, product_ref = work_refs
    reach = product_ref.shape[-1]
    for comp in range(tpl_ref.shape[0]):
        fill_hankel(ext_ref[ext_at + comp : ext_at + comp + 1, :], hankel_ref.at[comp])
    lhs = [lag_rows(tpl_ref[comp].astype(F32), rows, length) for comp in range(tpl_ref.shape[0])]
    for comp in range(tpl_ref.shape[0]):
        rhs = jnp.concatenate(
            [hankel_ref[comp, :, :reach], hankel_ref[comp, :, LANES : LANES + reach]], axis=0
        )
        product_ref[comp] = jnp.dot(lhs[comp], rhs, preferred_element_type=F32)


def collect(inv_at, rows, comps, inv_ref, acc_refs, work_refs, store):
    product_ref = work_refs[1]
    splits = product_ref.shape[1] // rows
    total = product_ref.shape[-1] - (splits - 1) * 2 * LANES
    for start in range(0, total, CHUNK):
        stop = min(start + CHUNK, total)
        chunk = None
        for ref in acc_refs:
            part = ref[:, start:stop]
            chunk = part if chunk is None else chunk + part
        for comp in range(comps):
            part = product_ref[comp, :rows, start:stop]
            for split in range(1, splits):
                shift = split * 2 * LANES
                part = part + product_ref[comp, split * rows : (split + 1) * rows, shift + start : shift + stop]
            part = part * inv_ref[inv_at + comp : inv_at + comp + 1, start:stop]
            chunk = part if chunk is None else chunk + part
        store(start, stop, chunk)


def correlate(at, rows, length, tpl_ref, ext_ref, inv_ref, acc_refs, work_refs, store):
    multiply(at, rows, length, tpl_ref, ext_ref, work_refs)
    collect(at, rows, tpl_ref.shape[0], inv_ref, acc_refs, work_refs, store)


def storing(ref):
    def store(start, stop, chunk):
        ref[:, start:stop] = chunk

    return store


def first_kernel(shards, chips, rows, length, halo, place_ref, tpl_ref, *refs):
    shard_refs, tail_refs = refs[:shards], refs[shards : shards + chips]
    ext_ref, inv_ref, sum_ref, both_ref, *work_refs = refs[shards + chips :]
    fill_samples(halo, place_ref[1], shard_refs, tail_refs, ext_ref)
    multiply(0, rows, length, tpl_ref, ext_ref, work_refs)
    fill_inverse(length, ext_ref, both_ref, inv_ref)
    collect(0, rows, tpl_ref.shape[0], inv_ref, [], work_refs, storing(sum_ref))


def middle_kernel(at, rows, length, tpl_ref, ext_ref, inv_ref, acc_ref, sum_ref, *work_refs):
    correlate(at, rows, length, tpl_ref, ext_ref, inv_ref, [acc_ref], work_refs, storing(sum_ref))


def parting_kernel(at, rows, length, place_ref, tpl_ref, ext_ref, inv_ref, acc_ref, keep_ref, send_ref, *work_refs):
    own = rows // 2
    low = place_ref[2] == 0

    def store(start, stop, chunk):
        keep_ref[:, start:stop] = jnp.where(low, chunk[:own], chunk[own:])
        send_ref[:, start:stop] = jnp.where(low, chunk[own:], chunk[:own]).astype(BF16)

    correlate(at, rows, length, tpl_ref, ext_ref, inv_ref, [acc_ref], work_refs, store)


def work_buffers(comps, rows, total, width, length):
    splits = -(-length // (2 * LANES))
    reach = total + (splits - 1) * 2 * LANES
    return [pltpu.VMEM((comps, LANES, width), BF16), pltpu.VMEM((comps, splits * rows, reach), F32)]


def first(place, rows, length, halo, tpl, shards, tails):
    chips, comps, samples = shards[0].shape
    total = samples * len(shards)
    width = total + up(length, LANES)
    count = chips * comps
    return pl.pallas_call(
        functools.partial(first_kernel, len(shards), chips, rows, length, halo),
        out_shape=[
            jax.ShapeDtypeStruct((count, width), F32),
            jax.ShapeDtypeStruct((count, total), F32),
            jax.ShapeDtypeStruct((rows, total), F32),
        ],
        in_specs=[SMEM] + [VMEM] * (1 + len(shards) + chips),
        out_specs=[VMEM] * 3,
        scratch_shapes=[pltpu.VMEM((up(2 * count, 8), width), F32)]
        + work_buffers(comps, rows, total, width, length),
        compiler_params=params(24),
        cost_estimate=CHEAP,
    )(place, tpl, *shards, *tails)


def later(kernel, place, rows, total, length, out_shape, inputs, scratch=(), flops=1):
    comps, width = inputs[0].shape[0], inputs[1].shape[-1]
    given = ([] if place is None else [place]) + list(inputs)
    specs = [VMEM] * len(inputs) if place is None else [SMEM] + [VMEM] * len(inputs)
    return pl.pallas_call(
        kernel,
        out_shape=out_shape,
        in_specs=specs,
        out_specs=[VMEM] * len(out_shape),
        scratch_shapes=list(scratch) + work_buffers(comps, rows, total, width, length),
        compiler_params=params(24),
        cost_estimate=pl.CostEstimate(flops=flops, bytes_accessed=1, transcendentals=0),
    )(*given)


def shard_kernel(place_ref, keep_ref, came_ref, own_ref, *send_refs):
    samples = own_ref.shape[-1]
    for offset, ref in enumerate((own_ref,) + send_refs):
        at = pl.multiple_of((place_ref[1] ^ offset) * samples, LANES)
        total = keep_ref[:, pl.ds(at, samples)] + came_ref[:, pl.ds(at, samples)].astype(F32)
        total = total.astype(ref.dtype)
        if ref.shape[0] > total.shape[0]:
            total = jnp.concatenate([total, jnp.zeros((ref.shape[0] - total.shape[0], samples), ref.dtype)], axis=0)
        ref[...] = total


def shard(place, keep, came, count):
    own, total = keep.shape
    samples = total // count
    return pl.pallas_call(
        shard_kernel,
        out_shape=[jax.ShapeDtypeStruct((own, samples), F32)]
        + [
            jax.ShapeDtypeStruct((own + (EXTRA if offset & (offset - 1) else 0), samples), BF16)
            for offset in range(1, count)
        ],
        in_specs=[SMEM, VMEM, VMEM],
        out_specs=[VMEM] * count,
        compiler_params=params(16),
        cost_estimate=CHEAP,
    )(place, keep, came)


def gather_kernel(place_ref, *refs):
    *part_refs, out_ref, held_ref, left = refs
    copies = []
    for offset, ref in enumerate(part_refs):
        held_ref[offset] = ref[: out_ref.shape[1], :].astype(F32)
        copies.append(
            pltpu.make_async_copy(held_ref.at[offset], out_ref.at[place_ref[1] ^ offset], left.at[offset])
        )
        copies[-1].start()
    for copy in copies:
        copy.wait()


def gather(place, parts):
    shape = (len(parts),) + parts[0].shape
    return pl.pallas_call(
        gather_kernel,
        out_shape=jax.ShapeDtypeStruct(shape, F32),
        in_specs=[SMEM] + [VMEM] * len(parts),
        out_specs=HBM,
        scratch_shapes=[pltpu.VMEM(shape, F32), pltpu.SemaphoreType.DMA((len(parts),))],
        compiler_params=params(16),
    )(place, *parts)


def per_device(templates, channel_mask, waveforms, waveform_tail):
    length = templates.shape[-1]
    samples = waveforms.shape[-1]
    halo = waveform_tail.shape[-1]
    tm_count = lax.axis_size("tm")
    chips = lax.axis_size("sta") // 2
    tm_index, sta_index = lax.axis_index("tm"), lax.axis_index("sta")
    chip_index, core_index = sta_index // 2, sta_index % 2
    place = jnp.stack([chip_index, tm_index, core_index]).astype(jnp.int32)
    tpl = jnp.transpose(templates[0, :, 0], (1, 2, 0))
    mask = channel_mask[..., 0]
    rows = tpl.shape[-1] // chips
    own = rows // 2
    total = samples * tm_count
    comps = tpl.shape[0]
    final = chips // 2
    between = [1] + [offset for offset in range(chips - 1, 1, -1) if offset != final]

    wave = join(waveforms[0], waveform_tail[0])
    waves = [wave] + [swap_with(wave, "sta", 2 * offset) for offset in range(1, chips)]
    offsets = [0] + between + [final, final]
    parts = [(0, comps)] * (len(offsets) - 2) + [(0, comps - 1), (comps - 1, comps)]
    starts = jnp.stack([(chip_index ^ offset) * rows for offset in offsets]).astype(jnp.int32)
    messages = pack(starts, parts, rows, tpl, mask)
    messages, waves = lax.optimization_barrier((messages, waves))
    pieces = {offset: swap_with(messages[1 + i], "sta", 2 * offset) for i, offset in enumerate(between)}
    stacked = jnp.stack([part[:, :samples] for part in waves])
    shards = [stacked] + [swap_with(stacked, "tm", offset) for offset in range(1, tm_count)]
    late, shards = lax.optimization_barrier((messages[-2:], shards))
    late = [swap_with(part, "sta", 2 * final) for part in late]
    ext, inv, acc = first(place, rows, length, halo, messages[0], shards, waves)
    whole = jax.ShapeDtypeStruct((rows, total), F32)
    stations = [(offset * comps, pieces[offset]) for offset in between] + [(final * comps, late[0])]
    for step, (at, piece) in enumerate(stations):
        kernel = functools.partial(middle_kernel, at, rows, length)
        flops = COSTS[min(step, len(COSTS) - 1)]
        (acc,) = later(kernel, None, rows, total, length, [whole], [piece, ext, inv, acc], flops=flops)
    kernel = functools.partial(parting_kernel, final * comps + comps - 1, rows, length)
    halves = [jax.ShapeDtypeStruct((own, total), F32), jax.ShapeDtypeStruct((own, total), BF16)]
    keep, send = later(kernel, place, rows, total, length, halves, [late[1], ext, inv, acc])
    parts = shard(place, keep, swap_with(send, "sta", 1), tm_count)
    parts = [parts[0]] + [swap_with(parts[offset], "tm", offset) for offset in range(1, tm_count)]
    return gather(place, parts)


def solution(mesh):
    placed = (
        P("tm", None, "sta", None, None),
        P("tm", None, "sta"),
        P("sta", None, "tm"),
        P("sta", None, None),
    )
    return jax.shard_map(
        per_device, mesh=mesh, in_specs=placed, out_specs=P(None, "sta", "tm"), check_vma=False
    )
```

time: 48.9 us -> 45.2 us (0.924)
  Pallas kernels: 18.3 us -> 15.8 us
  waiting for transfers between devices: 12.2 us -> 10.3 us
  starting transfers between devices: 17.9 us -> 18.4 us
    pallas_call x8 -> x7, Pallas kernels: 16.9 us -> 14.5 us  [the longest x4 7.43 us: later(): pl.pallas_call(kernel, out_shape=out_shape, in_specs=specs, out_specs=[VM...]
    ppermute x13 -> x14, waiting for transfers between devices: 12.2 us -> 10.3 us  [swap_with(): return lax.ppermute(x, axis, [(i, i ^ offset) for i in range(size)])]
    ppermute x13 -> x14, starting transfers between devices: 17.9 us -> 18.4 us  [swap_with(): return lax.ppermute(x, axis, [(i, i ^ offset) for i in range(size)])]
  transfers between devices with their start and end apart: 13 -> 14, of which waited for: 8 -> 8; matrix products, arithmetic and copies ran while one was open for 0% -> 0% of each run, Pallas kernels for 27% -> 25%
where the time goes in v3:
time: 45.2 us; the launch traced here: 44.9 us
  starting transfers between devices  18.4 us (41%)
  Pallas kernels  15.8 us (35%)
  waiting for transfers between devices  10.3 us (23%)
    ppermute x14, starting transfers between devices, swap_with(): return lax.ppermute(x, axis, [(i, i ^ offset) for i in range(size)])  18.4 us
    ppermute x14, waiting for transfers between devices, swap_with(): return lax.ppermute(x, axis, [(i, i ^ offset) for i in range(size)])  10.3 us
    pallas_call x4, Pallas kernels, later(): pl.pallas_call(kernel, out_shape=out_shape, in_specs=specs, out_specs=[VM...  7.43 us
    pallas_call x1, Pallas kernels, first(): pl.pallas_call(functools.partial(first_kernel, len(shards), chips, rows,...  3.41 us
    pallas_call x1, Pallas kernels, pack(): pl.pallas_call(functools.partial(pack_kernel, parts, rows, length), out_s...  2.28 us
    pallas_call x1, Pallas kernels, gather(): pl.pallas_call(gather_kernel, out_shape=jax.ShapeDtypeStruct(shape, F32),...  1.34 us
  transfers between devices with their start and end apart: 14, of which 8 were waited for; matrix products, arithmetic and copies ran while one was open for 0% of the time, Pallas kernels for 25%

profile of v3, /device:TPU:0, one launch (start us, length us, event | category | flops | bytes accessed | tf_op | source)
XLA Modules:
  0.0 44.9 jit_solution(27491292113672974)
XLA Ops:
  0.0 0.7 %shard_map.47.refs_4_ = bf16[3,1536]{1,0:T(4,128)(2,1)S(1)} custom-call(bf16[3,896]{1,0:T(4,128)(2,1)} %bitcast.22, bf16[3,599]{1,0:T(4,128)(2,1)} %bitcast.23), custom_call_target="tpu_custom_call" | custom-call | flops 1 | bytes 1 | tf_op jit(solution)/shard_map/pallas_call | solution.py:50
  0.7 5.1 %collective-permute-start.2 = (bf16[3,1536]{1,0:T(4,128)(2,1)S(1)}, bf16[3,1536]{1,0:T(4,128)(2,1)S(1)}, u32[]{:S(2)}, u32[]{:S(2)}) collective-permute-start(bf16[3,1536]{1,0:T(4,128)(2,1)S(1)} %shard_map.47.refs_4_), channel_id=1, source_target_pairs={{0,6},{1,7},{2,4},{3,5},{4,2},{5,3},{6,0},{7,1},{8,14},{9,15},{10,... | collective-permute-start | bytes 27656 | tf_op jit(solution)/shard_map/ppermute | solution.py:31
  5.9 0.0 collective-permute-start.1
  5.9 0.6 %collective-permute-start = (bf16[3,1536]{1,0:T(4,128)(2,1)S(1)}, bf16[3,1536]{1,0:T(4,128)(2,1)S(1)}, u32[]{:S(2)}, u32[]{:S(2)}) collective-permute-start(bf16[3,1536]{1,0:T(4,128)(2,1)S(1)} %shard_map.47.refs_4_), channel_id=1, source_target_pairs={{0,2},{1,3},{2,0},{3,1},{4,6},{5,7},{6,4},{7,5},{8,10},{9,11},{10,... | collective-permute-start | bytes 27656 | tf_op jit(solution)/shard_map/ppermute | solution.py:31
  6.5 0.1 stack.51.starts_ref
  6.6 2.3 %shard_map.46 = (bf16[3,304,128]{2,1,0:T(8,128)(2,1)S(1)}, bf16[3,304,128]{2,1,0:T(8,128)(2,1)S(1)}, bf16[3,304,128]{2,1,0:T(8,128)(2,1)S(1)}, bf16[2,304,128]{2,1,0:T(8,128)(2,1)S(1)}, bf16[1,304,128]{2,1,0:T(8,128)(2,1)S(1)}) custom-call(s32[5]{0:T(128)S(1)} %stack.51.starts_ref, bf16[3,600,256]{2,1,0:T(8,128)(2,1)} %bitcast.21, s32[1,256]{1,0:T(1,128)} %bitcast.24), custom_call_target="tpu_custom_call" | custom-call | flops 1 | bytes 1 | tf_op jit(solution)/shard_map/pallas_call | solution.py:100
  8.9 0.0 collective-permute-done.2.refs_7_
  8.9 1.6 %collective-permute-done.1.refs_6_ = bf16[3,1536]{1,0:T(4,128)(2,1)S(1)} collective-permute-done((bf16[3,1536]{1,0:T(4,128)(2,1)S(1)}, bf16[3,1536]{1,0:T(4,128)(2,1)S(1)}, u32[]{:S(2)}, u32[]{:S(2)}) %collective-permute-start.1) | collective-permute-done | bytes 9248 | tf_op jit(solution)/shard_map/ppermute | solution.py:31
  10.5 0.0 collective-permute-done.refs_5_
  10.5 2.3 %collective-permute-start.8 = (bf16[3,304,128]{2,1,0:T(8,128)(2,1)S(1)}, bf16[3,304,128]{2,1,0:T(8,128)(2,1)S(1)}, u32[]{:S(2)}, u32[]{:S(2)}) collective-permute-start(bf16[3,304,128]{2,1,0:T(8,128)(2,1)S(1)} %get-tuple-element.54), channel_id=1, source_target_pairs={{0,6},{1,7},{2,4},{3,5},{4,2},{5,3},{6,0},{7,1},{8,14},{9,15},{10,... | collective-permute-start | bytes 700424 | tf_op jit(solution)/shard_map/ppermute | solution.py:31
  12.7 0.3 collective-permute-start.9
  13.1 2.5 %collective-permute-start.5 = (bf16[4,3,896]{2,1,0:T(4,128)(2,1)S(1)}, bf16[4,3,896]{2,1,0:T(4,128)(2,1)S(1)}, u32[]{:S(2)}, u32[]{:S(2)}) collective-permute-start(bf16[4,3,896]{2,1,0:T(4,128)(2,1)S(1)} %pad_maximum_fusion.refs_0_), channel_id=1, source_target_pairs={{0,24},{8,16},{16,8},{24,0},{1,25},{9,17},{17,9},{25,1},{2,26},{10... | collective-permute-start | bytes 64520 | tf_op jit(solution)/shard_map/ppermute | solution.py:31
  15.6 0.5 %collective-permute-start.4 = (bf16[4,3,896]{2,1,0:T(4,128)(2,1)S(1)}, bf16[4,3,896]{2,1,0:T(4,128)(2,1)S(1)}, u32[]{:S(2)}, u32[]{:S(2)}) collective-permute-start(bf16[4,3,896]{2,1,0:T(4,128)(2,1)S(1)} %pad_maximum_fusion.refs_0_), channel_id=1, source_target_pairs={{0,16},{8,24},{16,0},{24,8},{1,17},{9,25},{17,1},{25,9},{2,18},{10... | collective-permute-start | bytes 64520 | tf_op jit(solution)/shard_map/ppermute | solution.py:31
  16.1 0.5 %collective-permute-start.3 = (bf16[4,3,896]{2,1,0:T(4,128)(2,1)S(1)}, bf16[4,3,896]{2,1,0:T(4,128)(2,1)S(1)}, u32[]{:S(2)}, u32[]{:S(2)}) collective-permute-start(bf16[4,3,896]{2,1,0:T(4,128)(2,1)S(1)} %pad_maximum_fusion.refs_0_), channel_id=1, source_target_pairs={{0,8},{8,0},{16,24},{24,16},{1,9},{9,1},{17,25},{25,17},{2,10},{10... | collective-permute-start | bytes 64520 | tf_op jit(solution)/shard_map/ppermute | solution.py:31
  16.7 1.5 %collective-permute-done.5.refs_3_ = bf16[4,3,896]{2,1,0:T(4,128)(2,1)S(1)} collective-permute-done((bf16[4,3,896]{2,1,0:T(4,128)(2,1)S(1)}, bf16[4,3,896]{2,1,0:T(4,128)(2,1)S(1)}, u32[]{:S(2)}, u32[]{:S(2)}) %collective-permute-start.5) | collective-permute-done | bytes 21536 | tf_op jit(solution)/shard_map/ppermute | solution.py:31
  18.1 1.4 %collective-permute-done.4.refs_2_ = bf16[4,3,896]{2,1,0:T(4,128)(2,1)S(1)} collective-permute-done((bf16[4,3,896]{2,1,0:T(4,128)(2,1)S(1)}, bf16[4,3,896]{2,1,0:T(4,128)(2,1)S(1)}, u32[]{:S(2)}, u32[]{:S(2)}) %collective-permute-start.4) | collective-permute-done | bytes 21536 | tf_op jit(solution)/shard_map/ppermute | solution.py:31
  19.5 0.5 %collective-permute-done.3.refs_1_ = bf16[4,3,896]{2,1,0:T(4,128)(2,1)S(1)} collective-permute-done((bf16[4,3,896]{2,1,0:T(4,128)(2,1)S(1)}, bf16[4,3,896]{2,1,0:T(4,128)(2,1)S(1)}, u32[]{:S(2)}, u32[]{:S(2)}) %collective-permute-start.3) | collective-permute-done | bytes 21536 | tf_op jit(solution)/shard_map/ppermute | solution.py:31
  20.0 1.8 %collective-permute-start.7 = (bf16[2,304,128]{2,1,0:T(8,128)(2,1)S(1)}, bf16[2,304,128]{2,1,0:T(8,128)(2,1)S(1)}, u32[]{:S(2)}, u32[]{:S(2)}) collective-permute-start(bf16[2,304,128]{2,1,0:T(8,128)(2,1)S(1)} %get-tuple-element.53), channel_id=1, source_target_pairs={{0,4},{1,5},{2,6},{3,7},{4,0},{5,1},{6,2},{7,3},{8,12},{9,13},{10,... | collective-permute-start | bytes 466952 | tf_op jit(solution)/shard_map/ppermute | solution.py:31
  21.8 0.1 pad_add_fusion.place_ref
  21.9 1.1 %collective-permute-start.6 = (bf16[1,304,128]{2,1,0:T(8,128)(2,1)S(1)}, bf16[1,304,128]{2,1,0:T(8,128)(2,1)S(1)}, u32[]{:S(2)}, u32[]{:S(2)}) collective-permute-start(bf16[1,304,128]{2,1,0:T(8,128)(2,1)S(1)} %get-tuple-element.45), channel_id=1, source_target_pairs={{0,4},{1,5},{2,6},{3,7},{4,0},{5,1},{6,2},{7,3},{8,12},{9,13},{10,... | collective-permute-start | bytes 233480 | tf_op jit(solution)/shard_map/ppermute | solution.py:31
  23.0 3.4 %shard_map.48 = (f32[12,4224]{1,0:T(8,128)S(1)}, f32[12,3584]{1,0:T(8,128)S(1)}, f32[64,3584]{1,0:T(8,128)S(1)}) custom-call(s32[3]{0:T(128)S(1)} %pad_add_fusion.place_ref, bf16[3,304,128]{2,1,0:T(8,128)(2,1)S(1)} %get-tuple-element.46.tpl_ref, bf16[4,3,896]{2,1,0:T(4,128)(2,1)S(1)} %pad_maximum_fusion.refs_0_, ...), custom_call_target="tpu_custom_call" | custom-call | flops 1 | bytes 1 | tf_op jit(solution)/shard_map/pallas_call | solution.py:270
  26.4 0.0 collective-permute-done.9.tpl_ref
  26.4 2.1 %shard_map.49.acc_ref = f32[64,3584]{1,0:T(8,128)S(1)} custom-call(bf16[3,304,128]{2,1,0:T(8,128)(2,1)S(1)} %collective-permute-done.9.tpl_ref, f32[12,4224]{1,0:T(8,128)S(1)} %get-tuple-element.51.ext_ref, f32[12,3584]{1,0:T(8,128)S(1)} %get-tuple-element.52.inv_ref, f32[64,3584]{1,0:T(8,128)S(1)} %get-tuple-element.56.acc_ref), custom_call_target="tpu_custom_call" | custom-call | flops 500000000 | bytes 1 | tf_op jit(solution)/shard_map/pallas_call | solution.py:290
  28.5 0.0 collective-permute-done.8.tpl_ref
  28.5 2.1 %shard_map.50.acc_ref = f32[64,3584]{1,0:T(8,128)S(1)} custom-call(bf16[3,304,128]{2,1,0:T(8,128)(2,1)S(1)} %collective-permute-done.8.tpl_ref, f32[12,4224]{1,0:T(8,128)S(1)} %get-tuple-element.51.ext_ref, f32[12,3584]{1,0:T(8,128)S(1)} %get-tuple-element.52.inv_ref, f32[64,3584]{1,0:T(8,128)S(1)} %shard_map.49.acc_ref), custom_call_target="tpu_custom_call" | custom-call | flops 1 | bytes 1 | tf_op jit(solution)/shard_map/pallas_call | solution.py:290
  30.6 0.3 collective-permute-done.7.tpl_ref
  30.8 1.6 %shard_map.51.acc_ref = f32[64,3584]{1,0:T(8,128)S(1)} custom-call(bf16[2,304,128]{2,1,0:T(8,128)(2,1)S(1)} %collective-permute-done.7.tpl_ref, f32[12,4224]{1,0:T(8,128)S(1)} %get-tuple-element.51.ext_ref, f32[12,3584]{1,0:T(8,128)S(1)} %get-tuple-element.52.inv_ref, f32[64,3584]{1,0:T(8,128)S(1)} %shard_map.50.acc_ref), custom_call_target="tpu_custom_call" | custom-call | flops 500000000 | bytes 1 | tf_op jit(solution)/shard_map/pallas_call | solution.py:290
  32.5 0.0 collective-permute-done.6.tpl_ref
  32.5 1.7 %shard_map.52 = (f32[32,3584]{1,0:T(8,128)S(1)}, bf16[32,3584]{1,0:T(8,128)(2,1)S(1)}) custom-call(s32[3]{0:T(128)S(1)} %pad_add_fusion.place_ref, bf16[1,304,128]{2,1,0:T(8,128)(2,1)S(1)} %collective-permute-done.6.tpl_ref, f32[12,4224]{1,0:T(8,128)S(1)} %get-tuple-element.51.ext_ref, f32[12,3584]{1,0:T(8,128)S(1)} %get-tuple-element.52.inv_ref, ...), custom_call_target="tpu_custom_call" | custom-call | flops 1 | bytes 1 | tf_op jit(solution)/shard_map/pallas_call | solution.py:290
  34.2 0.1 collective-permute-start.10
  34.3 1.5 %collective-permute-done.10.came_ref = bf16[32,3584]{1,0:T(8,128)(2,1)S(1)} collective-permute-done((bf16[32,3584]{1,0:T(8,128)(2,1)S(1)}, bf16[32,3584]{1,0:T(8,128)(2,1)S(1)}, u32[]{:S(2)}, u32[]{:S(2)}) %collective-permute-start.10) | collective-permute-done | bytes 229408 | tf_op jit(solution)/shard_map/ppermute | solution.py:31
  35.7 0.6 %shard_map.53 = (f32[32,896]{1,0:T(8,128)S(1)}, bf16[32,896]{1,0:T(8,128)(2,1)S(1)}, bf16[32,896]{1,0:T(8,128)(2,1)S(1)}, bf16[40,896]{1,0:T(8,128)(2,1)S(1)}) custom-call(s32[3]{0:T(128)S(1)} %pad_add_fusion.place_ref, f32[32,3584]{1,0:T(8,128)S(1)} %get-tuple-element.57.keep_ref, bf16[32,3584]{1,0:T(8,128)(2,1)S(1)} %collective-permute-done.10.came_ref), custom_call_target="tpu_custom_call" | custom-call | flops 1 | bytes 1 | tf_op jit(solution)/shard_map/pallas_call | solution.py:315
  36.3 2.5 %collective-permute-start.13 = (bf16[40,896]{1,0:T(8,128)(2,1)S(1)}, bf16[40,896]{1,0:T(8,128)(2,1)S(1)}, u32[]{:S(2)}, u32[]{:S(2)}) collective-permute-start(bf16[40,896]{1,0:T(8,128)(2,1)S(1)} %get-tuple-element.62), channel_id=1, source_target_pairs={{0,24},{8,16},{16,8},{24,0},{1,25},{9,17},{17,9},{25,1},{2,26},{10... | collective-permute-start | bytes 215048 | tf_op jit(solution)/shard_map/ppermute | solution.py:31
  38.9 0.5 %collective-permute-start.11 = (bf16[32,896]{1,0:T(8,128)(2,1)S(1)}, bf16[32,896]{1,0:T(8,128)(2,1)S(1)}, u32[]{:S(2)}, u32[]{:S(2)}) collective-permute-start(bf16[32,896]{1,0:T(8,128)(2,1)S(1)} %get-tuple-element.60), channel_id=1, source_target_pairs={{0,8},{8,0},{16,24},{24,16},{1,9},{9,1},{17,25},{25,17},{2,10},{10... | collective-permute-start | bytes 172040 | tf_op jit(solution)/shard_map/ppermute | solution.py:31
  39.4 0.5 %collective-permute-start.12 = (bf16[32,896]{1,0:T(8,128)(2,1)S(1)}, bf16[32,896]{1,0:T(8,128)(2,1)S(1)}, u32[]{:S(2)}, u32[]{:S(2)}) collective-permute-start(bf16[32,896]{1,0:T(8,128)(2,1)S(1)} %get-tuple-element.61), channel_id=1, source_target_pairs={{0,16},{8,24},{16,0},{24,8},{1,17},{9,25},{17,1},{25,9},{2,18},{10... | collective-permute-start | bytes 172040 | tf_op jit(solution)/shard_map/ppermute | solution.py:31
  39.9 3.1 %collective-permute-done.11.refs_1_ = bf16[32,896]{1,0:T(8,128)(2,1)S(1)} collective-permute-done((bf16[32,896]{1,0:T(8,128)(2,1)S(1)}, bf16[32,896]{1,0:T(8,128)(2,1)S(1)}, u32[]{:S(2)}, u32[]{:S(2)}) %collective-permute-start.11) | collective-permute-done | bytes 57376 | tf_op jit(solution)/shard_map/ppermute | solution.py:31
  43.0 0.5 %collective-permute-done.12.refs_2_ = bf16[32,896]{1,0:T(8,128)(2,1)S(1)} collective-permute-done((bf16[32,896]{1,0:T(8,128)(2,1)S(1)}, bf16[32,896]{1,0:T(8,128)(2,1)S(1)}, u32[]{:S(2)}, u32[]{:S(2)}) %collective-permute-start.12) | collective-permute-done | bytes 57376 | tf_op jit(solution)/shard_map/ppermute | solution.py:31
  43.6 0.0 collective-permute-done.13.refs_3_
  43.6 1.3 %shard_map.54 = f32[4,32,896]{2,1,0:T(8,128)} custom-call(s32[3]{0:T(128)S(1)} %pad_add_fusion.place_ref, f32[32,896]{1,0:T(8,128)S(1)} %get-tuple-element.59.refs_0_, bf16[32,896]{1,0:T(8,128)(2,1)S(1)} %collective-permute-done.11.refs_1_, bf16[32,896]{1,0:T(8,128)(2,1)S(1)} %collective-permute-done.12.refs_2_, ...), custom_call_target="tpu_custom_call" | custom-call | tf_op jit(solution)/shard_map/pallas_call | solution.py:344
  (3 shorter events, 0.0 us)
Async XLA Ops:
  0.7 8.1 %collective-permute-start.2 = (bf16[3,1536]{1,0:T(4,128)(2,1)S(1)}, bf16[3,1536]{1,0:T(4,128)(2,1)S(1)}, u32[]{:S(2)}, u32[]{:S(2)}) collective-permute-start(bf16[3,1536]{1,0:T(4,128)(2,1)S(1)} %shard_map.47.refs_4_), channel_id=1, source_target_pairs={{0,6},{1,7},{2,4},{3,5},{4,2},{5,3},{6,0},{7,1},{8,14},{9,15},{10,... | collective-permute-start | bytes 27656 | tf_op jit(solution)/shard_map/ppermute | solution.py:31
  5.9 4.6 %collective-permute-start.1 = (bf16[3,1536]{1,0:T(4,128)(2,1)S(1)}, bf16[3,1536]{1,0:T(4,128)(2,1)S(1)}, u32[]{:S(2)}, u32[]{:S(2)}) collective-permute-start(bf16[3,1536]{1,0:T(4,128)(2,1)S(1)} %shard_map.47.refs_4_), channel_id=1, source_target_pairs={{0,4},{1,5},{2,6},{3,7},{4,0},{5,1},{6,2},{7,3},{8,12},{9,13},{10,... | collective-permute-start | bytes 27656 | tf_op jit(solution)/shard_map/ppermute | solution.py:31
  5.9 4.6 %collective-permute-start = (bf16[3,1536]{1,0:T(4,128)(2,1)S(1)}, bf16[3,1536]{1,0:T(4,128)(2,1)S(1)}, u32[]{:S(2)}, u32[]{:S(2)}) collective-permute-start(bf16[3,1536]{1,0:T(4,128)(2,1)S(1)} %shard_map.47.refs_4_), channel_id=1, source_target_pairs={{0,2},{1,3},{2,0},{3,1},{4,6},{5,7},{6,4},{7,5},{8,10},{9,11},{10,... | collective-permute-start | bytes 27656 | tf_op jit(solution)/shard_map/ppermute | solution.py:31
  10.5 18.0 %collective-permute-start.8 = (bf16[3,304,128]{2,1,0:T(8,128)(2,1)S(1)}, bf16[3,304,128]{2,1,0:T(8,128)(2,1)S(1)}, u32[]{:S(2)}, u32[]{:S(2)}) collective-permute-start(bf16[3,304,128]{2,1,0:T(8,128)(2,1)S(1)} %get-tuple-element.54), channel_id=1, source_target_pairs={{0,6},{1,7},{2,4},{3,5},{4,2},{5,3},{6,0},{7,1},{8,14},{9,15},{10,... | collective-permute-start | bytes 700424 | tf_op jit(solution)/shard_map/ppermute | solution.py:31
  12.7 13.7 %collective-permute-start.9 = (bf16[3,304,128]{2,1,0:T(8,128)(2,1)S(1)}, bf16[3,304,128]{2,1,0:T(8,128)(2,1)S(1)}, u32[]{:S(2)}, u32[]{:S(2)}) collective-permute-start(bf16[3,304,128]{2,1,0:T(8,128)(2,1)S(1)} %get-tuple-element.55), channel_id=1, source_target_pairs={{0,2},{1,3},{2,0},{3,1},{4,6},{5,7},{6,4},{7,5},{8,10},{9,11},{10,... | collective-permute-start | bytes 700424 | tf_op jit(solution)/shard_map/ppermute | solution.py:31
  13.1 5.0 %collective-permute-start.5 = (bf16[4,3,896]{2,1,0:T(4,128)(2,1)S(1)}, bf16[4,3,896]{2,1,0:T(4,128)(2,1)S(1)}, u32[]{:S(2)}, u32[]{:S(2)}) collective-permute-start(bf16[4,3,896]{2,1,0:T(4,128)(2,1)S(1)} %pad_maximum_fusion.refs_0_), channel_id=1, source_target_pairs={{0,24},{8,16},{16,8},{24,0},{1,25},{9,17},{17,9},{25,1},{2,26},{10... | collective-permute-start | bytes 64520 | tf_op jit(solution)/shard_map/ppermute | solution.py:31
  15.6 3.9 %collective-permute-start.4 = (bf16[4,3,896]{2,1,0:T(4,128)(2,1)S(1)}, bf16[4,3,896]{2,1,0:T(4,128)(2,1)S(1)}, u32[]{:S(2)}, u32[]{:S(2)}) collective-permute-start(bf16[4,3,896]{2,1,0:T(4,128)(2,1)S(1)} %pad_maximum_fusion.refs_0_), channel_id=1, source_target_pairs={{0,16},{8,24},{16,0},{24,8},{1,17},{9,25},{17,1},{25,9},{2,18},{10... | collective-permute-start | bytes 64520 | tf_op jit(solution)/shard_map/ppermute | solution.py:31
  16.1 3.9 %collective-permute-start.3 = (bf16[4,3,896]{2,1,0:T(4,128)(2,1)S(1)}, bf16[4,3,896]{2,1,0:T(4,128)(2,1)S(1)}, u32[]{:S(2)}, u32[]{:S(2)}) collective-permute-start(bf16[4,3,896]{2,1,0:T(4,128)(2,1)S(1)} %pad_maximum_fusion.refs_0_), channel_id=1, source_target_pairs={{0,8},{8,0},{16,24},{24,16},{1,9},{9,1},{17,25},{25,17},{2,10},{10... | collective-permute-start | bytes 64520 | tf_op jit(solution)/shard_map/ppermute | solution.py:31
  20.0 10.9 %collective-permute-start.7 = (bf16[2,304,128]{2,1,0:T(8,128)(2,1)S(1)}, bf16[2,304,128]{2,1,0:T(8,128)(2,1)S(1)}, u32[]{:S(2)}, u32[]{:S(2)}) collective-permute-start(bf16[2,304,128]{2,1,0:T(8,128)(2,1)S(1)} %get-tuple-element.53), channel_id=1, source_target_pairs={{0,4},{1,5},{2,6},{3,7},{4,0},{5,1},{6,2},{7,3},{8,12},{9,13},{10,... | collective-permute-start | bytes 466952 | tf_op jit(solution)/shard_map/ppermute | solution.py:31
  21.9 10.6 %collective-permute-start.6 = (bf16[1,304,128]{2,1,0:T(8,128)(2,1)S(1)}, bf16[1,304,128]{2,1,0:T(8,128)(2,1)S(1)}, u32[]{:S(2)}, u32[]{:S(2)}) collective-permute-start(bf16[1,304,128]{2,1,0:T(8,128)(2,1)S(1)} %get-tuple-element.45), channel_id=1, source_target_pairs={{0,4},{1,5},{2,6},{3,7},{4,0},{5,1},{6,2},{7,3},{8,12},{9,13},{10,... | collective-permute-start | bytes 233480 | tf_op jit(solution)/shard_map/ppermute | solution.py:31
  34.2 1.6 %collective-permute-start.10 = (bf16[32,3584]{1,0:T(8,128)(2,1)S(1)}, bf16[32,3584]{1,0:T(8,128)(2,1)S(1)}, u32[]{:S(2)}, u32[]{:S(2)}) collective-permute-start(bf16[32,3584]{1,0:T(8,128)(2,1)S(1)} %get-tuple-element.58), channel_id=1, source_target_pairs={{0,1},{1,0},{2,3},{3,2},{4,5},{5,4},{6,7},{7,6},{8,9},{9,8},{10,11... | collective-permute-start | bytes 688136 | tf_op jit(solution)/shard_map/ppermute | solution.py:31
  36.3 7.2 %collective-permute-start.13 = (bf16[40,896]{1,0:T(8,128)(2,1)S(1)}, bf16[40,896]{1,0:T(8,128)(2,1)S(1)}, u32[]{:S(2)}, u32[]{:S(2)}) collective-permute-start(bf16[40,896]{1,0:T(8,128)(2,1)S(1)} %get-tuple-element.62), channel_id=1, source_target_pairs={{0,24},{8,16},{16,8},{24,0},{1,25},{9,17},{17,9},{25,1},{2,26},{10... | collective-permute-start | bytes 215048 | tf_op jit(solution)/shard_map/ppermute | solution.py:31
  38.9 4.2 %collective-permute-start.11 = (bf16[32,896]{1,0:T(8,128)(2,1)S(1)}, bf16[32,896]{1,0:T(8,128)(2,1)S(1)}, u32[]{:S(2)}, u32[]{:S(2)}) collective-permute-start(bf16[32,896]{1,0:T(8,128)(2,1)S(1)} %get-tuple-element.60), channel_id=1, source_target_pairs={{0,8},{8,0},{16,24},{24,16},{1,9},{9,1},{17,25},{25,17},{2,10},{10... | collective-permute-start | bytes 172040 | tf_op jit(solution)/shard_map/ppermute | solution.py:31
  39.4 4.2 %collective-permute-start.12 = (bf16[32,896]{1,0:T(8,128)(2,1)S(1)}, bf16[32,896]{1,0:T(8,128)(2,1)S(1)}, u32[]{:S(2)}, u32[]{:S(2)}) collective-permute-start(bf16[32,896]{1,0:T(8,128)(2,1)S(1)} %get-tuple-element.61), channel_id=1, source_target_pairs={{0,16},{8,24},{16,0},{24,8},{1,17},{9,25},{17,1},{25,9},{2,18},{10... | collective-permute-start | bytes 172040 | tf_op jit(solution)/shard_map/ppermute | solution.py:31

commit v4 on v3

--- a/solution.py
+++ b/solution.py
@@ -12,9 +12,8 @@
 CHUNK = 512
 EXTRA = 8
 VMEM = pl.BlockSpec(memory_space=pltpu.VMEM)
-SMEM = pl.BlockSpec(memory_space=pltpu.SMEM)
 HBM = pl.BlockSpec(memory_space=pltpu.HBM)
-COSTS = (500000000, 1, 500000000)
+F_MID, F_PART, F_JOIN, F_CLOSE = 500000000, 1, 500000000, 1
 CHEAP = pl.CostEstimate(flops=1, bytes_accessed=1, transcendentals=0)
 
 
@@ -58,13 +57,19 @@
     )(*[pltpu.with_memory_space_constraint(x, pltpu.HBM) for x in (wave, tail)])
 
 
+def first_row(chip_offset, core_offset, all_rows):
+    index = lax.axis_index("sta")
+    rows = all_rows // (lax.axis_size("sta") // 2)
+    row = (index // 2 ^ chip_offset) * rows
+    return row if core_offset is None else row + (index % 2 ^ core_offset) * (rows // 2)
+
+
 def fold_lags(rows, length):
     return up(-(-length // (LANES // rows)), 8)
 
 
-def pack_kernel(parts, rows, length, starts_ref, tpl_ref, mask_ref, *refs):
-    tpl_outs, (held_ref, mask_held, arrived) = refs[: len(parts)], refs[len(parts) :]
-    lags = fold_lags(rows, length)
+def pack_kernel(targets, counts, length, tpl_ref, mask_ref, *refs):
+    tpl_outs, (held_ref, mask_held, arrived) = refs[: len(counts)], refs[len(counts) :]
     comps = tpl_ref.shape[0]
     copies = [pltpu.make_async_copy(mask_ref, mask_held, arrived.at[comps])]
     copies += [pltpu.make_async_copy(tpl_ref.at[c], held_ref.at[c], arrived.at[c]) for c in range(comps)]
@@ -74,10 +79,9 @@
     lane = lax.broadcasted_iota(jnp.int32, (1, LANES), 1)
     for comp in range(comps):
         copies[1 + comp].wait()
-        for index, (low, high) in enumerate(parts):
-            if not low <= comp < high:
-                continue
-            row = starts_ref[index]
+        for index, rows in enumerate(counts):
+            lags = fold_lags(rows, length)
+            row = first_row(*targets[index], tpl_ref.shape[-1])
             tile = pl.multiple_of(row // LANES * LANES, LANES)
             mask = mask_held[:, pl.ds(tile, LANES)].astype(F32)
             values = held_ref[comp, :, pl.ds(tile, LANES)].astype(F32) * mask
@@ -91,22 +95,21 @@
                 turned = pltpu.roll(piece, (fold * rows - row % LANES + LANES) % LANES, 1)
                 here = (lane >= fold * rows) & (lane < (fold + 1) * rows)
                 folded = jnp.where(here, turned, folded)
-            tpl_outs[index][comp - low] = folded.astype(BF16)
-
-
-def pack(starts, parts, rows, tpl, mask):
+            tpl_outs[index][comp] = folded.astype(BF16)
+
+
+def pack(targets, counts, tpl, mask):
     comps, length, _ = tpl.shape
-    lags = fold_lags(rows, length)
     return pl.pallas_call(
-        functools.partial(pack_kernel, parts, rows, length),
-        out_shape=[jax.ShapeDtypeStruct((high - low, lags, LANES), BF16) for low, high in parts],
-        in_specs=[SMEM] + [HBM] * 2,
-        out_specs=[VMEM] * len(parts),
+        functools.partial(pack_kernel, targets, counts, length),
+        out_shape=[jax.ShapeDtypeStruct((comps, fold_lags(rows, length), LANES), BF16) for rows in counts],
+        in_specs=[HBM] * 2,
+        out_specs=[VMEM] * len(counts),
         scratch_shapes=[pltpu.VMEM(x.shape, x.dtype) for x in (tpl, mask)]
         + [pltpu.SemaphoreType.DMA((comps + 1,))],
         compiler_params=params(16),
         cost_estimate=CHEAP,
-    )(starts, *[pltpu.with_memory_space_constraint(x, pltpu.HBM) for x in (tpl, mask)])
+    )(*[pltpu.with_memory_space_constraint(x, pltpu.HBM) for x in (tpl, mask)])
 
 
 def fill_samples(halo, tm_index, shard_refs, tail_refs, ext_ref):
@@ -200,60 +203,101 @@
         product_ref[comp] = jnp.dot(lhs[comp], rhs, preferred_element_type=F32)
 
 
-def collect(inv_at, rows, comps, inv_ref, acc_refs, work_refs, store):
+def collect(inv_at, rows, comps, inv_ref, acc_refs, work_refs, spans):
     product_ref = work_refs[1]
     splits = product_ref.shape[1] // rows
-    total = product_ref.shape[-1] - (splits - 1) * 2 * LANES
-    for start in range(0, total, CHUNK):
-        stop = min(start + CHUNK, total)
+    for start, size, store in spans:
         chunk = None
         for ref in acc_refs:
-            part = ref[:, start:stop]
+            part = ref[:, pl.ds(start, size)]
             chunk = part if chunk is None else chunk + part
         for comp in range(comps):
-            part = product_ref[comp, :rows, start:stop]
+            part = product_ref[comp, :rows, pl.ds(start, size)]
             for split in range(1, splits):
                 shift = split * 2 * LANES
-                part = part + product_ref[comp, split * rows : (split + 1) * rows, shift + start : shift + stop]
-            part = part * inv_ref[inv_at + comp : inv_at + comp + 1, start:stop]
+                part = part + product_ref[comp, split * rows : (split + 1) * rows, pl.ds(start + shift, size)]
+            part = part * inv_ref[inv_at + comp : inv_at + comp + 1, pl.ds(start, size)]
             chunk = part if chunk is None else chunk + part
-        store(start, stop, chunk)
+        store(chunk)
+
+
+def spans_of(total, store):
+    return [
+        (start, min(CHUNK, total - start), functools.partial(store, start)) for start in range(0, total, CHUNK)
+    ]
+
+
+def storing(ref):
+    def store(start, chunk):
+        ref[:, start : start + chunk.shape[1]] = chunk
+
+    return store
 
 
 def correlate(at, rows, length, tpl_ref, ext_ref, inv_ref, acc_refs, work_refs, store):
     multiply(at, rows, length, tpl_ref, ext_ref, work_refs)
-    collect(at, rows, tpl_ref.shape[0], inv_ref, acc_refs, work_refs, store)
-
-
-def storing(ref):
-    def store(start, stop, chunk):
-        ref[:, start:stop] = chunk
-
-    return store
-
-
-def first_kernel(shards, chips, rows, length, halo, place_ref, tpl_ref, *refs):
+    spans = spans_of(inv_ref.shape[-1], store)
+    collect(at, rows, tpl_ref.shape[0], inv_ref, acc_refs, work_refs, spans)
+
+
+def first_kernel(shards, chips, rows, length, halo, crossing, tpl_ref, *refs):
     shard_refs, tail_refs = refs[:shards], refs[shards : shards + chips]
-    ext_ref, inv_ref, sum_ref, both_ref, *work_refs = refs[shards + chips :]
-    fill_samples(halo, place_ref[1], shard_refs, tail_refs, ext_ref)
+    ext_ref, inv_ref, cross_ref, sum_ref, both_ref, *work_refs = refs[shards + chips :]
+    comps, total = tpl_ref.shape[0], inv_ref.shape[-1]
+    fill_samples(halo, lax.axis_index("tm"), shard_refs, tail_refs, ext_ref)
     multiply(0, rows, length, tpl_ref, ext_ref, work_refs)
     fill_inverse(length, ext_ref, both_ref, inv_ref)
-    collect(0, rows, tpl_ref.shape[0], inv_ref, [], work_refs, storing(sum_ref))
+    cross_ref[:comps, :] = ext_ref[crossing * comps : (crossing + 1) * comps, :]
+    cross_ref[comps:, :total] = inv_ref[crossing * comps : (crossing + 1) * comps, :]
+    cross_ref[comps:, total:] = jnp.zeros((comps, cross_ref.shape[-1] - total), F32)
+    collect(0, rows, comps, inv_ref, [], work_refs, spans_of(total, storing(sum_ref)))
 
 
 def middle_kernel(at, rows, length, tpl_ref, ext_ref, inv_ref, acc_ref, sum_ref, *work_refs):
     correlate(at, rows, length, tpl_ref, ext_ref, inv_ref, [acc_ref], work_refs, storing(sum_ref))
 
 
-def parting_kernel(at, rows, length, place_ref, tpl_ref, ext_ref, inv_ref, acc_ref, keep_ref, send_ref, *work_refs):
+def parting_kernel(at, rows, length, tpl_ref, ext_ref, inv_ref, acc_ref, keep_ref, early_ref, late_ref, *work_refs):
     own = rows // 2
-    low = place_ref[2] == 0
-
-    def store(start, stop, chunk):
+    low = lax.axis_index("sta") % 2 == 0
+    middle = early_ref.shape[-1]
+
+    def store(start, chunk):
+        stop = start + chunk.shape[1]
         keep_ref[:, start:stop] = jnp.where(low, chunk[:own], chunk[own:])
-        send_ref[:, start:stop] = jnp.where(low, chunk[own:], chunk[:own]).astype(BF16)
+        send = jnp.where(low, chunk[own:], chunk[:own]).astype(BF16)
+        if start < middle:
+            early_ref[:, start : min(stop, middle)] = send[:, : min(stop, middle) - start]
+        if stop > middle:
+            late_ref[:, max(start, middle) - middle : stop - middle] = send[:, max(start, middle) - start :]
 
     correlate(at, rows, length, tpl_ref, ext_ref, inv_ref, [acc_ref], work_refs, store)
+
+
+def closing_kernel(shards, rows, length, tpl_ref, cross_ref, acc_ref, early_ref, late_ref, *refs):
+    out_refs, (sum_ref, *work_refs) = refs[:shards], refs[shards:]
+    comps, middle = tpl_ref.shape[0], early_ref.shape[-1]
+    sum_ref[:, :middle] = acc_ref[:, :middle] + early_ref[...].astype(F32)
+    sum_ref[:, middle:] = acc_ref[:, middle:] + late_ref[...].astype(F32)
+    multiply(0, rows, length, tpl_ref, cross_ref, work_refs)
+    samples = out_refs[0].shape[-1]
+    tm_index = lax.axis_index("tm")
+
+    def storing_in(ref):
+        def store(chunk):
+            chunk = chunk.astype(ref.dtype)
+            if ref.shape[0] > rows:
+                more = jnp.zeros((ref.shape[0] - rows, samples), ref.dtype)
+                chunk = jnp.concatenate([chunk, more], axis=0)
+            ref[...] = chunk
+
+        return store
+
+    spans = [
+        (pl.multiple_of((tm_index ^ offset) * samples, LANES), samples, storing_in(ref))
+        for offset, ref in enumerate(out_refs)
+    ]
+    collect(comps, rows, comps, cross_ref, [sum_ref], work_refs, spans)
 
 
 def work_buffers(comps, rows, total, width, length):
@@ -262,93 +306,65 @@
     return [pltpu.VMEM((comps, LANES, width), BF16), pltpu.VMEM((comps, splits * rows, reach), F32)]
 
 
-def first(place, rows, length, halo, tpl, shards, tails):
+def first(rows, length, halo, crossing, tpl, shards, tails):
     chips, comps, samples = shards[0].shape
     total = samples * len(shards)
     width = total + up(length, LANES)
     count = chips * comps
     return pl.pallas_call(
-        functools.partial(first_kernel, len(shards), chips, rows, length, halo),
+        functools.partial(first_kernel, len(shards), chips, rows, length, halo, crossing),
         out_shape=[
             jax.ShapeDtypeStruct((count, width), F32),
             jax.ShapeDtypeStruct((count, total), F32),
+            jax.ShapeDtypeStruct((2 * comps, width), F32),
             jax.ShapeDtypeStruct((rows, total), F32),
         ],
-        in_specs=[SMEM] + [VMEM] * (1 + len(shards) + chips),
-        out_specs=[VMEM] * 3,
+        in_specs=[VMEM] * (1 + len(shards) + chips),
+        out_specs=[VMEM] * 4,
         scratch_shapes=[pltpu.VMEM((up(2 * count, 8), width), F32)]
         + work_buffers(comps, rows, total, width, length),
         compiler_params=params(24),
         cost_estimate=CHEAP,
-    )(place, tpl, *shards, *tails)
-
-
-def later(kernel, place, rows, total, length, out_shape, inputs, scratch=(), flops=1):
+    )(tpl, *shards, *tails)
+
+
+def later(kernel, rows, total, length, out_shape, inputs, scratch=(), flops=1):
     comps, width = inputs[0].shape[0], inputs[1].shape[-1]
-    given = ([] if place is None else [place]) + list(inputs)
-    specs = [VMEM] * len(inputs) if place is None else [SMEM] + [VMEM] * len(inputs)
     return pl.pallas_call(
         kernel,
         out_shape=out_shape,
-        in_specs=specs,
+        in_specs=[VMEM] * len(inputs),
         out_specs=[VMEM] * len(out_shape),
         scratch_shapes=list(scratch) + work_buffers(comps, rows, total, width, length),
         compiler_params=params(24),
         cost_estimate=pl.CostEstimate(flops=flops, bytes_accessed=1, transcendentals=0),
-    )(*given)
-
-
-def shard_kernel(place_ref, keep_ref, came_ref, own_ref, *send_refs):
-    samples = own_ref.shape[-1]
-    for offset, ref in enumerate((own_ref,) + send_refs):
-        at = pl.multiple_of((place_ref[1] ^ offset) * samples, LANES)
-        total = keep_ref[:, pl.ds(at, samples)] + came_ref[:, pl.ds(at, samples)].astype(F32)
-        total = total.astype(ref.dtype)
-        if ref.shape[0] > total.shape[0]:
-            total = jnp.concatenate([total, jnp.zeros((ref.shape[0] - total.shape[0], samples), ref.dtype)], axis=0)
-        ref[...] = total
-
-
-def shard(place, keep, came, count):
-    own, total = keep.shape
-    samples = total // count
-    return pl.pallas_call(
-        shard_kernel,
-        out_shape=[jax.ShapeDtypeStruct((own, samples), F32)]
-        + [
-            jax.ShapeDtypeStruct((own + (EXTRA if offset & (offset - 1) else 0), samples), BF16)
-            for offset in range(1, count)
-        ],
-        in_specs=[SMEM, VMEM, VMEM],
-        out_specs=[VMEM] * count,
-        compiler_params=params(16),
-        cost_estimate=CHEAP,
-    )(place, keep, came)
-
-
-def gather_kernel(place_ref, *refs):
+    )(*inputs)
+
+
+def gather_kernel(*refs):
     *part_refs, out_ref, held_ref, left = refs
+    tm_index = lax.axis_index("tm")
     copies = []
     for offset, ref in enumerate(part_refs):
         held_ref[offset] = ref[: out_ref.shape[1], :].astype(F32)
         copies.append(
-            pltpu.make_async_copy(held_ref.at[offset], out_ref.at[place_ref[1] ^ offset], left.at[offset])
+            pltpu.make_async_copy(held_ref.at[offset], out_ref.at[tm_index ^ offset], left.at[offset])
         )
         copies[-1].start()
     for copy in copies:
         copy.wait()
 
 
-def gather(place, parts):
+def gather(parts):
     shape = (len(parts),) + parts[0].shape
     return pl.pallas_call(
         gather_kernel,
         out_shape=jax.ShapeDtypeStruct(shape, F32),
-        in_specs=[SMEM] + [VMEM] * len(parts),
+        in_specs=[VMEM] * len(parts),
         out_specs=HBM,
         scratch_shapes=[pltpu.VMEM(shape, F32), pltpu.SemaphoreType.DMA((len(parts),))],
         compiler_params=params(16),
-    )(place, *parts)
+    )(*parts)
 
 
 def per_device(templates, channel_mask, waveforms, waveform_tail):
@@ -357,9 +373,6 @@
     halo = waveform_tail.shape[-1]
     tm_count = lax.axis_size("tm")
     chips = lax.axis_size("sta") // 2
-    tm_index, sta_index = lax.axis_index("tm"), lax.axis_index("sta")
-    chip_index, core_index = sta_index // 2, sta_index % 2
-    place = jnp.stack([chip_index, tm_index, core_index]).astype(jnp.int32)
     tpl = jnp.transpose(templates[0, :, 0], (1, 2, 0))
     mask = channel_mask[..., 0]
     rows = tpl.shape[-1] // chips
@@ -371,29 +384,42 @@
 
     wave = join(waveforms[0], waveform_tail[0])
     waves = [wave] + [swap_with(wave, "sta", 2 * offset) for offset in range(1, chips)]
-    offsets = [0] + between + [final, final]
-    parts = [(0, comps)] * (len(offsets) - 2) + [(0, comps - 1), (comps - 1, comps)]
-    starts = jnp.stack([(chip_index ^ offset) * rows for offset in offsets]).astype(jnp.int32)
-    messages = pack(starts, parts, rows, tpl, mask)
+    offsets = [0] + between
+    targets = [(offset, None) for offset in offsets] + [(final, 0), (final, 1)]
+    messages = pack(targets, [rows] * len(offsets) + [own] * 2, tpl, mask)
     messages, waves = lax.optimization_barrier((messages, waves))
     pieces = {offset: swap_with(messages[1 + i], "sta", 2 * offset) for i, offset in enumerate(between)}
     stacked = jnp.stack([part[:, :samples] for part in waves])
     shards = [stacked] + [swap_with(stacked, "tm", offset) for offset in range(1, tm_count)]
-    late, shards = lax.optimization_barrier((messages[-2:], shards))
-    late = [swap_with(part, "sta", 2 * final) for part in late]
-    ext, inv, acc = first(place, rows, length, halo, messages[0], shards, waves)
+    late = [None, None]
+    late[0], shards[-1] = lax.optimization_barrier((messages[-2], shards[-1]))
+    late[1], shards[-2] = lax.optimization_barrier((messages[-1], shards[-2]))
+    straight = swap_with(late[0], "sta", 2 * final)
+    crossed = swap_with(late[1], "sta", 2 * final + 1)
+    ext, inv, cross, acc = first(rows, length, halo, final, messages[0], shards, waves)
+    cross = swap_with(cross, "sta", 1)
     whole = jax.ShapeDtypeStruct((rows, total), F32)
-    stations = [(offset * comps, pieces[offset]) for offset in between] + [(final * comps, late[0])]
-    for step, (at, piece) in enumerate(stations):
-        kernel = functools.partial(middle_kernel, at, rows, length)
-        flops = COSTS[min(step, len(COSTS) - 1)]
-        (acc,) = later(kernel, None, rows, total, length, [whole], [piece, ext, inv, acc], flops=flops)
-    kernel = functools.partial(parting_kernel, final * comps + comps - 1, rows, length)
-    halves = [jax.ShapeDtypeStruct((own, total), F32), jax.ShapeDtypeStruct((own, total), BF16)]
-    keep, send = later(kernel, place, rows, total, length, halves, [late[1], ext, inv, acc])
-    parts = shard(place, keep, swap_with(send, "sta", 1), tm_count)
+    for offset in between[:-1]:
+        kernel = functools.partial(middle_kernel, offset * comps, rows, length)
+        (acc,) = later(kernel, rows, total, length, [whole], [pieces[offset], ext, inv, acc], flops=F_MID)
+    middle = up(total // 2, LANES)
+    half = jax.ShapeDtypeStruct((own, total), F32)
+    halves = [jax.ShapeDtypeStruct((own, size), BF16) for size in (middle, total - middle)]
+    kernel = functools.partial(parting_kernel, between[-1] * comps, rows, length)
+    inputs = [pieces[between[-1]], ext, inv, acc]
+    keep, *send = later(kernel, rows, total, length, [half] + halves, inputs, flops=F_PART)
+    came = [swap_with(part, "sta", 1) for part in send]
+    kernel = functools.partial(middle_kernel, final * comps, own, length)
+    (acc,) = later(kernel, own, total, length, [half], [straight, ext, inv, keep], flops=F_JOIN)
+    kernel = functools.partial(closing_kernel, tm_count, own, length)
+    parts = [jax.ShapeDtypeStruct((own, samples), F32)] + [
+        jax.ShapeDtypeStruct((own + (EXTRA if offset & (offset - 1) else 0), samples), BF16)
+        for offset in range(1, tm_count)
+    ]
+    inputs = [crossed, cross, acc, *came]
+    parts = later(kernel, own, total, length, parts, inputs, [pltpu.VMEM((own, total), F32)], F_CLOSE)
     parts = [parts[0]] + [swap_with(parts[offset], "tm", offset) for offset in range(1, tm_count)]
-    return gather(place, parts)
+    return gather(parts)
 
 
 def solution(mesh):

time: 45.2 us -> 42.8 us (0.947)
  Pallas kernels: 15.8 us -> 14.5 us
  starting transfers between devices: 18.4 us -> 17.9 us
    ppermute x14 -> x16, starting transfers between devices: 18.4 us -> 17.9 us  [swap_with(): return lax.ppermute(x, axis, [(i, i ^ offset) for i in range(size)])]
    pallas_call x1, Pallas kernels: 1.34 us -> 0.8 us  [gather(): pl.pallas_call(gather_kernel, out_shape=jax.ShapeDtypeStruct(shape, F32),...]
    pallas_call x1, Pallas kernels: 3.41 us -> 2.92 us  [first(): pl.pallas_call(functools.partial(first_kernel, len(shards), chips, rows,...]
    ppermute x14 -> x16, waiting for transfers between devices: 10.3 us -> 9.88 us  [swap_with(): return lax.ppermute(x, axis, [(i, i ^ offset) for i in range(size)])]
    pallas_call x6 -> x5, Pallas kernels: 10.3 us -> 10.1 us  [the longest x4 8.22 us: later(): pl.pallas_call(kernel, out_shape=out_shape, in_specs=[VMEM] * len(inputs)...]
  transfers between devices with their start and end apart: 14 -> 16, of which waited for: 8 -> 7; matrix products, arithmetic and copies ran while one was open for 0% -> 0% of each run, Pallas kernels for 25% -> 25%
where the time goes in v4:
time: 42.8 us; the launch traced here: 42.5 us
  starting transfers between devices  17.9 us (42%)
  Pallas kernels  14.5 us (34%)
  waiting for transfers between devices  9.88 us (23%)
    ppermute x16, starting transfers between devices, swap_with(): return lax.ppermute(x, axis, [(i, i ^ offset) for i in range(size)])  17.9 us
    ppermute x16, waiting for transfers between devices, swap_with(): return lax.ppermute(x, axis, [(i, i ^ offset) for i in range(size)])  9.88 us
    pallas_call x4, Pallas kernels, later(): pl.pallas_call(kernel, out_shape=out_shape, in_specs=[VMEM] * len(inputs)...  8.22 us
    pallas_call x1, Pallas kernels, first(): pl.pallas_call(functools.partial(first_kernel, len(shards), chips, rows,...  2.92 us
    pallas_call x1, Pallas kernels, pack(): pl.pallas_call(functools.partial(pack_kernel, targets, counts, length), o...  1.86 us
  transfers between devices with their start and end apart: 16, of which 7 were waited for; matrix products, arithmetic and copies ran while one was open for 0% of the time, Pallas kernels for 25%

profile of v4, /device:TPU:0, one launch (start us, length us, event | category | flops | bytes accessed | tf_op | source)
XLA Modules:
  0.0 42.5 jit_solution(5869191438925368664)
XLA Ops:
  0.0 0.7 %shard_map.47.refs_4_ = bf16[3,1536]{1,0:T(4,128)(2,1)S(1)} custom-call(bf16[3,896]{1,0:T(4,128)(2,1)} %bitcast.15, bf16[3,599]{1,0:T(4,128)(2,1)} %bitcast.16), custom_call_target="tpu_custom_call" | custom-call | flops 1 | bytes 1 | tf_op jit(solution)/shard_map/pallas_call | solution.py:49
  0.7 5.1 %collective-permute-start.2 = (bf16[3,1536]{1,0:T(4,128)(2,1)S(1)}, bf16[3,1536]{1,0:T(4,128)(2,1)S(1)}, u32[]{:S(2)}, u32[]{:S(2)}) collective-permute-start(bf16[3,1536]{1,0:T(4,128)(2,1)S(1)} %shard_map.47.refs_4_), channel_id=1, source_target_pairs={{0,6},{1,7},{2,4},{3,5},{4,2},{5,3},{6,0},{7,1},{8,14},{9,15},{10,... | collective-permute-start | bytes 27656 | tf_op jit(solution)/shard_map/ppermute | solution.py:30
  5.9 0.0 collective-permute-start.1
  5.9 0.6 %collective-permute-start = (bf16[3,1536]{1,0:T(4,128)(2,1)S(1)}, bf16[3,1536]{1,0:T(4,128)(2,1)S(1)}, u32[]{:S(2)}, u32[]{:S(2)}) collective-permute-start(bf16[3,1536]{1,0:T(4,128)(2,1)S(1)} %shard_map.47.refs_4_), channel_id=1, source_target_pairs={{0,2},{1,3},{2,0},{3,1},{4,6},{5,7},{6,4},{7,5},{8,10},{9,11},{10,... | collective-permute-start | bytes 27656 | tf_op jit(solution)/shard_map/ppermute | solution.py:30
  6.5 1.9 %shard_map.46 = (bf16[3,304,128]{2,1,0:T(8,128)(2,1)S(1)}, bf16[3,304,128]{2,1,0:T(8,128)(2,1)S(1)}, bf16[3,304,128]{2,1,0:T(8,128)(2,1)S(1)}, bf16[3,152,128]{2,1,0:T(8,128)(2,1)S(1)}, bf16[3,152,128]{2,1,0:T(8,128)(2,1)S(1)}) custom-call(bf16[3,600,256]{2,1,0:T(8,128)(2,1)} %bitcast.14, s32[1,256]{1,0:T(1,128)} %bitcast.17), custom_call_target="tpu_custom_call" | custom-call | flops 1 | bytes 1 | tf_op jit(solution)/shard_map/pallas_call | solution.py:103
  8.4 0.0 collective-permute-done.2.refs_7_
  8.4 2.1 %collective-permute-done.1.refs_6_ = bf16[3,1536]{1,0:T(4,128)(2,1)S(1)} collective-permute-done((bf16[3,1536]{1,0:T(4,128)(2,1)S(1)}, bf16[3,1536]{1,0:T(4,128)(2,1)S(1)}, u32[]{:S(2)}, u32[]{:S(2)}) %collective-permute-start.1) | collective-permute-done | bytes 9248 | tf_op jit(solution)/shard_map/ppermute | solution.py:30
  10.5 0.0 collective-permute-done.refs_5_
  10.5 1.8 %collective-permute-start.9 = (bf16[3,304,128]{2,1,0:T(8,128)(2,1)S(1)}, bf16[3,304,128]{2,1,0:T(8,128)(2,1)S(1)}, u32[]{:S(2)}, u32[]{:S(2)}) collective-permute-start(bf16[3,304,128]{2,1,0:T(8,128)(2,1)S(1)} %get-tuple-element.53), channel_id=1, source_target_pairs={{0,6},{1,7},{2,4},{3,5},{4,2},{5,3},{6,0},{7,1},{8,14},{9,15},{10,... | collective-permute-start | bytes 700424 | tf_op jit(solution)/shard_map/ppermute | solution.py:30
  12.2 0.8 %collective-permute-start.10 = (bf16[3,304,128]{2,1,0:T(8,128)(2,1)S(1)}, bf16[3,304,128]{2,1,0:T(8,128)(2,1)S(1)}, u32[]{:S(2)}, u32[]{:S(2)}) collective-permute-start(bf16[3,304,128]{2,1,0:T(8,128)(2,1)S(1)} %get-tuple-element.54), channel_id=1, source_target_pairs={{0,2},{1,3},{2,0},{3,1},{4,6},{5,7},{6,4},{7,5},{8,10},{9,11},{10,... | collective-permute-start | bytes 700424 | tf_op jit(solution)/shard_map/ppermute | solution.py:30
  13.1 2.5 %collective-permute-start.6 = (bf16[4,3,896]{2,1,0:T(4,128)(2,1)S(1)}, bf16[4,3,896]{2,1,0:T(4,128)(2,1)S(1)}, u32[]{:S(2)}, u32[]{:S(2)}) collective-permute-start(bf16[4,3,896]{2,1,0:T(4,128)(2,1)S(1)} %pad_maximum_fusion.refs_0_), channel_id=1, source_target_pairs={{0,24},{8,16},{16,8},{24,0},{1,25},{9,17},{17,9},{25,1},{2,26},{10... | collective-permute-start | bytes 64520 | tf_op jit(solution)/shard_map/ppermute | solution.py:30
  15.6 0.5 %collective-permute-start.3 = (bf16[4,3,896]{2,1,0:T(4,128)(2,1)S(1)}, bf16[4,3,896]{2,1,0:T(4,128)(2,1)S(1)}, u32[]{:S(2)}, u32[]{:S(2)}) collective-permute-start(bf16[4,3,896]{2,1,0:T(4,128)(2,1)S(1)} %pad_maximum_fusion.refs_0_), channel_id=1, source_target_pairs={{0,16},{8,24},{16,0},{24,8},{1,17},{9,25},{17,1},{25,9},{2,18},{10... | collective-permute-start | bytes 64520 | tf_op jit(solution)/shard_map/ppermute | solution.py:30
  16.1 0.5 %collective-permute-start.5 = (bf16[4,3,896]{2,1,0:T(4,128)(2,1)S(1)}, bf16[4,3,896]{2,1,0:T(4,128)(2,1)S(1)}, u32[]{:S(2)}, u32[]{:S(2)}) collective-permute-start(bf16[4,3,896]{2,1,0:T(4,128)(2,1)S(1)} %pad_maximum_fusion.refs_0_), channel_id=1, source_target_pairs={{0,8},{8,0},{16,24},{24,16},{1,9},{9,1},{17,25},{25,17},{2,10},{10... | collective-permute-start | bytes 64520 | tf_op jit(solution)/shard_map/ppermute | solution.py:30
  16.7 1.3 %collective-permute-done.6.refs_3_ = bf16[4,3,896]{2,1,0:T(4,128)(2,1)S(1)} collective-permute-done((bf16[4,3,896]{2,1,0:T(4,128)(2,1)S(1)}, bf16[4,3,896]{2,1,0:T(4,128)(2,1)S(1)}, u32[]{:S(2)}, u32[]{:S(2)}) %collective-permute-start.6) | collective-permute-done | bytes 21536 | tf_op jit(solution)/shard_map/ppermute | solution.py:30
  17.9 1.8 %collective-permute-start.8 = (bf16[3,152,128]{2,1,0:T(8,128)(2,1)S(1)}, bf16[3,152,128]{2,1,0:T(8,128)(2,1)S(1)}, u32[]{:S(2)}, u32[]{:S(2)}) collective-permute-start(bf16[3,152,128]{2,1,0:T(8,128)(2,1)S(1)} %get-tuple-element.50), channel_id=1, source_target_pairs={{0,4},{1,5},{2,6},{3,7},{4,0},{5,1},{6,2},{7,3},{8,12},{9,13},{10,... | collective-permute-start | bytes 350216 | tf_op jit(solution)/shard_map/ppermute | solution.py:30
  19.7 0.0 collective-permute-done.3.refs_2_
  19.7 0.0 collective-permute-start.4
  19.7 0.2 collective-permute-done.5.refs_1_
  20.0 2.9 %shard_map.48 = (f32[12,4224]{1,0:T(8,128)S(1)}, f32[12,3584]{1,0:T(8,128)S(1)}, f32[6,4224]{1,0:T(8,128)S(1)}, f32[64,3584]{1,0:T(8,128)S(1)}) custom-call(bf16[3,304,128]{2,1,0:T(8,128)(2,1)S(1)} %get-tuple-element.45.tpl_ref, bf16[4,3,896]{2,1,0:T(4,128)(2,1)S(1)} %pad_maximum_fusion.refs_0_, bf16[4,3,896]{2,1,0:T(4,128)(2,1)S(1)} %collective-permute-done.5.refs_1_, ...), custom_call_target="tpu_custom_call" | custom-call | flops 1 | bytes 1 | tf_op jit(solution)/shard_map/pallas_call | solution.py:314
  22.9 2.3 %collective-permute-done.10.tpl_ref = bf16[3,304,128]{2,1,0:T(8,128)(2,1)S(1)} collective-permute-done((bf16[3,304,128]{2,1,0:T(8,128)(2,1)S(1)}, bf16[3,304,128]{2,1,0:T(8,128)(2,1)S(1)}, u32[]{:S(2)}, u32[]{:S(2)}) %collective-permute-start.10) | collective-permute-done | bytes 233504 | tf_op jit(solution)/shard_map/ppermute | solution.py:30
  25.2 2.1 %shard_map.49.acc_ref = f32[64,3584]{1,0:T(8,128)S(1)} custom-call(bf16[3,304,128]{2,1,0:T(8,128)(2,1)S(1)} %collective-permute-done.10.tpl_ref, f32[12,4224]{1,0:T(8,128)S(1)} %get-tuple-element.51.ext_ref, f32[12,3584]{1,0:T(8,128)S(1)} %get-tuple-element.52.inv_ref, f32[64,3584]{1,0:T(8,128)S(1)} %get-tuple-element.55.acc_ref), custom_call_target="tpu_custom_call" | custom-call | flops 500000000 | bytes 1 | tf_op jit(solution)/shard_map/pallas_call | solution.py:333
  27.3 0.0 collective-permute-done.9.tpl_ref
  27.3 2.1 %shard_map.50 = (f32[32,3584]{1,0:T(8,128)S(1)}, bf16[32,1792]{1,0:T(8,128)(2,1)S(1)}, bf16[32,1792]{1,0:T(8,128)(2,1)S(1)}) custom-call(bf16[3,304,128]{2,1,0:T(8,128)(2,1)S(1)} %collective-permute-done.9.tpl_ref, f32[12,4224]{1,0:T(8,128)S(1)} %get-tuple-element.51.ext_ref, f32[12,3584]{1,0:T(8,128)S(1)} %get-tuple-element.52.inv_ref, ...), custom_call_target="tpu_custom_call" | custom-call | flops 1 | bytes 1 | tf_op jit(solution)/shard_map/pallas_call | solution.py:333
  29.4 0.1 collective-permute-start.11
  29.4 0.5 %collective-permute-start.12 = (bf16[32,1792]{1,0:T(8,128)(2,1)S(1)}, bf16[32,1792]{1,0:T(8,128)(2,1)S(1)}, u32[]{:S(2)}, u32[]{:S(2)}) collective-permute-start(bf16[32,1792]{1,0:T(8,128)(2,1)S(1)} %get-tuple-element.58), channel_id=1, source_target_pairs={{0,1},{1,0},{2,3},{3,2},{4,5},{5,4},{6,7},{7,6},{8,9},{9,8},{10,11... | collective-permute-start | bytes 344072 | tf_op jit(solution)/shard_map/ppermute | solution.py:30
  29.9 0.1 collective-permute-start.7
  30.0 0.3 collective-permute-done.8.tpl_ref
  30.3 1.9 %shard_map.51.acc_ref = f32[32,3584]{1,0:T(8,128)S(1)} custom-call(bf16[3,152,128]{2,1,0:T(8,128)(2,1)S(1)} %collective-permute-done.8.tpl_ref, f32[12,4224]{1,0:T(8,128)S(1)} %get-tuple-element.51.ext_ref, f32[12,3584]{1,0:T(8,128)S(1)} %get-tuple-element.52.inv_ref, f32[32,3584]{1,0:T(8,128)S(1)} %get-tuple-element.56.acc_ref), custom_call_target="tpu_custom_call" | custom-call | flops 500000000 | bytes 1 | tf_op jit(solution)/shard_map/pallas_call | solution.py:333
  32.2 0.0 collective-permute-done.7.cross_ref
  32.2 0.0 collective-permute-done.4.tpl_ref
  32.2 0.0 collective-permute-done.11.early_ref
  32.2 0.0 collective-permute-done.12.late_ref
  32.2 2.2 %shard_map.52 = (f32[32,896]{1,0:T(8,128)S(1)}, bf16[32,896]{1,0:T(8,128)(2,1)S(1)}, bf16[32,896]{1,0:T(8,128)(2,1)S(1)}, bf16[40,896]{1,0:T(8,128)(2,1)S(1)}) custom-call(bf16[3,152,128]{2,1,0:T(8,128)(2,1)S(1)} %collective-permute-done.4.tpl_ref, f32[6,4224]{1,0:T(8,128)S(1)} %collective-permute-done.7.cross_ref, f32[32,3584]{1,0:T(8,128)S(1)} %shard_map.51.acc_ref, ...), custom_call_target="tpu_custom_call" | custom-call | flops 1 | bytes 1 | tf_op jit(solution)/shard_map/pallas_call | solution.py:333
  34.5 2.5 %collective-permute-start.15 = (bf16[40,896]{1,0:T(8,128)(2,1)S(1)}, bf16[40,896]{1,0:T(8,128)(2,1)S(1)}, u32[]{:S(2)}, u32[]{:S(2)}) collective-permute-start(bf16[40,896]{1,0:T(8,128)(2,1)S(1)} %get-tuple-element.62), channel_id=1, source_target_pairs={{0,24},{8,16},{16,8},{24,0},{1,25},{9,17},{17,9},{25,1},{2,26},{10... | collective-permute-start | bytes 215048 | tf_op jit(solution)/shard_map/ppermute | solution.py:30
  37.0 0.5 %collective-permute-start.13 = (bf16[32,896]{1,0:T(8,128)(2,1)S(1)}, bf16[32,896]{1,0:T(8,128)(2,1)S(1)}, u32[]{:S(2)}, u32[]{:S(2)}) collective-permute-start(bf16[32,896]{1,0:T(8,128)(2,1)S(1)} %get-tuple-element.60), channel_id=1, source_target_pairs={{0,8},{8,0},{16,24},{24,16},{1,9},{9,1},{17,25},{25,17},{2,10},{10... | collective-permute-start | bytes 172040 | tf_op jit(solution)/shard_map/ppermute | solution.py:30
  37.5 0.5 %collective-permute-start.14 = (bf16[32,896]{1,0:T(8,128)(2,1)S(1)}, bf16[32,896]{1,0:T(8,128)(2,1)S(1)}, u32[]{:S(2)}, u32[]{:S(2)}) collective-permute-start(bf16[32,896]{1,0:T(8,128)(2,1)S(1)} %get-tuple-element.61), channel_id=1, source_target_pairs={{0,16},{8,24},{16,0},{24,8},{1,17},{9,25},{17,1},{25,9},{2,18},{10... | collective-permute-start | bytes 172040 | tf_op jit(solution)/shard_map/ppermute | solution.py:30
  38.0 3.1 %collective-permute-done.13.refs_1_ = bf16[32,896]{1,0:T(8,128)(2,1)S(1)} collective-permute-done((bf16[32,896]{1,0:T(8,128)(2,1)S(1)}, bf16[32,896]{1,0:T(8,128)(2,1)S(1)}, u32[]{:S(2)}, u32[]{:S(2)}) %collective-permute-start.13) | collective-permute-done | bytes 57376 | tf_op jit(solution)/shard_map/ppermute | solution.py:30
  41.2 0.5 %collective-permute-done.14.refs_2_ = bf16[32,896]{1,0:T(8,128)(2,1)S(1)} collective-permute-done((bf16[32,896]{1,0:T(8,128)(2,1)S(1)}, bf16[32,896]{1,0:T(8,128)(2,1)S(1)}, u32[]{:S(2)}, u32[]{:S(2)}) %collective-permute-start.14) | collective-permute-done | bytes 57376 | tf_op jit(solution)/shard_map/ppermute | solution.py:30
  41.7 0.0 collective-permute-done.15.refs_3_
  41.7 0.8 %shard_map.53 = f32[4,32,896]{2,1,0:T(8,128)} custom-call(f32[32,896]{1,0:T(8,128)S(1)} %get-tuple-element.59.refs_0_, bf16[32,896]{1,0:T(8,128)(2,1)S(1)} %collective-permute-done.13.refs_1_, bf16[32,896]{1,0:T(8,128)(2,1)S(1)} %collective-permute-done.14.refs_2_, bf16[40,896]{1,0:T(8,128)(2,1)S(1)} %collective-permute-done.15.refs_3_), custom_call_target="tpu_custom_call" | custom-call | tf_op jit(solution)/shard_map/pallas_call | solution.py:360
  (3 shorter events, 0.0 us)
Async XLA Ops:
  0.7 7.6 %collective-permute-start.2 = (bf16[3,1536]{1,0:T(4,128)(2,1)S(1)}, bf16[3,1536]{1,0:T(4,128)(2,1)S(1)}, u32[]{:S(2)}, u32[]{:S(2)}) collective-permute-start(bf16[3,1536]{1,0:T(4,128)(2,1)S(1)} %shard_map.47.refs_4_), channel_id=1, source_target_pairs={{0,6},{1,7},{2,4},{3,5},{4,2},{5,3},{6,0},{7,1},{8,14},{9,15},{10,... | collective-permute-start | bytes 27656 | tf_op jit(solution)/shard_map/ppermute | solution.py:30
  5.9 4.6 %collective-permute-start.1 = (bf16[3,1536]{1,0:T(4,128)(2,1)S(1)}, bf16[3,1536]{1,0:T(4,128)(2,1)S(1)}, u32[]{:S(2)}, u32[]{:S(2)}) collective-permute-start(bf16[3,1536]{1,0:T(4,128)(2,1)S(1)} %shard_map.47.refs_4_), channel_id=1, source_target_pairs={{0,4},{1,5},{2,6},{3,7},{4,0},{5,1},{6,2},{7,3},{8,12},{9,13},{10,... | collective-permute-start | bytes 27656 | tf_op jit(solution)/shard_map/ppermute | solution.py:30
  5.9 4.6 %collective-permute-start = (bf16[3,1536]{1,0:T(4,128)(2,1)S(1)}, bf16[3,1536]{1,0:T(4,128)(2,1)S(1)}, u32[]{:S(2)}, u32[]{:S(2)}) collective-permute-start(bf16[3,1536]{1,0:T(4,128)(2,1)S(1)} %shard_map.47.refs_4_), channel_id=1, source_target_pairs={{0,2},{1,3},{2,0},{3,1},{4,6},{5,7},{6,4},{7,5},{8,10},{9,11},{10,... | collective-permute-start | bytes 27656 | tf_op jit(solution)/shard_map/ppermute | solution.py:30
  10.5 16.8 %collective-permute-start.9 = (bf16[3,304,128]{2,1,0:T(8,128)(2,1)S(1)}, bf16[3,304,128]{2,1,0:T(8,128)(2,1)S(1)}, u32[]{:S(2)}, u32[]{:S(2)}) collective-permute-start(bf16[3,304,128]{2,1,0:T(8,128)(2,1)S(1)} %get-tuple-element.53), channel_id=1, source_target_pairs={{0,6},{1,7},{2,4},{3,5},{4,2},{5,3},{6,0},{7,1},{8,14},{9,15},{10,... | collective-permute-start | bytes 700424 | tf_op jit(solution)/shard_map/ppermute | solution.py:30
  12.2 13.0 %collective-permute-start.10 = (bf16[3,304,128]{2,1,0:T(8,128)(2,1)S(1)}, bf16[3,304,128]{2,1,0:T(8,128)(2,1)S(1)}, u32[]{:S(2)}, u32[]{:S(2)}) collective-permute-start(bf16[3,304,128]{2,1,0:T(8,128)(2,1)S(1)} %get-tuple-element.54), channel_id=1, source_target_pairs={{0,2},{1,3},{2,0},{3,1},{4,6},{5,7},{6,4},{7,5},{8,10},{9,11},{10,... | collective-permute-start | bytes 700424 | tf_op jit(solution)/shard_map/ppermute | solution.py:30
  13.1 4.8 %collective-permute-start.6 = (bf16[4,3,896]{2,1,0:T(4,128)(2,1)S(1)}, bf16[4,3,896]{2,1,0:T(4,128)(2,1)S(1)}, u32[]{:S(2)}, u32[]{:S(2)}) collective-permute-start(bf16[4,3,896]{2,1,0:T(4,128)(2,1)S(1)} %pad_maximum_fusion.refs_0_), channel_id=1, source_target_pairs={{0,24},{8,16},{16,8},{24,0},{1,25},{9,17},{17,9},{25,1},{2,26},{10... | collective-permute-start | bytes 64520 | tf_op jit(solution)/shard_map/ppermute | solution.py:30
  15.6 4.1 %collective-permute-start.3 = (bf16[4,3,896]{2,1,0:T(4,128)(2,1)S(1)}, bf16[4,3,896]{2,1,0:T(4,128)(2,1)S(1)}, u32[]{:S(2)}, u32[]{:S(2)}) collective-permute-start(bf16[4,3,896]{2,1,0:T(4,128)(2,1)S(1)} %pad_maximum_fusion.refs_0_), channel_id=1, source_target_pairs={{0,16},{8,24},{16,0},{24,8},{1,17},{9,25},{17,1},{25,9},{2,18},{10... | collective-permute-start | bytes 64520 | tf_op jit(solution)/shard_map/ppermute | solution.py:30
  16.1 3.9 %collective-permute-start.5 = (bf16[4,3,896]{2,1,0:T(4,128)(2,1)S(1)}, bf16[4,3,896]{2,1,0:T(4,128)(2,1)S(1)}, u32[]{:S(2)}, u32[]{:S(2)}) collective-permute-start(bf16[4,3,896]{2,1,0:T(4,128)(2,1)S(1)} %pad_maximum_fusion.refs_0_), channel_id=1, source_target_pairs={{0,8},{8,0},{16,24},{24,16},{1,9},{9,1},{17,25},{25,17},{2,10},{10... | collective-permute-start | bytes 64520 | tf_op jit(solution)/shard_map/ppermute | solution.py:30
  17.9 12.4 %collective-permute-start.8 = (bf16[3,152,128]{2,1,0:T(8,128)(2,1)S(1)}, bf16[3,152,128]{2,1,0:T(8,128)(2,1)S(1)}, u32[]{:S(2)}, u32[]{:S(2)}) collective-permute-start(bf16[3,152,128]{2,1,0:T(8,128)(2,1)S(1)} %get-tuple-element.50), channel_id=1, source_target_pairs={{0,4},{1,5},{2,6},{3,7},{4,0},{5,1},{6,2},{7,3},{8,12},{9,13},{10,... | collective-permute-start | bytes 350216 | tf_op jit(solution)/shard_map/ppermute | solution.py:30
  19.7 12.5 %collective-permute-start.4 = (bf16[3,152,128]{2,1,0:T(8,128)(2,1)S(1)}, bf16[3,152,128]{2,1,0:T(8,128)(2,1)S(1)}, u32[]{:S(2)}, u32[]{:S(2)}) collective-permute-start(bf16[3,152,128]{2,1,0:T(8,128)(2,1)S(1)} %get-tuple-element.44), channel_id=1, source_target_pairs={{0,5},{1,4},{2,7},{3,6},{4,1},{5,0},{6,3},{7,2},{8,13},{9,12},{10,... | collective-permute-start | bytes 350216 | tf_op jit(solution)/shard_map/ppermute | solution.py:30
  29.4 2.9 %collective-permute-start.11 = (bf16[32,1792]{1,0:T(8,128)(2,1)S(1)}, bf16[32,1792]{1,0:T(8,128)(2,1)S(1)}, u32[]{:S(2)}, u32[]{:S(2)}) collective-permute-start(bf16[32,1792]{1,0:T(8,128)(2,1)S(1)} %get-tuple-element.57), channel_id=1, source_target_pairs={{0,1},{1,0},{2,3},{3,2},{4,5},{5,4},{6,7},{7,6},{8,9},{9,8},{10,11... | collective-permute-start | bytes 344072 | tf_op jit(solution)/shard_map/ppermute | solution.py:30
  29.4 2.8 %collective-permute-start.12 = (bf16[32,1792]{1,0:T(8,128)(2,1)S(1)}, bf16[32,1792]{1,0:T(8,128)(2,1)S(1)}, u32[]{:S(2)}, u32[]{:S(2)}) collective-permute-start(bf16[32,1792]{1,0:T(8,128)(2,1)S(1)} %get-tuple-element.58), channel_id=1, source_target_pairs={{0,1},{1,0},{2,3},{3,2},{4,5},{5,4},{6,7},{7,6},{8,9},{9,8},{10,11... | collective-permute-start | bytes 344072 | tf_op jit(solution)/shard_map/ppermute | solution.py:30
  29.9 2.3 %collective-permute-start.7 = (f32[6,4224]{1,0:T(8,128)S(1)}, f32[6,4224]{1,0:T(8,128)S(1)}, u32[]{:S(2)}, u32[]{:S(2)}) collective-permute-start(f32[6,4224]{1,0:T(8,128)S(1)} %get-tuple-element.49), channel_id=1, source_target_pairs={{0,1},{1,0},{2,3},{3,2},{4,5},{5,4},{6,7},{7,6},{8,9},{9,8},{10,11... | collective-permute-start | bytes 304136 | tf_op jit(solution)/shard_map/ppermute | solution.py:30
  34.5 7.2 %collective-permute-start.15 = (bf16[40,896]{1,0:T(8,128)(2,1)S(1)}, bf16[40,896]{1,0:T(8,128)(2,1)S(1)}, u32[]{:S(2)}, u32[]{:S(2)}) collective-permute-start(bf16[40,896]{1,0:T(8,128)(2,1)S(1)} %get-tuple-element.62), channel_id=1, source_target_pairs={{0,24},{8,16},{16,8},{24,0},{1,25},{9,17},{17,9},{25,1},{2,26},{10... | collective-permute-start | bytes 215048 | tf_op jit(solution)/shard_map/ppermute | solution.py:30
  37.0 4.2 %collective-permute-start.13 = (bf16[32,896]{1,0:T(8,128)(2,1)S(1)}, bf16[32,896]{1,0:T(8,128)(2,1)S(1)}, u32[]{:S(2)}, u32[]{:S(2)}) collective-permute-start(bf16[32,896]{1,0:T(8,128)(2,1)S(1)} %get-tuple-element.60), channel_id=1, source_target_pairs={{0,8},{8,0},{16,24},{24,16},{1,9},{9,1},{17,25},{25,17},{2,10},{10... | collective-permute-start | bytes 172040 | tf_op jit(solution)/shard_map/ppermute | solution.py:30
  37.5 4.2 %collective-permute-start.14 = (bf16[32,896]{1,0:T(8,128)(2,1)S(1)}, bf16[32,896]{1,0:T(8,128)(2,1)S(1)}, u32[]{:S(2)}, u32[]{:S(2)}) collective-permute-start(bf16[32,896]{1,0:T(8,128)(2,1)S(1)} %get-tuple-element.61), channel_id=1, source_target_pairs={{0,16},{8,24},{16,0},{24,8},{1,17},{9,25},{17,1},{25,9},{2,18},{10... | collective-permute-start | bytes 172040 | tf_op jit(solution)/shard_map/ppermute | solution.py:30

commit v5 on v4

--- a/solution.py
+++ b/solution.py
@@ -10,7 +10,7 @@
 BF16 = jnp.bfloat16
 LANES = 128
 CHUNK = 512
-EXTRA = 8
+EXTRA = 128
 VMEM = pl.BlockSpec(memory_space=pltpu.VMEM)
 HBM = pl.BlockSpec(memory_space=pltpu.HBM)
 F_MID, F_PART, F_JOIN, F_CLOSE = 500000000, 1, 500000000, 1
@@ -30,31 +30,36 @@
     return lax.ppermute(x, axis, [(i, i ^ offset) for i in range(size)])
 
 
-def join_kernel(wave_ref, tail_ref, out_ref, wave_held, tail_held, arrived):
-    copies = [
-        pltpu.make_async_copy(wave_ref, wave_held, arrived.at[0]),
-        pltpu.make_async_copy(tail_ref, tail_held, arrived.at[1]),
-    ]
+def join_kernel(wave_ref, tail_ref, tpl_ref, mask_ref, out_ref, tpl_out, mask_out, wave_held, tail_held, arrived):
+    pairs = ((wave_ref, wave_held), (tail_ref, tail_held), (mask_ref, mask_out), (tpl_ref, tpl_out))
+    copies = [pltpu.make_async_copy(source, held, arrived.at[i]) for i, (source, held) in enumerate(pairs)]
     for copy in copies:
         copy.start()
-    for copy in copies:
-        copy.wait()
+    copies[0].wait()
+    copies[1].wait()
     samples = wave_held.shape[-1]
     out_ref[...] = jnp.zeros_like(out_ref)
     out_ref[:, :samples] = wave_held[...]
     out_ref[:, samples : samples + tail_held.shape[-1]] = tail_held[...]
-
-
-def join(wave, tail):
+    copies[2].wait()
+    copies[3].wait()
+
+
+def join(wave, tail, tpl, mask):
+    inputs = (wave, tail, tpl, mask)
     return pl.pallas_call(
         join_kernel,
-        out_shape=jax.ShapeDtypeStruct((wave.shape[0], up(wave.shape[-1] + tail.shape[-1], LANES)), BF16),
-        in_specs=[HBM] * 2,
-        out_specs=VMEM,
-        scratch_shapes=[pltpu.VMEM(x.shape, x.dtype) for x in (wave, tail)] + [pltpu.SemaphoreType.DMA((2,))],
+        out_shape=[
+            jax.ShapeDtypeStruct((wave.shape[0], up(wave.shape[-1] + tail.shape[-1], LANES)), BF16),
+            jax.ShapeDtypeStruct(tpl.shape, tpl.dtype),
+            jax.ShapeDtypeStruct(mask.shape, mask.dtype),
+        ],
+        in_specs=[HBM] * 4,
+        out_specs=[VMEM] * 3,
+        scratch_shapes=[pltpu.VMEM(x.shape, x.dtype) for x in (wave, tail)] + [pltpu.SemaphoreType.DMA((4,))],
         compiler_params=params(16),
         cost_estimate=CHEAP,
-    )(*[pltpu.with_memory_space_constraint(x, pltpu.HBM) for x in (wave, tail)])
+    )(*[pltpu.with_memory_space_constraint(x, pltpu.HBM) for x in inputs])
 
 
 def first_row(chip_offset, core_offset, all_rows):
@@ -68,23 +73,15 @@
     return up(-(-length // (LANES // rows)), 8)
 
 
-def pack_kernel(targets, counts, length, tpl_ref, mask_ref, *refs):
-    tpl_outs, (held_ref, mask_held, arrived) = refs[: len(counts)], refs[len(counts) :]
-    comps = tpl_ref.shape[0]
-    copies = [pltpu.make_async_copy(mask_ref, mask_held, arrived.at[comps])]
-    copies += [pltpu.make_async_copy(tpl_ref.at[c], held_ref.at[c], arrived.at[c]) for c in range(comps)]
-    for copy in copies:
-        copy.start()
-    copies[0].wait()
+def pack_kernel(targets, counts, length, tpl_ref, mask_ref, *tpl_outs):
     lane = lax.broadcasted_iota(jnp.int32, (1, LANES), 1)
-    for comp in range(comps):
-        copies[1 + comp].wait()
-        for index, rows in enumerate(counts):
-            lags = fold_lags(rows, length)
-            row = first_row(*targets[index], tpl_ref.shape[-1])
-            tile = pl.multiple_of(row // LANES * LANES, LANES)
-            mask = mask_held[:, pl.ds(tile, LANES)].astype(F32)
-            values = held_ref[comp, :, pl.ds(tile, LANES)].astype(F32) * mask
+    for target, rows, out_ref in zip(targets, counts, tpl_outs):
+        lags = fold_lags(rows, length)
+        row = first_row(*target, tpl_ref.shape[-1])
+        tile = pl.multiple_of(row // LANES * LANES, LANES)
+        mask = mask_ref[:, pl.ds(tile, LANES)].astype(F32)
+        for comp in range(tpl_ref.shape[0]):
+            values = tpl_ref[comp, :, pl.ds(tile, LANES)].astype(F32) * mask
             folded = jnp.zeros((lags, LANES), F32)
             for fold in range(LANES // rows):
                 piece = values[fold * lags : min((fold + 1) * lags, length)]
@@ -95,7 +92,7 @@
                 turned = pltpu.roll(piece, (fold * rows - row % LANES + LANES) % LANES, 1)
                 here = (lane >= fold * rows) & (lane < (fold + 1) * rows)
                 folded = jnp.where(here, turned, folded)
-            tpl_outs[index][comp] = folded.astype(BF16)
+            out_ref[comp] = folded.astype(BF16)
 
 
 def pack(targets, counts, tpl, mask):
@@ -103,13 +100,11 @@
     return pl.pallas_call(
         functools.partial(pack_kernel, targets, counts, length),
         out_shape=[jax.ShapeDtypeStruct((comps, fold_lags(rows, length), LANES), BF16) for rows in counts],
-        in_specs=[HBM] * 2,
+        in_specs=[VMEM] * 2,
         out_specs=[VMEM] * len(counts),
-        scratch_shapes=[pltpu.VMEM(x.shape, x.dtype) for x in (tpl, mask)]
-        + [pltpu.SemaphoreType.DMA((comps + 1,))],
         compiler_params=params(16),
         cost_estimate=CHEAP,
-    )(*[pltpu.with_memory_space_constraint(x, pltpu.HBM) for x in (tpl, mask)])
+    )(tpl, mask)
 
 
 def fill_samples(halo, tm_index, shard_refs, tail_refs, ext_ref):
@@ -285,11 +280,9 @@
 
     def storing_in(ref):
         def store(chunk):
-            chunk = chunk.astype(ref.dtype)
-            if ref.shape[0] > rows:
-                more = jnp.zeros((ref.shape[0] - rows, samples), ref.dtype)
-                chunk = jnp.concatenate([chunk, more], axis=0)
-            ref[...] = chunk
+            ref[:, :samples] = chunk.astype(ref.dtype)
+            if ref.shape[1] > samples:
+                ref[:, samples:] = jnp.zeros((rows, ref.shape[1] - samples), ref.dtype)
 
         return store
 
@@ -346,7 +339,7 @@
     tm_index = lax.axis_index("tm")
     copies = []
     for offset, ref in enumerate(part_refs):
-        held_ref[offset] = ref[: out_ref.shape[1], :].astype(F32)
+        held_ref[offset] = ref[:, : out_ref.shape[2]].astype(F32)
         copies.append(
             pltpu.make_async_copy(held_ref.at[offset], out_ref.at[tm_index ^ offset], left.at[offset])
         )
@@ -382,12 +375,11 @@
     final = chips // 2
     between = [1] + [offset for offset in range(chips - 1, 1, -1) if offset != final]
 
-    wave = join(waveforms[0], waveform_tail[0])
+    wave, tpl, mask = join(waveforms[0], waveform_tail[0], tpl, mask)
     waves = [wave] + [swap_with(wave, "sta", 2 * offset) for offset in range(1, chips)]
     offsets = [0] + between
     targets = [(offset, None) for offset in offsets] + [(final, 0), (final, 1)]
     messages = pack(targets, [rows] * len(offsets) + [own] * 2, tpl, mask)
-    messages, waves = lax.optimization_barrier((messages, waves))
     pieces = {offset: swap_with(messages[1 + i], "sta", 2 * offset) for i, offset in enumerate(between)}
     stacked = jnp.stack([part[:, :samples] for part in waves])
     shards = [stacked] + [swap_with(stacked, "tm", offset) for offset in range(1, tm_count)]
@@ -413,7 +405,7 @@
     (acc,) = later(kernel, own, total, length, [half], [straight, ext, inv, keep], flops=F_JOIN)
     kernel = functools.partial(closing_kernel, tm_count, own, length)
     parts = [jax.ShapeDtypeStruct((own, samples), F32)] + [
-        jax.ShapeDtypeStruct((own + (EXTRA if offset & (offset - 1) else 0), samples), BF16)
+        jax.ShapeDtypeStruct((own, samples + (EXTRA if offset & (offset - 1) else 0)), BF16)
         for offset in range(1, tm_count)
     ]
     inputs = [crossed, cross, acc, *came]

time: 42.8 us -> 41.6 us (0.972)
  waiting for transfers between devices: 9.88 us -> 8.55 us
  starting transfers between devices: 17.9 us -> 18.6 us
  Pallas kernels: 14.5 us -> 13.9 us
    ppermute x16, waiting for transfers between devices: 9.88 us -> 8.55 us  [swap_with(): return lax.ppermute(x, axis, [(i, i ^ offset) for i in range(size)])]
    pallas_call x1, Pallas kernels: 1.86 us -> 0.75 us  [pack(): pl.pallas_call(functools.partial(pack_kernel, targets, counts, length), o...]
    ppermute x16, starting transfers between devices: 17.9 us -> 18.6 us  [swap_with(): return lax.ppermute(x, axis, [(i, i ^ offset) for i in range(size)])]
    pallas_call x1, Pallas kernels: 0.73 us -> 1.26 us  [join(): pl.pallas_call(join_kernel, out_shape=[jax.ShapeDtypeStruct((wave.shape[0...]
  transfers between devices with their start and end apart: 16 -> 16, of which waited for: 7 -> 7; matrix products, arithmetic and copies ran while one was open for 0% -> 0% of each run, Pallas kernels for 25% -> 23%
where the time goes in v5:
time: 41.6 us; the launch traced here: 41.4 us
  starting transfers between devices  18.6 us (45%)
  Pallas kernels  13.9 us (33%)
  waiting for transfers between devices  8.55 us (21%)
    ppermute x16, starting transfers between devices, swap_with(): return lax.ppermute(x, axis, [(i, i ^ offset) for i in range(size)])  18.6 us
    ppermute x16, waiting for transfers between devices, swap_with(): return lax.ppermute(x, axis, [(i, i ^ offset) for i in range(size)])  8.55 us
    pallas_call x4, Pallas kernels, later(): pl.pallas_call(kernel, out_shape=out_shape, in_specs=[VMEM] * len(inputs)...  8.2 us
    pallas_call x1, Pallas kernels, first(): pl.pallas_call(functools.partial(first_kernel, len(shards), chips, rows,...  2.93 us
    pallas_call x1, Pallas kernels, join(): pl.pallas_call(join_kernel, out_shape=[jax.ShapeDtypeStruct((wave.shape[0...  1.26 us
  transfers between devices with their start and end apart: 16, of which 7 were waited for; matrix products, arithmetic and copies ran while one was open for 0% of the time, Pallas kernels for 23%

profile of v5, /device:TPU:0, one launch (start us, length us, event | category | flops | bytes accessed | tf_op | source)
XLA Modules:
  0.0 41.4 jit_solution(15239475013398859167)
XLA Ops:
  0.0 1.3 %shard_map.46 = (bf16[3,1536]{1,0:T(4,128)(2,1)S(1)}, bf16[3,600,256]{2,1,0:T(8,128)(2,1)S(1)}, s32[1,256]{1,0:T(1,128)S(1)}) custom-call(bf16[3,896]{1,0:T(4,128)(2,1)} %bitcast.15, bf16[3,599]{1,0:T(4,128)(2,1)} %bitcast.16, bf16[3,600,256]{2,1,0:T(8,128)(2,1)} %bitcast.14, s32[1,256]{1,0:T(1,128)} %bitcast.17), custom_call_target="tpu_custom_call" | custom-call | flops 1 | bytes 1 | tf_op jit(solution)/shard_map/pallas_call | solution.py:50
  1.3 5.1 %collective-permute-start.2 = (bf16[3,1536]{1,0:T(4,128)(2,1)S(1)}, bf16[3,1536]{1,0:T(4,128)(2,1)S(1)}, u32[]{:S(2)}, u32[]{:S(2)}) collective-permute-start(bf16[3,1536]{1,0:T(4,128)(2,1)S(1)} %get-tuple-element.31.refs_4_), channel_id=1, source_target_pairs={{0,6},{1,7},{2,4},{3,5},{4,2},{5,3},{6,0},{7,1},{8,14},{9,15},{10,... | collective-permute-start | bytes 27656 | tf_op jit(solution)/shard_map/ppermute | solution.py:30
  6.4 0.0 collective-permute-start.1
  6.4 0.6 %collective-permute-start = (bf16[3,1536]{1,0:T(4,128)(2,1)S(1)}, bf16[3,1536]{1,0:T(4,128)(2,1)S(1)}, u32[]{:S(2)}, u32[]{:S(2)}) collective-permute-start(bf16[3,1536]{1,0:T(4,128)(2,1)S(1)} %get-tuple-element.31.refs_4_), channel_id=1, source_target_pairs={{0,2},{1,3},{2,0},{3,1},{4,6},{5,7},{6,4},{7,5},{8,10},{9,11},{10,... | collective-permute-start | bytes 27656 | tf_op jit(solution)/shard_map/ppermute | solution.py:30
  7.0 0.8 %shard_map.47 = (bf16[3,304,128]{2,1,0:T(8,128)(2,1)S(1)}, bf16[3,304,128]{2,1,0:T(8,128)(2,1)S(1)}, bf16[3,304,128]{2,1,0:T(8,128)(2,1)S(1)}, bf16[3,152,128]{2,1,0:T(8,128)(2,1)S(1)}, bf16[3,152,128]{2,1,0:T(8,128)(2,1)S(1)}) custom-call(bf16[3,600,256]{2,1,0:T(8,128)(2,1)S(1)} %get-tuple-element.28.tpl_ref, s32[1,256]{1,0:T(1,128)S(1)} %get-tuple-element.29.mask_ref), custom_call_target="tpu_custom_call" | custom-call | flops 1 | bytes 1 | tf_op jit(solution)/shard_map/pallas_call | solution.py:100
  7.8 3.8 %collective-permute-start.9 = (bf16[3,304,128]{2,1,0:T(8,128)(2,1)S(1)}, bf16[3,304,128]{2,1,0:T(8,128)(2,1)S(1)}, u32[]{:S(2)}, u32[]{:S(2)}) collective-permute-start(bf16[3,304,128]{2,1,0:T(8,128)(2,1)S(1)} %get-tuple-element.41), channel_id=1, source_target_pairs={{0,6},{1,7},{2,4},{3,5},{4,2},{5,3},{6,0},{7,1},{8,14},{9,15},{10,... | collective-permute-start | bytes 700424 | tf_op jit(solution)/shard_map/ppermute | solution.py:30
  11.6 0.0 collective-permute-start.10
  11.6 0.0 collective-permute-done.2.refs_7_
  11.7 0.0 collective-permute-done.1.refs_6_
  11.7 0.0 collective-permute-done.refs_5_
  11.7 2.5 %collective-permute-start.6 = (bf16[4,3,896]{2,1,0:T(4,128)(2,1)S(1)}, bf16[4,3,896]{2,1,0:T(4,128)(2,1)S(1)}, u32[]{:S(2)}, u32[]{:S(2)}) collective-permute-start(bf16[4,3,896]{2,1,0:T(4,128)(2,1)S(1)} %pad_maximum_fusion.refs_0_), channel_id=1, source_target_pairs={{0,24},{8,16},{16,8},{24,0},{1,25},{9,17},{17,9},{25,1},{2,26},{10... | collective-permute-start | bytes 64520 | tf_op jit(solution)/shard_map/ppermute | solution.py:30
  14.2 0.5 %collective-permute-start.3 = (bf16[4,3,896]{2,1,0:T(4,128)(2,1)S(1)}, bf16[4,3,896]{2,1,0:T(4,128)(2,1)S(1)}, u32[]{:S(2)}, u32[]{:S(2)}) collective-permute-start(bf16[4,3,896]{2,1,0:T(4,128)(2,1)S(1)} %pad_maximum_fusion.refs_0_), channel_id=1, source_target_pairs={{0,16},{8,24},{16,0},{24,8},{1,17},{9,25},{17,1},{25,9},{2,18},{10... | collective-permute-start | bytes 64520 | tf_op jit(solution)/shard_map/ppermute | solution.py:30
  14.8 0.5 %collective-permute-start.5 = (bf16[4,3,896]{2,1,0:T(4,128)(2,1)S(1)}, bf16[4,3,896]{2,1,0:T(4,128)(2,1)S(1)}, u32[]{:S(2)}, u32[]{:S(2)}) collective-permute-start(bf16[4,3,896]{2,1,0:T(4,128)(2,1)S(1)} %pad_maximum_fusion.refs_0_), channel_id=1, source_target_pairs={{0,8},{8,0},{16,24},{24,16},{1,9},{9,1},{17,25},{25,17},{2,10},{10... | collective-permute-start | bytes 64520 | tf_op jit(solution)/shard_map/ppermute | solution.py:30
  15.3 1.4 %collective-permute-done.6.refs_3_ = bf16[4,3,896]{2,1,0:T(4,128)(2,1)S(1)} collective-permute-done((bf16[4,3,896]{2,1,0:T(4,128)(2,1)S(1)}, bf16[4,3,896]{2,1,0:T(4,128)(2,1)S(1)}, u32[]{:S(2)}, u32[]{:S(2)}) %collective-permute-start.6) | collective-permute-done | bytes 21536 | tf_op jit(solution)/shard_map/ppermute | solution.py:30
  16.7 1.3 %collective-permute-start.8 = (bf16[3,152,128]{2,1,0:T(8,128)(2,1)S(1)}, bf16[3,152,128]{2,1,0:T(8,128)(2,1)S(1)}, u32[]{:S(2)}, u32[]{:S(2)}) collective-permute-start(bf16[3,152,128]{2,1,0:T(8,128)(2,1)S(1)} %get-tuple-element.38), channel_id=1, source_target_pairs={{0,4},{1,5},{2,6},{3,7},{4,0},{5,1},{6,2},{7,3},{8,12},{9,13},{10,... | collective-permute-start | bytes 350216 | tf_op jit(solution)/shard_map/ppermute | solution.py:30
  18.0 0.1 collective-permute-done.3.refs_2_
  18.1 0.0 collective-permute-start.4
  18.1 0.5 %collective-permute-done.5.refs_1_ = bf16[4,3,896]{2,1,0:T(4,128)(2,1)S(1)} collective-permute-done((bf16[4,3,896]{2,1,0:T(4,128)(2,1)S(1)}, bf16[4,3,896]{2,1,0:T(4,128)(2,1)S(1)}, u32[]{:S(2)}, u32[]{:S(2)}) %collective-permute-start.5) | collective-permute-done | bytes 21536 | tf_op jit(solution)/shard_map/ppermute | solution.py:30
  18.6 2.9 %shard_map.48 = (f32[12,4224]{1,0:T(8,128)S(1)}, f32[12,3584]{1,0:T(8,128)S(1)}, f32[6,4224]{1,0:T(8,128)S(1)}, f32[64,3584]{1,0:T(8,128)S(1)}) custom-call(bf16[3,304,128]{2,1,0:T(8,128)(2,1)S(1)} %get-tuple-element.33.tpl_ref, bf16[4,3,896]{2,1,0:T(4,128)(2,1)S(1)} %pad_maximum_fusion.refs_0_, bf16[4,3,896]{2,1,0:T(4,128)(2,1)S(1)} %collective-permute-done.5.refs_1_, ...), custom_call_target="tpu_custom_call" | custom-call | flops 1 | bytes 1 | tf_op jit(solution)/shard_map/pallas_call | solution.py:307
  21.6 1.2 %collective-permute-done.10.tpl_ref = bf16[3,304,128]{2,1,0:T(8,128)(2,1)S(1)} collective-permute-done((bf16[3,304,128]{2,1,0:T(8,128)(2,1)S(1)}, bf16[3,304,128]{2,1,0:T(8,128)(2,1)S(1)}, u32[]{:S(2)}, u32[]{:S(2)}) %collective-permute-start.10) | collective-permute-done | bytes 233504 | tf_op jit(solution)/shard_map/ppermute | solution.py:30
  22.8 2.1 %shard_map.49.acc_ref = f32[64,3584]{1,0:T(8,128)S(1)} custom-call(bf16[3,304,128]{2,1,0:T(8,128)(2,1)S(1)} %collective-permute-done.10.tpl_ref, f32[12,4224]{1,0:T(8,128)S(1)} %get-tuple-element.39.ext_ref, f32[12,3584]{1,0:T(8,128)S(1)} %get-tuple-element.40.inv_ref, f32[64,3584]{1,0:T(8,128)S(1)} %get-tuple-element.43.acc_ref), custom_call_target="tpu_custom_call" | custom-call | flops 500000000 | bytes 1 | tf_op jit(solution)/shard_map/pallas_call | solution.py:326
  24.8 0.0 collective-permute-done.9.tpl_ref
  24.8 2.1 %shard_map.50 = (f32[32,3584]{1,0:T(8,128)S(1)}, bf16[32,1792]{1,0:T(8,128)(2,1)S(1)}, bf16[32,1792]{1,0:T(8,128)(2,1)S(1)}) custom-call(bf16[3,304,128]{2,1,0:T(8,128)(2,1)S(1)} %collective-permute-done.9.tpl_ref, f32[12,4224]{1,0:T(8,128)S(1)} %get-tuple-element.39.ext_ref, f32[12,3584]{1,0:T(8,128)S(1)} %get-tuple-element.40.inv_ref, ...), custom_call_target="tpu_custom_call" | custom-call | flops 1 | bytes 1 | tf_op jit(solution)/shard_map/pallas_call | solution.py:326
  26.9 0.1 collective-permute-start.11
  27.0 0.5 %collective-permute-start.12 = (bf16[32,1792]{1,0:T(8,128)(2,1)S(1)}, bf16[32,1792]{1,0:T(8,128)(2,1)S(1)}, u32[]{:S(2)}, u32[]{:S(2)}) collective-permute-start(bf16[32,1792]{1,0:T(8,128)(2,1)S(1)} %get-tuple-element.46), channel_id=1, source_target_pairs={{0,1},{1,0},{2,3},{3,2},{4,5},{5,4},{6,7},{7,6},{8,9},{9,8},{10,11... | collective-permute-start | bytes 344072 | tf_op jit(solution)/shard_map/ppermute | solution.py:30
  27.5 0.1 collective-permute-start.7
  27.6 1.6 %collective-permute-done.8.tpl_ref = bf16[3,152,128]{2,1,0:T(8,128)(2,1)S(1)} collective-permute-done((bf16[3,152,128]{2,1,0:T(8,128)(2,1)S(1)}, bf16[3,152,128]{2,1,0:T(8,128)(2,1)S(1)}, u32[]{:S(2)}, u32[]{:S(2)}) %collective-permute-start.8) | collective-permute-done | bytes 116768 | tf_op jit(solution)/shard_map/ppermute | solution.py:30
  29.2 1.9 %shard_map.51.acc_ref = f32[32,3584]{1,0:T(8,128)S(1)} custom-call(bf16[3,152,128]{2,1,0:T(8,128)(2,1)S(1)} %collective-permute-done.8.tpl_ref, f32[12,4224]{1,0:T(8,128)S(1)} %get-tuple-element.39.ext_ref, f32[12,3584]{1,0:T(8,128)S(1)} %get-tuple-element.40.inv_ref, f32[32,3584]{1,0:T(8,128)S(1)} %get-tuple-element.44.acc_ref), custom_call_target="tpu_custom_call" | custom-call | flops 500000000 | bytes 1 | tf_op jit(solution)/shard_map/pallas_call | solution.py:326
  31.1 0.0 collective-permute-done.7.cross_ref
  31.1 0.0 collective-permute-done.4.tpl_ref
  31.1 0.0 collective-permute-done.11.early_ref
  31.1 0.0 collective-permute-done.12.late_ref
  31.1 2.2 %shard_map.52 = (f32[32,896]{1,0:T(8,128)S(1)}, bf16[32,896]{1,0:T(8,128)(2,1)S(1)}, bf16[32,896]{1,0:T(8,128)(2,1)S(1)}, bf16[32,1024]{1,0:T(8,128)(2,1)S(1)}) custom-call(bf16[3,152,128]{2,1,0:T(8,128)(2,1)S(1)} %collective-permute-done.4.tpl_ref, f32[6,4224]{1,0:T(8,128)S(1)} %collective-permute-done.7.cross_ref, f32[32,3584]{1,0:T(8,128)S(1)} %shard_map.51.acc_ref, ...), custom_call_target="tpu_custom_call" | custom-call | flops 1 | bytes 1 | tf_op jit(solution)/shard_map/pallas_call | solution.py:326
  33.3 2.5 %collective-permute-start.15 = (bf16[32,1024]{1,0:T(8,128)(2,1)S(1)}, bf16[32,1024]{1,0:T(8,128)(2,1)S(1)}, u32[]{:S(2)}, u32[]{:S(2)}) collective-permute-start(bf16[32,1024]{1,0:T(8,128)(2,1)S(1)} %get-tuple-element.50), channel_id=1, source_target_pairs={{0,24},{8,16},{16,8},{24,0},{1,25},{9,17},{17,9},{25,1},{2,26},{10... | collective-permute-start | bytes 196616 | tf_op jit(solution)/shard_map/ppermute | solution.py:30
  35.8 0.5 %collective-permute-start.13 = (bf16[32,896]{1,0:T(8,128)(2,1)S(1)}, bf16[32,896]{1,0:T(8,128)(2,1)S(1)}, u32[]{:S(2)}, u32[]{:S(2)}) collective-permute-start(bf16[32,896]{1,0:T(8,128)(2,1)S(1)} %get-tuple-element.48), channel_id=1, source_target_pairs={{0,8},{8,0},{16,24},{24,16},{1,9},{9,1},{17,25},{25,17},{2,10},{10... | collective-permute-start | bytes 172040 | tf_op jit(solution)/shard_map/ppermute | solution.py:30
  36.4 0.5 %collective-permute-start.14 = (bf16[32,896]{1,0:T(8,128)(2,1)S(1)}, bf16[32,896]{1,0:T(8,128)(2,1)S(1)}, u32[]{:S(2)}, u32[]{:S(2)}) collective-permute-start(bf16[32,896]{1,0:T(8,128)(2,1)S(1)} %get-tuple-element.49), channel_id=1, source_target_pairs={{0,16},{8,24},{16,0},{24,8},{1,17},{9,25},{17,1},{25,9},{2,18},{10... | collective-permute-start | bytes 172040 | tf_op jit(solution)/shard_map/ppermute | solution.py:30
  36.9 3.1 %collective-permute-done.13.refs_1_ = bf16[32,896]{1,0:T(8,128)(2,1)S(1)} collective-permute-done((bf16[32,896]{1,0:T(8,128)(2,1)S(1)}, bf16[32,896]{1,0:T(8,128)(2,1)S(1)}, u32[]{:S(2)}, u32[]{:S(2)}) %collective-permute-start.13) | collective-permute-done | bytes 57376 | tf_op jit(solution)/shard_map/ppermute | solution.py:30
  40.0 0.5 %collective-permute-done.14.refs_2_ = bf16[32,896]{1,0:T(8,128)(2,1)S(1)} collective-permute-done((bf16[32,896]{1,0:T(8,128)(2,1)S(1)}, bf16[32,896]{1,0:T(8,128)(2,1)S(1)}, u32[]{:S(2)}, u32[]{:S(2)}) %collective-permute-start.14) | collective-permute-done | bytes 57376 | tf_op jit(solution)/shard_map/ppermute | solution.py:30
  40.6 0.0 collective-permute-done.15.refs_3_
  40.6 0.8 %shard_map.53 = f32[4,32,896]{2,1,0:T(8,128)} custom-call(f32[32,896]{1,0:T(8,128)S(1)} %get-tuple-element.47.refs_0_, bf16[32,896]{1,0:T(8,128)(2,1)S(1)} %collective-permute-done.13.refs_1_, bf16[32,896]{1,0:T(8,128)(2,1)S(1)} %collective-permute-done.14.refs_2_, bf16[32,1024]{1,0:T(8,128)(2,1)S(1)} %collective-permute-done.15.refs_3_), custom_call_target="tpu_custom_call" | custom-call | tf_op jit(solution)/shard_map/pallas_call | solution.py:353
  (5 shorter events, 0.1 us)
Async XLA Ops:
  1.3 10.4 %collective-permute-start.2 = (bf16[3,1536]{1,0:T(4,128)(2,1)S(1)}, bf16[3,1536]{1,0:T(4,128)(2,1)S(1)}, u32[]{:S(2)}, u32[]{:S(2)}) collective-permute-start(bf16[3,1536]{1,0:T(4,128)(2,1)S(1)} %get-tuple-element.31.refs_4_), channel_id=1, source_target_pairs={{0,6},{1,7},{2,4},{3,5},{4,2},{5,3},{6,0},{7,1},{8,14},{9,15},{10,... | collective-permute-start | bytes 27656 | tf_op jit(solution)/shard_map/ppermute | solution.py:30
  6.4 5.3 %collective-permute-start.1 = (bf16[3,1536]{1,0:T(4,128)(2,1)S(1)}, bf16[3,1536]{1,0:T(4,128)(2,1)S(1)}, u32[]{:S(2)}, u32[]{:S(2)}) collective-permute-start(bf16[3,1536]{1,0:T(4,128)(2,1)S(1)} %get-tuple-element.31.refs_4_), channel_id=1, source_target_pairs={{0,4},{1,5},{2,6},{3,7},{4,0},{5,1},{6,2},{7,3},{8,12},{9,13},{10,... | collective-permute-start | bytes 27656 | tf_op jit(solution)/shard_map/ppermute | solution.py:30
  6.4 5.3 %collective-permute-start = (bf16[3,1536]{1,0:T(4,128)(2,1)S(1)}, bf16[3,1536]{1,0:T(4,128)(2,1)S(1)}, u32[]{:S(2)}, u32[]{:S(2)}) collective-permute-start(bf16[3,1536]{1,0:T(4,128)(2,1)S(1)} %get-tuple-element.31.refs_4_), channel_id=1, source_target_pairs={{0,2},{1,3},{2,0},{3,1},{4,6},{5,7},{6,4},{7,5},{8,10},{9,11},{10,... | collective-permute-start | bytes 27656 | tf_op jit(solution)/shard_map/ppermute | solution.py:30
  7.8 17.0 %collective-permute-start.9 = (bf16[3,304,128]{2,1,0:T(8,128)(2,1)S(1)}, bf16[3,304,128]{2,1,0:T(8,128)(2,1)S(1)}, u32[]{:S(2)}, u32[]{:S(2)}) collective-permute-start(bf16[3,304,128]{2,1,0:T(8,128)(2,1)S(1)} %get-tuple-element.41), channel_id=1, source_target_pairs={{0,6},{1,7},{2,4},{3,5},{4,2},{5,3},{6,0},{7,1},{8,14},{9,15},{10,... | collective-permute-start | bytes 700424 | tf_op jit(solution)/shard_map/ppermute | solution.py:30
  11.6 11.2 %collective-permute-start.10 = (bf16[3,304,128]{2,1,0:T(8,128)(2,1)S(1)}, bf16[3,304,128]{2,1,0:T(8,128)(2,1)S(1)}, u32[]{:S(2)}, u32[]{:S(2)}) collective-permute-start(bf16[3,304,128]{2,1,0:T(8,128)(2,1)S(1)} %get-tuple-element.42), channel_id=1, source_target_pairs={{0,2},{1,3},{2,0},{3,1},{4,6},{5,7},{6,4},{7,5},{8,10},{9,11},{10,... | collective-permute-start | bytes 700424 | tf_op jit(solution)/shard_map/ppermute | solution.py:30
  11.7 5.0 %collective-permute-start.6 = (bf16[4,3,896]{2,1,0:T(4,128)(2,1)S(1)}, bf16[4,3,896]{2,1,0:T(4,128)(2,1)S(1)}, u32[]{:S(2)}, u32[]{:S(2)}) collective-permute-start(bf16[4,3,896]{2,1,0:T(4,128)(2,1)S(1)} %pad_maximum_fusion.refs_0_), channel_id=1, source_target_pairs={{0,24},{8,16},{16,8},{24,0},{1,25},{9,17},{17,9},{25,1},{2,26},{10... | collective-permute-start | bytes 64520 | tf_op jit(solution)/shard_map/ppermute | solution.py:30
  14.2 3.9 %collective-permute-start.3 = (bf16[4,3,896]{2,1,0:T(4,128)(2,1)S(1)}, bf16[4,3,896]{2,1,0:T(4,128)(2,1)S(1)}, u32[]{:S(2)}, u32[]{:S(2)}) collective-permute-start(bf16[4,3,896]{2,1,0:T(4,128)(2,1)S(1)} %pad_maximum_fusion.refs_0_), channel_id=1, source_target_pairs={{0,16},{8,24},{16,0},{24,8},{1,17},{9,25},{17,1},{25,9},{2,18},{10... | collective-permute-start | bytes 64520 | tf_op jit(solution)/shard_map/ppermute | solution.py:30
  14.8 3.9 %collective-permute-start.5 = (bf16[4,3,896]{2,1,0:T(4,128)(2,1)S(1)}, bf16[4,3,896]{2,1,0:T(4,128)(2,1)S(1)}, u32[]{:S(2)}, u32[]{:S(2)}) collective-permute-start(bf16[4,3,896]{2,1,0:T(4,128)(2,1)S(1)} %pad_maximum_fusion.refs_0_), channel_id=1, source_target_pairs={{0,8},{8,0},{16,24},{24,16},{1,9},{9,1},{17,25},{25,17},{2,10},{10... | collective-permute-start | bytes 64520 | tf_op jit(solution)/shard_map/ppermute | solution.py:30
  16.7 12.5 %collective-permute-start.8 = (bf16[3,152,128]{2,1,0:T(8,128)(2,1)S(1)}, bf16[3,152,128]{2,1,0:T(8,128)(2,1)S(1)}, u32[]{:S(2)}, u32[]{:S(2)}) collective-permute-start(bf16[3,152,128]{2,1,0:T(8,128)(2,1)S(1)} %get-tuple-element.38), channel_id=1, source_target_pairs={{0,4},{1,5},{2,6},{3,7},{4,0},{5,1},{6,2},{7,3},{8,12},{9,13},{10,... | collective-permute-start | bytes 350216 | tf_op jit(solution)/shard_map/ppermute | solution.py:30
  18.1 13.0 %collective-permute-start.4 = (bf16[3,152,128]{2,1,0:T(8,128)(2,1)S(1)}, bf16[3,152,128]{2,1,0:T(8,128)(2,1)S(1)}, u32[]{:S(2)}, u32[]{:S(2)}) collective-permute-start(bf16[3,152,128]{2,1,0:T(8,128)(2,1)S(1)} %get-tuple-element.32), channel_id=1, source_target_pairs={{0,5},{1,4},{2,7},{3,6},{4,1},{5,0},{6,3},{7,2},{8,13},{9,12},{10,... | collective-permute-start | bytes 350216 | tf_op jit(solution)/shard_map/ppermute | solution.py:30
  26.9 4.2 %collective-permute-start.11 = (bf16[32,1792]{1,0:T(8,128)(2,1)S(1)}, bf16[32,1792]{1,0:T(8,128)(2,1)S(1)}, u32[]{:S(2)}, u32[]{:S(2)}) collective-permute-start(bf16[32,1792]{1,0:T(8,128)(2,1)S(1)} %get-tuple-element.45), channel_id=1, source_target_pairs={{0,1},{1,0},{2,3},{3,2},{4,5},{5,4},{6,7},{7,6},{8,9},{9,8},{10,11... | collective-permute-start | bytes 344072 | tf_op jit(solution)/shard_map/ppermute | solution.py:30
  27.0 4.1 %collective-permute-start.12 = (bf16[32,1792]{1,0:T(8,128)(2,1)S(1)}, bf16[32,1792]{1,0:T(8,128)(2,1)S(1)}, u32[]{:S(2)}, u32[]{:S(2)}) collective-permute-start(bf16[32,1792]{1,0:T(8,128)(2,1)S(1)} %get-tuple-element.46), channel_id=1, source_target_pairs={{0,1},{1,0},{2,3},{3,2},{4,5},{5,4},{6,7},{7,6},{8,9},{9,8},{10,11... | collective-permute-start | bytes 344072 | tf_op jit(solution)/shard_map/ppermute | solution.py:30
  27.5 3.6 %collective-permute-start.7 = (f32[6,4224]{1,0:T(8,128)S(1)}, f32[6,4224]{1,0:T(8,128)S(1)}, u32[]{:S(2)}, u32[]{:S(2)}) collective-permute-start(f32[6,4224]{1,0:T(8,128)S(1)} %get-tuple-element.37), channel_id=1, source_target_pairs={{0,1},{1,0},{2,3},{3,2},{4,5},{5,4},{6,7},{7,6},{8,9},{9,8},{10,11... | collective-permute-start | bytes 304136 | tf_op jit(solution)/shard_map/ppermute | solution.py:30
  33.3 7.2 %collective-permute-start.15 = (bf16[32,1024]{1,0:T(8,128)(2,1)S(1)}, bf16[32,1024]{1,0:T(8,128)(2,1)S(1)}, u32[]{:S(2)}, u32[]{:S(2)}) collective-permute-start(bf16[32,1024]{1,0:T(8,128)(2,1)S(1)} %get-tuple-element.50), channel_id=1, source_target_pairs={{0,24},{8,16},{16,8},{24,0},{1,25},{9,17},{17,9},{25,1},{2,26},{10... | collective-permute-start | bytes 196616 | tf_op jit(solution)/shard_map/ppermute | solution.py:30
  35.8 4.2 %collective-permute-start.13 = (bf16[32,896]{1,0:T(8,128)(2,1)S(1)}, bf16[32,896]{1,0:T(8,128)(2,1)S(1)}, u32[]{:S(2)}, u32[]{:S(2)}) collective-permute-start(bf16[32,896]{1,0:T(8,128)(2,1)S(1)} %get-tuple-element.48), channel_id=1, source_target_pairs={{0,8},{8,0},{16,24},{24,16},{1,9},{9,1},{17,25},{25,17},{2,10},{10... | collective-permute-start | bytes 172040 | tf_op jit(solution)/shard_map/ppermute | solution.py:30
  36.4 4.2 %collective-permute-start.14 = (bf16[32,896]{1,0:T(8,128)(2,1)S(1)}, bf16[32,896]{1,0:T(8,128)(2,1)S(1)}, u32[]{:S(2)}, u32[]{:S(2)}) collective-permute-start(bf16[32,896]{1,0:T(8,128)(2,1)S(1)} %get-tuple-element.49), channel_id=1, source_target_pairs={{0,16},{8,24},{16,0},{24,8},{1,17},{9,25},{17,1},{25,9},{2,18},{10... | collective-permute-start | bytes 172040 | tf_op jit(solution)/shard_map/ppermute | solution.py:30

commit v6 on v5

--- a/solution.py
+++ b/solution.py
@@ -185,13 +185,16 @@
     out_ref[...] = pltpu.roll(spread, width - (LANES - 1), 1, stride=1, stride_axis=0)
 
 
-def multiply(ext_at, rows, length, tpl_ref, ext_ref, work_refs):
+def multiply(ext_at, rows, length, tpl_ref, ext_ref, work_refs, between=None):
     hankel_ref, product_ref = work_refs
     reach = product_ref.shape[-1]
-    for comp in range(tpl_ref.shape[0]):
+    comps = tpl_ref.shape[0]
+    for comp in range(comps):
         fill_hankel(ext_ref[ext_at + comp : ext_at + comp + 1, :], hankel_ref.at[comp])
-    lhs = [lag_rows(tpl_ref[comp].astype(F32), rows, length) for comp in range(tpl_ref.shape[0])]
-    for comp in range(tpl_ref.shape[0]):
+    lhs = [lag_rows(tpl_ref[comp].astype(F32), rows, length) for comp in range(comps)]
+    for comp in range(comps):
+        if comp == comps - 1 and between is not None:
+            between()
         rhs = jnp.concatenate(
             [hankel_ref[comp, :, :reach], hankel_ref[comp, :, LANES : LANES + reach]], axis=0
         )
@@ -206,7 +209,7 @@
         for ref in acc_refs:
             part = ref[:, pl.ds(start, size)]
             chunk = part if chunk is None else chunk + part
-        for comp in range(comps):
+        for comp in comps:
             part = product_ref[comp, :rows, pl.ds(start, size)]
             for split in range(1, splits):
                 shift = split * 2 * LANES
@@ -232,7 +235,7 @@
 def correlate(at, rows, length, tpl_ref, ext_ref, inv_ref, acc_refs, work_refs, store):
     multiply(at, rows, length, tpl_ref, ext_ref, work_refs)
     spans = spans_of(inv_ref.shape[-1], store)
-    collect(at, rows, tpl_ref.shape[0], inv_ref, acc_refs, work_refs, spans)
+    collect(at, rows, range(tpl_ref.shape[0]), inv_ref, acc_refs, work_refs, spans)
 
 
 def first_kernel(shards, chips, rows, length, halo, crossing, tpl_ref, *refs):
@@ -245,7 +248,7 @@
     cross_ref[:comps, :] = ext_ref[crossing * comps : (crossing + 1) * comps, :]
     cross_ref[comps:, :total] = inv_ref[crossing * comps : (crossing + 1) * comps, :]
     cross_ref[comps:, total:] = jnp.zeros((comps, cross_ref.shape[-1] - total), F32)
-    collect(0, rows, comps, inv_ref, [], work_refs, spans_of(total, storing(sum_ref)))
+    collect(0, rows, range(comps), inv_ref, [], work_refs, spans_of(total, storing(sum_ref)))
 
 
 def middle_kernel(at, rows, length, tpl_ref, ext_ref, inv_ref, acc_ref, sum_ref, *work_refs):
@@ -274,8 +277,13 @@
     comps, middle = tpl_ref.shape[0], early_ref.shape[-1]
     sum_ref[:, :middle] = acc_ref[:, :middle] + early_ref[...].astype(F32)
     sum_ref[:, middle:] = acc_ref[:, middle:] + late_ref[...].astype(F32)
-    multiply(0, rows, length, tpl_ref, cross_ref, work_refs)
     samples = out_refs[0].shape[-1]
+
+    def early_components():
+        spans = spans_of(sum_ref.shape[-1], storing(sum_ref))
+        collect(comps, rows, range(comps - 1), cross_ref, [sum_ref], work_refs, spans)
+
+    multiply(0, rows, length, tpl_ref, cross_ref, work_refs, early_components)
     tm_index = lax.axis_index("tm")
 
     def storing_in(ref):
@@ -290,7 +298,7 @@
         (pl.multiple_of((tm_index ^ offset) * samples, LANES), samples, storing_in(ref))
         for offset, ref in enumerate(out_refs)
     ]
-    collect(comps, rows, comps, cross_ref, [sum_ref], work_refs, spans)
+    collect(comps, rows, [comps - 1], cross_ref, [sum_ref], work_refs, spans)
 
 
 def work_buffers(comps, rows, total, width, length):
@@ -387,8 +395,9 @@
     late[0], shards[-1] = lax.optimization_barrier((messages[-2], shards[-1]))
     late[1], shards[-2] = lax.optimization_barrier((messages[-1], shards[-2]))
     straight = swap_with(late[0], "sta", 2 * final)
-    crossed = swap_with(late[1], "sta", 2 * final + 1)
     ext, inv, cross, acc = first(rows, length, halo, final, messages[0], shards, waves)
+    latest, acc = lax.optimization_barrier((late[1], acc))
+    crossed = swap_with(latest, "sta", 2 * final + 1)
     cross = swap_with(cross, "sta", 1)
     whole = jax.ShapeDtypeStruct((rows, total), F32)
     for offset in between[:-1]:

time: 41.6 us -> 40.8 us (0.981)
  waiting for transfers between devices: 8.55 us -> 7.34 us
  starting transfers between devices: 18.6 us -> 19.3 us
    ppermute x16, waiting for transfers between devices: 8.55 us -> 7.34 us  [swap_with(): return lax.ppermute(x, axis, [(i, i ^ offset) for i in range(size)])]
    ppermute x16, starting transfers between devices: 18.6 us -> 19.3 us  [swap_with(): return lax.ppermute(x, axis, [(i, i ^ offset) for i in range(size)])]
  transfers between devices with their start and end apart: 16 -> 16, of which waited for: 7 -> 7; matrix products, arithmetic and copies ran while one was open for 0% -> 0% of each run, Pallas kernels for 23% -> 24%
where the time goes in v6:
time: 40.8 us; the launch traced here: 40.6 us
  starting transfers between devices  19.3 us (47%)
  Pallas kernels  13.7 us (34%)
  waiting for transfers between devices  7.34 us (18%)
    ppermute x16, starting transfers between devices, swap_with(): return lax.ppermute(x, axis, [(i, i ^ offset) for i in range(size)])  19.3 us
    pallas_call x4, Pallas kernels, later(): pl.pallas_call(kernel, out_shape=out_shape, in_specs=[VMEM] * len(inputs)...  8 us
    ppermute x16, waiting for transfers between devices, swap_with(): return lax.ppermute(x, axis, [(i, i ^ offset) for i in range(size)])  7.34 us
    pallas_call x1, Pallas kernels, first(): pl.pallas_call(functools.partial(first_kernel, len(shards), chips, rows,...  2.93 us
    pallas_call x1, Pallas kernels, join(): pl.pallas_call(join_kernel, out_shape=[jax.ShapeDtypeStruct((wave.shape[0...  1.26 us
  transfers between devices with their start and end apart: 16, of which 7 were waited for; matrix products, arithmetic and copies ran while one was open for 0% of the time, Pallas kernels for 24%

profile of v6, /device:TPU:0, one launch (start us, length us, event | category | flops | bytes accessed | tf_op | source)
XLA Modules:
  0.0 40.6 jit_solution(1048243757804804524)
XLA Ops:
  0.0 1.3 %shard_map.46 = (bf16[3,1536]{1,0:T(4,128)(2,1)S(1)}, bf16[3,600,256]{2,1,0:T(8,128)(2,1)S(1)}, s32[1,256]{1,0:T(1,128)S(1)}) custom-call(bf16[3,896]{1,0:T(4,128)(2,1)} %bitcast.15, bf16[3,599]{1,0:T(4,128)(2,1)} %bitcast.16, bf16[3,600,256]{2,1,0:T(8,128)(2,1)} %bitcast.14, s32[1,256]{1,0:T(1,128)} %bitcast.17), custom_call_target="tpu_custom_call" | custom-call | flops 1 | bytes 1 | tf_op jit(solution)/shard_map/pallas_call | solution.py:50
  1.3 5.1 %collective-permute-start.2 = (bf16[3,1536]{1,0:T(4,128)(2,1)S(1)}, bf16[3,1536]{1,0:T(4,128)(2,1)S(1)}, u32[]{:S(2)}, u32[]{:S(2)}) collective-permute-start(bf16[3,1536]{1,0:T(4,128)(2,1)S(1)} %get-tuple-element.33.refs_4_), channel_id=1, source_target_pairs={{0,6},{1,7},{2,4},{3,5},{4,2},{5,3},{6,0},{7,1},{8,14},{9,15},{10,... | collective-permute-start | bytes 27656 | tf_op jit(solution)/shard_map/ppermute | solution.py:30
  6.4 0.0 collective-permute-start.1
  6.4 0.6 %collective-permute-start = (bf16[3,1536]{1,0:T(4,128)(2,1)S(1)}, bf16[3,1536]{1,0:T(4,128)(2,1)S(1)}, u32[]{:S(2)}, u32[]{:S(2)}) collective-permute-start(bf16[3,1536]{1,0:T(4,128)(2,1)S(1)} %get-tuple-element.33.refs_4_), channel_id=1, source_target_pairs={{0,2},{1,3},{2,0},{3,1},{4,6},{5,7},{6,4},{7,5},{8,10},{9,11},{10,... | collective-permute-start | bytes 27656 | tf_op jit(solution)/shard_map/ppermute | solution.py:30
  7.0 0.8 %shard_map.47 = (bf16[3,304,128]{2,1,0:T(8,128)(2,1)S(1)}, bf16[3,304,128]{2,1,0:T(8,128)(2,1)S(1)}, bf16[3,304,128]{2,1,0:T(8,128)(2,1)S(1)}, bf16[3,152,128]{2,1,0:T(8,128)(2,1)S(1)}, bf16[3,152,128]{2,1,0:T(8,128)(2,1)S(1)}) custom-call(bf16[3,600,256]{2,1,0:T(8,128)(2,1)S(1)} %get-tuple-element.30.tpl_ref, s32[1,256]{1,0:T(1,128)S(1)} %get-tuple-element.31.mask_ref), custom_call_target="tpu_custom_call" | custom-call | flops 1 | bytes 1 | tf_op jit(solution)/shard_map/pallas_call | solution.py:100
  7.8 3.8 %collective-permute-start.9 = (bf16[3,304,128]{2,1,0:T(8,128)(2,1)S(1)}, bf16[3,304,128]{2,1,0:T(8,128)(2,1)S(1)}, u32[]{:S(2)}, u32[]{:S(2)}) collective-permute-start(bf16[3,304,128]{2,1,0:T(8,128)(2,1)S(1)} %get-tuple-element.45), channel_id=1, source_target_pairs={{0,6},{1,7},{2,4},{3,5},{4,2},{5,3},{6,0},{7,1},{8,14},{9,15},{10,... | collective-permute-start | bytes 700424 | tf_op jit(solution)/shard_map/ppermute | solution.py:30
  11.6 0.0 collective-permute-start.10
  11.6 0.0 collective-permute-done.2.refs_7_
  11.7 0.0 collective-permute-done.1.refs_6_
  11.7 0.0 collective-permute-done.refs_5_
  11.7 2.5 %collective-permute-start.5 = (bf16[4,3,896]{2,1,0:T(4,128)(2,1)S(1)}, bf16[4,3,896]{2,1,0:T(4,128)(2,1)S(1)}, u32[]{:S(2)}, u32[]{:S(2)}) collective-permute-start(bf16[4,3,896]{2,1,0:T(4,128)(2,1)S(1)} %pad_maximum_fusion.refs_0_), channel_id=1, source_target_pairs={{0,24},{8,16},{16,8},{24,0},{1,25},{9,17},{17,9},{25,1},{2,26},{10... | collective-permute-start | bytes 64520 | tf_op jit(solution)/shard_map/ppermute | solution.py:30
  14.2 0.5 %collective-permute-start.3 = (bf16[4,3,896]{2,1,0:T(4,128)(2,1)S(1)}, bf16[4,3,896]{2,1,0:T(4,128)(2,1)S(1)}, u32[]{:S(2)}, u32[]{:S(2)}) collective-permute-start(bf16[4,3,896]{2,1,0:T(4,128)(2,1)S(1)} %pad_maximum_fusion.refs_0_), channel_id=1, source_target_pairs={{0,16},{8,24},{16,0},{24,8},{1,17},{9,25},{17,1},{25,9},{2,18},{10... | collective-permute-start | bytes 64520 | tf_op jit(solution)/shard_map/ppermute | solution.py:30
  14.8 0.5 %collective-permute-start.4 = (bf16[4,3,896]{2,1,0:T(4,128)(2,1)S(1)}, bf16[4,3,896]{2,1,0:T(4,128)(2,1)S(1)}, u32[]{:S(2)}, u32[]{:S(2)}) collective-permute-start(bf16[4,3,896]{2,1,0:T(4,128)(2,1)S(1)} %pad_maximum_fusion.refs_0_), channel_id=1, source_target_pairs={{0,8},{8,0},{16,24},{24,16},{1,9},{9,1},{17,25},{25,17},{2,10},{10... | collective-permute-start | bytes 64520 | tf_op jit(solution)/shard_map/ppermute | solution.py:30
  15.3 1.4 %collective-permute-done.5.refs_3_ = bf16[4,3,896]{2,1,0:T(4,128)(2,1)S(1)} collective-permute-done((bf16[4,3,896]{2,1,0:T(4,128)(2,1)S(1)}, bf16[4,3,896]{2,1,0:T(4,128)(2,1)S(1)}, u32[]{:S(2)}, u32[]{:S(2)}) %collective-permute-start.5) | collective-permute-done | bytes 21536 | tf_op jit(solution)/shard_map/ppermute | solution.py:30
  16.7 1.3 %collective-permute-start.8 = (bf16[3,152,128]{2,1,0:T(8,128)(2,1)S(1)}, bf16[3,152,128]{2,1,0:T(8,128)(2,1)S(1)}, u32[]{:S(2)}, u32[]{:S(2)}) collective-permute-start(bf16[3,152,128]{2,1,0:T(8,128)(2,1)S(1)} %get-tuple-element.42), channel_id=1, source_target_pairs={{0,4},{1,5},{2,6},{3,7},{4,0},{5,1},{6,2},{7,3},{8,12},{9,13},{10,... | collective-permute-start | bytes 350216 | tf_op jit(solution)/shard_map/ppermute | solution.py:30
  18.0 0.1 collective-permute-done.3.refs_2_
  18.1 0.5 %collective-permute-done.4.refs_1_ = bf16[4,3,896]{2,1,0:T(4,128)(2,1)S(1)} collective-permute-done((bf16[4,3,896]{2,1,0:T(4,128)(2,1)S(1)}, bf16[4,3,896]{2,1,0:T(4,128)(2,1)S(1)}, u32[]{:S(2)}, u32[]{:S(2)}) %collective-permute-start.4) | collective-permute-done | bytes 21536 | tf_op jit(solution)/shard_map/ppermute | solution.py:30
  18.6 2.9 %shard_map.48 = (f32[12,4224]{1,0:T(8,128)S(1)}, f32[12,3584]{1,0:T(8,128)S(1)}, f32[6,4224]{1,0:T(8,128)S(1)}, f32[64,3584]{1,0:T(8,128)S(1)}) custom-call(bf16[3,304,128]{2,1,0:T(8,128)(2,1)S(1)} %get-tuple-element.35.tpl_ref, bf16[4,3,896]{2,1,0:T(4,128)(2,1)S(1)} %pad_maximum_fusion.refs_0_, bf16[4,3,896]{2,1,0:T(4,128)(2,1)S(1)} %collective-permute-done.4.refs_1_, ...), custom_call_target="tpu_custom_call" | custom-call | flops 1 | bytes 1 | tf_op jit(solution)/shard_map/pallas_call | solution.py:315
  21.6 0.1 collective-permute-start.6
  21.6 0.8 %collective-permute-done.10.tpl_ref = bf16[3,304,128]{2,1,0:T(8,128)(2,1)S(1)} collective-permute-done((bf16[3,304,128]{2,1,0:T(8,128)(2,1)S(1)}, bf16[3,304,128]{2,1,0:T(8,128)(2,1)S(1)}, u32[]{:S(2)}, u32[]{:S(2)}) %collective-permute-start.10) | collective-permute-done | bytes 233504 | tf_op jit(solution)/shard_map/ppermute | solution.py:30
  22.5 2.1 %shard_map.49.acc_ref = f32[64,3584]{1,0:T(8,128)S(1)} custom-call(bf16[3,304,128]{2,1,0:T(8,128)(2,1)S(1)} %collective-permute-done.10.tpl_ref, f32[12,4224]{1,0:T(8,128)S(1)} %get-tuple-element.43.ext_ref, f32[12,3584]{1,0:T(8,128)S(1)} %get-tuple-element.44.inv_ref, f32[64,3584]{1,0:T(8,128)S(1)} %get-tuple-element.47.acc_ref), custom_call_target="tpu_custom_call" | custom-call | flops 500000000 | bytes 1 | tf_op jit(solution)/shard_map/pallas_call | solution.py:334
  24.5 0.0 collective-permute-done.9.tpl_ref
  24.6 2.1 %shard_map.50 = (f32[32,3584]{1,0:T(8,128)S(1)}, bf16[32,1792]{1,0:T(8,128)(2,1)S(1)}, bf16[32,1792]{1,0:T(8,128)(2,1)S(1)}) custom-call(bf16[3,304,128]{2,1,0:T(8,128)(2,1)S(1)} %collective-permute-done.9.tpl_ref, f32[12,4224]{1,0:T(8,128)S(1)} %get-tuple-element.43.ext_ref, f32[12,3584]{1,0:T(8,128)S(1)} %get-tuple-element.44.inv_ref, ...), custom_call_target="tpu_custom_call" | custom-call | flops 1 | bytes 1 | tf_op jit(solution)/shard_map/pallas_call | solution.py:334
  26.6 0.8 %collective-permute-start.11 = (bf16[32,1792]{1,0:T(8,128)(2,1)S(1)}, bf16[32,1792]{1,0:T(8,128)(2,1)S(1)}, u32[]{:S(2)}, u32[]{:S(2)}) collective-permute-start(bf16[32,1792]{1,0:T(8,128)(2,1)S(1)} %get-tuple-element.49), channel_id=1, source_target_pairs={{0,1},{1,0},{2,3},{3,2},{4,5},{5,4},{6,7},{7,6},{8,9},{9,8},{10,11... | collective-permute-start | bytes 344072 | tf_op jit(solution)/shard_map/ppermute | solution.py:30
  27.4 0.1 collective-permute-start.12
  27.5 0.4 %collective-permute-start.7 = (f32[6,4224]{1,0:T(8,128)S(1)}, f32[6,4224]{1,0:T(8,128)S(1)}, u32[]{:S(2)}, u32[]{:S(2)}) collective-permute-start(f32[6,4224]{1,0:T(8,128)S(1)} %get-tuple-element.41), channel_id=1, source_target_pairs={{0,1},{1,0},{2,3},{3,2},{4,5},{5,4},{6,7},{7,6},{8,9},{9,8},{10,11... | collective-permute-start | bytes 304136 | tf_op jit(solution)/shard_map/ppermute | solution.py:30
  27.9 0.0 collective-permute-done.8.tpl_ref
  27.9 1.9 %shard_map.51.acc_ref = f32[32,3584]{1,0:T(8,128)S(1)} custom-call(bf16[3,152,128]{2,1,0:T(8,128)(2,1)S(1)} %collective-permute-done.8.tpl_ref, f32[12,4224]{1,0:T(8,128)S(1)} %get-tuple-element.43.ext_ref, f32[12,3584]{1,0:T(8,128)S(1)} %get-tuple-element.44.inv_ref, f32[32,3584]{1,0:T(8,128)S(1)} %get-tuple-element.48.acc_ref), custom_call_target="tpu_custom_call" | custom-call | flops 500000000 | bytes 1 | tf_op jit(solution)/shard_map/pallas_call | solution.py:334
  29.8 0.0 collective-permute-done.7.cross_ref
  29.8 0.8 %collective-permute-done.6.tpl_ref = bf16[3,152,128]{2,1,0:T(8,128)(2,1)S(1)} collective-permute-done((bf16[3,152,128]{2,1,0:T(8,128)(2,1)S(1)}, bf16[3,152,128]{2,1,0:T(8,128)(2,1)S(1)}, u32[]{:S(2)}, u32[]{:S(2)}) %collective-permute-start.6) | collective-permute-done | bytes 116768 | tf_op jit(solution)/shard_map/ppermute | solution.py:30
  30.6 0.0 collective-permute-done.11.early_ref
  30.6 0.0 collective-permute-done.12.late_ref
  30.6 2.0 %shard_map.52 = (f32[32,896]{1,0:T(8,128)S(1)}, bf16[32,896]{1,0:T(8,128)(2,1)S(1)}, bf16[32,896]{1,0:T(8,128)(2,1)S(1)}, bf16[32,1024]{1,0:T(8,128)(2,1)S(1)}) custom-call(bf16[3,152,128]{2,1,0:T(8,128)(2,1)S(1)} %collective-permute-done.6.tpl_ref, f32[6,4224]{1,0:T(8,128)S(1)} %collective-permute-done.7.cross_ref, f32[32,3584]{1,0:T(8,128)S(1)} %shard_map.51.acc_ref, ...), custom_call_target="tpu_custom_call" | custom-call | flops 1 | bytes 1 | tf_op jit(solution)/shard_map/pallas_call | solution.py:334
  32.6 2.8 %collective-permute-start.15 = (bf16[32,1024]{1,0:T(8,128)(2,1)S(1)}, bf16[32,1024]{1,0:T(8,128)(2,1)S(1)}, u32[]{:S(2)}, u32[]{:S(2)}) collective-permute-start(bf16[32,1024]{1,0:T(8,128)(2,1)S(1)} %get-tuple-element.54), channel_id=1, source_target_pairs={{0,24},{8,16},{16,8},{24,0},{1,25},{9,17},{17,9},{25,1},{2,26},{10... | collective-permute-start | bytes 196616 | tf_op jit(solution)/shard_map/ppermute | solution.py:30
  35.4 0.3 collective-permute-start.13
  35.6 0.5 %collective-permute-start.14 = (bf16[32,896]{1,0:T(8,128)(2,1)S(1)}, bf16[32,896]{1,0:T(8,128)(2,1)S(1)}, u32[]{:S(2)}, u32[]{:S(2)}) collective-permute-start(bf16[32,896]{1,0:T(8,128)(2,1)S(1)} %get-tuple-element.53), channel_id=1, source_target_pairs={{0,16},{8,24},{16,0},{24,8},{1,17},{9,25},{17,1},{25,9},{2,18},{10... | collective-permute-start | bytes 172040 | tf_op jit(solution)/shard_map/ppermute | solution.py:30
  36.1 3.4 %collective-permute-done.13.refs_1_ = bf16[32,896]{1,0:T(8,128)(2,1)S(1)} collective-permute-done((bf16[32,896]{1,0:T(8,128)(2,1)S(1)}, bf16[32,896]{1,0:T(8,128)(2,1)S(1)}, u32[]{:S(2)}, u32[]{:S(2)}) %collective-permute-start.13) | collective-permute-done | bytes 57376 | tf_op jit(solution)/shard_map/ppermute | solution.py:30
  39.5 0.3 collective-permute-done.14.refs_2_
  39.8 0.0 collective-permute-done.15.refs_3_
  39.8 0.8 %shard_map.53 = f32[4,32,896]{2,1,0:T(8,128)} custom-call(f32[32,896]{1,0:T(8,128)S(1)} %get-tuple-element.51.refs_0_, bf16[32,896]{1,0:T(8,128)(2,1)S(1)} %collective-permute-done.13.refs_1_, bf16[32,896]{1,0:T(8,128)(2,1)S(1)} %collective-permute-done.14.refs_2_, bf16[32,1024]{1,0:T(8,128)(2,1)S(1)} %collective-permute-done.15.refs_3_), custom_call_target="tpu_custom_call" | custom-call | tf_op jit(solution)/shard_map/pallas_call | solution.py:361
  (5 shorter events, 0.1 us)
Async XLA Ops:
  1.3 10.4 %collective-permute-start.2 = (bf16[3,1536]{1,0:T(4,128)(2,1)S(1)}, bf16[3,1536]{1,0:T(4,128)(2,1)S(1)}, u32[]{:S(2)}, u32[]{:S(2)}) collective-permute-start(bf16[3,1536]{1,0:T(4,128)(2,1)S(1)} %get-tuple-element.33.refs_4_), channel_id=1, source_target_pairs={{0,6},{1,7},{2,4},{3,5},{4,2},{5,3},{6,0},{7,1},{8,14},{9,15},{10,... | collective-permute-start | bytes 27656 | tf_op jit(solution)/shard_map/ppermute | solution.py:30
  6.4 5.3 %collective-permute-start.1 = (bf16[3,1536]{1,0:T(4,128)(2,1)S(1)}, bf16[3,1536]{1,0:T(4,128)(2,1)S(1)}, u32[]{:S(2)}, u32[]{:S(2)}) collective-permute-start(bf16[3,1536]{1,0:T(4,128)(2,1)S(1)} %get-tuple-element.33.refs_4_), channel_id=1, source_target_pairs={{0,4},{1,5},{2,6},{3,7},{4,0},{5,1},{6,2},{7,3},{8,12},{9,13},{10,... | collective-permute-start | bytes 27656 | tf_op jit(solution)/shard_map/ppermute | solution.py:30
  6.4 5.3 %collective-permute-start = (bf16[3,1536]{1,0:T(4,128)(2,1)S(1)}, bf16[3,1536]{1,0:T(4,128)(2,1)S(1)}, u32[]{:S(2)}, u32[]{:S(2)}) collective-permute-start(bf16[3,1536]{1,0:T(4,128)(2,1)S(1)} %get-tuple-element.33.refs_4_), channel_id=1, source_target_pairs={{0,2},{1,3},{2,0},{3,1},{4,6},{5,7},{6,4},{7,5},{8,10},{9,11},{10,... | collective-permute-start | bytes 27656 | tf_op jit(solution)/shard_map/ppermute | solution.py:30
  7.8 16.8 %collective-permute-start.9 = (bf16[3,304,128]{2,1,0:T(8,128)(2,1)S(1)}, bf16[3,304,128]{2,1,0:T(8,128)(2,1)S(1)}, u32[]{:S(2)}, u32[]{:S(2)}) collective-permute-start(bf16[3,304,128]{2,1,0:T(8,128)(2,1)S(1)} %get-tuple-element.45), channel_id=1, source_target_pairs={{0,6},{1,7},{2,4},{3,5},{4,2},{5,3},{6,0},{7,1},{8,14},{9,15},{10,... | collective-permute-start | bytes 700424 | tf_op jit(solution)/shard_map/ppermute | solution.py:30
  11.6 10.9 %collective-permute-start.10 = (bf16[3,304,128]{2,1,0:T(8,128)(2,1)S(1)}, bf16[3,304,128]{2,1,0:T(8,128)(2,1)S(1)}, u32[]{:S(2)}, u32[]{:S(2)}) collective-permute-start(bf16[3,304,128]{2,1,0:T(8,128)(2,1)S(1)} %get-tuple-element.46), channel_id=1, source_target_pairs={{0,2},{1,3},{2,0},{3,1},{4,6},{5,7},{6,4},{7,5},{8,10},{9,11},{10,... | collective-permute-start | bytes 700424 | tf_op jit(solution)/shard_map/ppermute | solution.py:30
  11.7 5.0 %collective-permute-start.5 = (bf16[4,3,896]{2,1,0:T(4,128)(2,1)S(1)}, bf16[4,3,896]{2,1,0:T(4,128)(2,1)S(1)}, u32[]{:S(2)}, u32[]{:S(2)}) collective-permute-start(bf16[4,3,896]{2,1,0:T(4,128)(2,1)S(1)} %pad_maximum_fusion.refs_0_), channel_id=1, source_target_pairs={{0,24},{8,16},{16,8},{24,0},{1,25},{9,17},{17,9},{25,1},{2,26},{10... | collective-permute-start | bytes 64520 | tf_op jit(solution)/shard_map/ppermute | solution.py:30
  14.2 3.9 %collective-permute-start.3 = (bf16[4,3,896]{2,1,0:T(4,128)(2,1)S(1)}, bf16[4,3,896]{2,1,0:T(4,128)(2,1)S(1)}, u32[]{:S(2)}, u32[]{:S(2)}) collective-permute-start(bf16[4,3,896]{2,1,0:T(4,128)(2,1)S(1)} %pad_maximum_fusion.refs_0_), channel_id=1, source_target_pairs={{0,16},{8,24},{16,0},{24,8},{1,17},{9,25},{17,1},{25,9},{2,18},{10... | collective-permute-start | bytes 64520 | tf_op jit(solution)/shard_map/ppermute | solution.py:30
  14.8 3.9 %collective-permute-start.4 = (bf16[4,3,896]{2,1,0:T(4,128)(2,1)S(1)}, bf16[4,3,896]{2,1,0:T(4,128)(2,1)S(1)}, u32[]{:S(2)}, u32[]{:S(2)}) collective-permute-start(bf16[4,3,896]{2,1,0:T(4,128)(2,1)S(1)} %pad_maximum_fusion.refs_0_), channel_id=1, source_target_pairs={{0,8},{8,0},{16,24},{24,16},{1,9},{9,1},{17,25},{25,17},{2,10},{10... | collective-permute-start | bytes 64520 | tf_op jit(solution)/shard_map/ppermute | solution.py:30
  16.7 11.2 %collective-permute-start.8 = (bf16[3,152,128]{2,1,0:T(8,128)(2,1)S(1)}, bf16[3,152,128]{2,1,0:T(8,128)(2,1)S(1)}, u32[]{:S(2)}, u32[]{:S(2)}) collective-permute-start(bf16[3,152,128]{2,1,0:T(8,128)(2,1)S(1)} %get-tuple-element.42), channel_id=1, source_target_pairs={{0,4},{1,5},{2,6},{3,7},{4,0},{5,1},{6,2},{7,3},{8,12},{9,13},{10,... | collective-permute-start | bytes 350216 | tf_op jit(solution)/shard_map/ppermute | solution.py:30
  21.6 9.0 %collective-permute-start.6 = (bf16[3,152,128]{2,1,0:T(8,128)(2,1)S(1)}, bf16[3,152,128]{2,1,0:T(8,128)(2,1)S(1)}, u32[]{:S(2)}, u32[]{:S(2)}) collective-permute-start(bf16[3,152,128]{2,1,0:T(8,128)(2,1)S(1)} %get-tuple-element.40), channel_id=1, source_target_pairs={{0,5},{1,4},{2,7},{3,6},{4,1},{5,0},{6,3},{7,2},{8,13},{9,12},{10,... | collective-permute-start | bytes 350216 | tf_op jit(solution)/shard_map/ppermute | solution.py:30
  26.6 4.0 %collective-permute-start.11 = (bf16[32,1792]{1,0:T(8,128)(2,1)S(1)}, bf16[32,1792]{1,0:T(8,128)(2,1)S(1)}, u32[]{:S(2)}, u32[]{:S(2)}) collective-permute-start(bf16[32,1792]{1,0:T(8,128)(2,1)S(1)} %get-tuple-element.49), channel_id=1, source_target_pairs={{0,1},{1,0},{2,3},{3,2},{4,5},{5,4},{6,7},{7,6},{8,9},{9,8},{10,11... | collective-permute-start | bytes 344072 | tf_op jit(solution)/shard_map/ppermute | solution.py:30
  27.4 3.2 %collective-permute-start.12 = (bf16[32,1792]{1,0:T(8,128)(2,1)S(1)}, bf16[32,1792]{1,0:T(8,128)(2,1)S(1)}, u32[]{:S(2)}, u32[]{:S(2)}) collective-permute-start(bf16[32,1792]{1,0:T(8,128)(2,1)S(1)} %get-tuple-element.50), channel_id=1, source_target_pairs={{0,1},{1,0},{2,3},{3,2},{4,5},{5,4},{6,7},{7,6},{8,9},{9,8},{10,11... | collective-permute-start | bytes 344072 | tf_op jit(solution)/shard_map/ppermute | solution.py:30
  27.5 2.3 %collective-permute-start.7 = (f32[6,4224]{1,0:T(8,128)S(1)}, f32[6,4224]{1,0:T(8,128)S(1)}, u32[]{:S(2)}, u32[]{:S(2)}) collective-permute-start(f32[6,4224]{1,0:T(8,128)S(1)} %get-tuple-element.41), channel_id=1, source_target_pairs={{0,1},{1,0},{2,3},{3,2},{4,5},{5,4},{6,7},{7,6},{8,9},{9,8},{10,11... | collective-permute-start | bytes 304136 | tf_op jit(solution)/shard_map/ppermute | solution.py:30
  32.6 7.2 %collective-permute-start.15 = (bf16[32,1024]{1,0:T(8,128)(2,1)S(1)}, bf16[32,1024]{1,0:T(8,128)(2,1)S(1)}, u32[]{:S(2)}, u32[]{:S(2)}) collective-permute-start(bf16[32,1024]{1,0:T(8,128)(2,1)S(1)} %get-tuple-element.54), channel_id=1, source_target_pairs={{0,24},{8,16},{16,8},{24,0},{1,25},{9,17},{17,9},{25,1},{2,26},{10... | collective-permute-start | bytes 196616 | tf_op jit(solution)/shard_map/ppermute | solution.py:30
  35.4 4.2 %collective-permute-start.13 = (bf16[32,896]{1,0:T(8,128)(2,1)S(1)}, bf16[32,896]{1,0:T(8,128)(2,1)S(1)}, u32[]{:S(2)}, u32[]{:S(2)}) collective-permute-start(bf16[32,896]{1,0:T(8,128)(2,1)S(1)} %get-tuple-element.52), channel_id=1, source_target_pairs={{0,8},{8,0},{16,24},{24,16},{1,9},{9,1},{17,25},{25,17},{2,10},{10... | collective-permute-start | bytes 172040 | tf_op jit(solution)/shard_map/ppermute | solution.py:30
  35.6 4.2 %collective-permute-start.14 = (bf16[32,896]{1,0:T(8,128)(2,1)S(1)}, bf16[32,896]{1,0:T(8,128)(2,1)S(1)}, u32[]{:S(2)}, u32[]{:S(2)}) collective-permute-start(bf16[32,896]{1,0:T(8,128)(2,1)S(1)} %get-tuple-element.53), channel_id=1, source_target_pairs={{0,16},{8,24},{16,0},{24,8},{1,17},{9,25},{17,1},{25,9},{2,18},{10... | collective-permute-start | bytes 172040 | tf_op jit(solution)/shard_map/ppermute | solution.py:30

commit v7 on v6

--- a/solution.py
+++ b/solution.py
@@ -31,7 +31,8 @@
 
 
 def join_kernel(wave_ref, tail_ref, tpl_ref, mask_ref, out_ref, tpl_out, mask_out, wave_held, tail_held, arrived):
-    pairs = ((wave_ref, wave_held), (tail_ref, tail_held), (mask_ref, mask_out), (tpl_ref, tpl_out))
+    pairs = [(wave_ref, wave_held), (tail_ref, tail_held), (mask_ref, mask_out)]
+    pairs += [(tpl_ref.at[comp], tpl_out.at[comp]) for comp in range(tpl_ref.shape[0])]
     copies = [pltpu.make_async_copy(source, held, arrived.at[i]) for i, (source, held) in enumerate(pairs)]
     for copy in copies:
         copy.start()
@@ -41,8 +42,8 @@
     out_ref[...] = jnp.zeros_like(out_ref)
     out_ref[:, :samples] = wave_held[...]
     out_ref[:, samples : samples + tail_held.shape[-1]] = tail_held[...]
-    copies[2].wait()
-    copies[3].wait()
+    for copy in copies[2:]:
+        copy.wait()
 
 
 def join(wave, tail, tpl, mask):
@@ -56,7 +57,7 @@
         ],
         in_specs=[HBM] * 4,
         out_specs=[VMEM] * 3,
-        scratch_shapes=[pltpu.VMEM(x.shape, x.dtype) for x in (wave, tail)] + [pltpu.SemaphoreType.DMA((4,))],
+        scratch_shapes=[pltpu.VMEM(x.shape, x.dtype) for x in (wave, tail)] + [pltpu.SemaphoreType.DMA((3 + tpl.shape[0],))],
         compiler_params=params(16),
         cost_estimate=CHEAP,
     )(*[pltpu.with_memory_space_constraint(x, pltpu.HBM) for x in inputs])

time: 40.8 us -> 40.8 us (level)
  no operation moved by 1% of the time
where the time goes in v7:
time: 40.8 us; the launch traced here: 40.6 us
  starting transfers between devices  19.3 us (47%)
  Pallas kernels  13.7 us (34%)
  waiting for transfers between devices  7.33 us (18%)
    ppermute x16, starting transfers between devices, swap_with(): return lax.ppermute(x, axis, [(i, i ^ offset) for i in range(size)])  19.3 us
    pallas_call x4, Pallas kernels, later(): pl.pallas_call(kernel, out_shape=out_shape, in_specs=[VMEM] * len(inputs)...  8 us
    ppermute x16, waiting for transfers between devices, swap_with(): return lax.ppermute(x, axis, [(i, i ^ offset) for i in range(size)])  7.33 us
    pallas_call x1, Pallas kernels, first(): pl.pallas_call(functools.partial(first_kernel, len(shards), chips, rows,...  2.92 us
    pallas_call x1, Pallas kernels, join(): pl.pallas_call(join_kernel, out_shape=[jax.ShapeDtypeStruct((wave.shape[0...  1.25 us
  transfers between devices with their start and end apart: 16, of which 7 were waited for; matrix products, arithmetic and copies ran while one was open for 0% of the time, Pallas kernels for 24%

profile of v7, /device:TPU:0, one launch (start us, length us, event | category | flops | bytes accessed | tf_op | source)
XLA Modules:
  0.0 40.6 jit_solution(412491884103043347)
XLA Ops:
  0.0 1.2 %shard_map.46 = (bf16[3,1536]{1,0:T(4,128)(2,1)S(1)}, bf16[3,600,256]{2,1,0:T(8,128)(2,1)S(1)}, s32[1,256]{1,0:T(1,128)S(1)}) custom-call(bf16[3,896]{1,0:T(4,128)(2,1)} %bitcast.15, bf16[3,599]{1,0:T(4,128)(2,1)} %bitcast.16, bf16[3,600,256]{2,1,0:T(8,128)(2,1)} %bitcast.14, s32[1,256]{1,0:T(1,128)} %bitcast.17), custom_call_target="tpu_custom_call" | custom-call | flops 1 | bytes 1 | tf_op jit(solution)/shard_map/pallas_call | solution.py:51
  1.3 5.1 %collective-permute-start.2 = (bf16[3,1536]{1,0:T(4,128)(2,1)S(1)}, bf16[3,1536]{1,0:T(4,128)(2,1)S(1)}, u32[]{:S(2)}, u32[]{:S(2)}) collective-permute-start(bf16[3,1536]{1,0:T(4,128)(2,1)S(1)} %get-tuple-element.33.refs_4_), channel_id=1, source_target_pairs={{0,6},{1,7},{2,4},{3,5},{4,2},{5,3},{6,0},{7,1},{8,14},{9,15},{10,... | collective-permute-start | bytes 27656 | tf_op jit(solution)/shard_map/ppermute | solution.py:30
  6.4 0.0 collective-permute-start.1
  6.4 0.6 %collective-permute-start = (bf16[3,1536]{1,0:T(4,128)(2,1)S(1)}, bf16[3,1536]{1,0:T(4,128)(2,1)S(1)}, u32[]{:S(2)}, u32[]{:S(2)}) collective-permute-start(bf16[3,1536]{1,0:T(4,128)(2,1)S(1)} %get-tuple-element.33.refs_4_), channel_id=1, source_target_pairs={{0,2},{1,3},{2,0},{3,1},{4,6},{5,7},{6,4},{7,5},{8,10},{9,11},{10,... | collective-permute-start | bytes 27656 | tf_op jit(solution)/shard_map/ppermute | solution.py:30
  7.0 0.8 %shard_map.47 = (bf16[3,304,128]{2,1,0:T(8,128)(2,1)S(1)}, bf16[3,304,128]{2,1,0:T(8,128)(2,1)S(1)}, bf16[3,304,128]{2,1,0:T(8,128)(2,1)S(1)}, bf16[3,152,128]{2,1,0:T(8,128)(2,1)S(1)}, bf16[3,152,128]{2,1,0:T(8,128)(2,1)S(1)}) custom-call(bf16[3,600,256]{2,1,0:T(8,128)(2,1)S(1)} %get-tuple-element.30.tpl_ref, s32[1,256]{1,0:T(1,128)S(1)} %get-tuple-element.31.mask_ref), custom_call_target="tpu_custom_call" | custom-call | flops 1 | bytes 1 | tf_op jit(solution)/shard_map/pallas_call | solution.py:101
  7.8 3.8 %collective-permute-start.9 = (bf16[3,304,128]{2,1,0:T(8,128)(2,1)S(1)}, bf16[3,304,128]{2,1,0:T(8,128)(2,1)S(1)}, u32[]{:S(2)}, u32[]{:S(2)}) collective-permute-start(bf16[3,304,128]{2,1,0:T(8,128)(2,1)S(1)} %get-tuple-element.45), channel_id=1, source_target_pairs={{0,6},{1,7},{2,4},{3,5},{4,2},{5,3},{6,0},{7,1},{8,14},{9,15},{10,... | collective-permute-start | bytes 700424 | tf_op jit(solution)/shard_map/ppermute | solution.py:30
  11.6 0.0 collective-permute-start.10
  11.6 0.0 collective-permute-done.2.refs_7_
  11.6 0.0 collective-permute-done.1.refs_6_
  11.7 0.0 collective-permute-done.refs_5_
  11.7 2.5 %collective-permute-start.5 = (bf16[4,3,896]{2,1,0:T(4,128)(2,1)S(1)}, bf16[4,3,896]{2,1,0:T(4,128)(2,1)S(1)}, u32[]{:S(2)}, u32[]{:S(2)}) collective-permute-start(bf16[4,3,896]{2,1,0:T(4,128)(2,1)S(1)} %pad_maximum_fusion.refs_0_), channel_id=1, source_target_pairs={{0,24},{8,16},{16,8},{24,0},{1,25},{9,17},{17,9},{25,1},{2,26},{10... | collective-permute-start | bytes 64520 | tf_op jit(solution)/shard_map/ppermute | solution.py:30
  14.2 0.5 %collective-permute-start.3 = (bf16[4,3,896]{2,1,0:T(4,128)(2,1)S(1)}, bf16[4,3,896]{2,1,0:T(4,128)(2,1)S(1)}, u32[]{:S(2)}, u32[]{:S(2)}) collective-permute-start(bf16[4,3,896]{2,1,0:T(4,128)(2,1)S(1)} %pad_maximum_fusion.refs_0_), channel_id=1, source_target_pairs={{0,16},{8,24},{16,0},{24,8},{1,17},{9,25},{17,1},{25,9},{2,18},{10... | collective-permute-start | bytes 64520 | tf_op jit(solution)/shard_map/ppermute | solution.py:30
  14.7 0.5 %collective-permute-start.4 = (bf16[4,3,896]{2,1,0:T(4,128)(2,1)S(1)}, bf16[4,3,896]{2,1,0:T(4,128)(2,1)S(1)}, u32[]{:S(2)}, u32[]{:S(2)}) collective-permute-start(bf16[4,3,896]{2,1,0:T(4,128)(2,1)S(1)} %pad_maximum_fusion.refs_0_), channel_id=1, source_target_pairs={{0,8},{8,0},{16,24},{24,16},{1,9},{9,1},{17,25},{25,17},{2,10},{10... | collective-permute-start | bytes 64520 | tf_op jit(solution)/shard_map/ppermute | solution.py:30
  15.3 1.4 %collective-permute-done.5.refs_3_ = bf16[4,3,896]{2,1,0:T(4,128)(2,1)S(1)} collective-permute-done((bf16[4,3,896]{2,1,0:T(4,128)(2,1)S(1)}, bf16[4,3,896]{2,1,0:T(4,128)(2,1)S(1)}, u32[]{:S(2)}, u32[]{:S(2)}) %collective-permute-start.5) | collective-permute-done | bytes 21536 | tf_op jit(solution)/shard_map/ppermute | solution.py:30
  16.7 1.3 %collective-permute-start.8 = (bf16[3,152,128]{2,1,0:T(8,128)(2,1)S(1)}, bf16[3,152,128]{2,1,0:T(8,128)(2,1)S(1)}, u32[]{:S(2)}, u32[]{:S(2)}) collective-permute-start(bf16[3,152,128]{2,1,0:T(8,128)(2,1)S(1)} %get-tuple-element.42), channel_id=1, source_target_pairs={{0,4},{1,5},{2,6},{3,7},{4,0},{5,1},{6,2},{7,3},{8,12},{9,13},{10,... | collective-permute-start | bytes 350216 | tf_op jit(solution)/shard_map/ppermute | solution.py:30
  18.0 0.1 collective-permute-done.3.refs_2_
  18.1 0.5 %collective-permute-done.4.refs_1_ = bf16[4,3,896]{2,1,0:T(4,128)(2,1)S(1)} collective-permute-done((bf16[4,3,896]{2,1,0:T(4,128)(2,1)S(1)}, bf16[4,3,896]{2,1,0:T(4,128)(2,1)S(1)}, u32[]{:S(2)}, u32[]{:S(2)}) %collective-permute-start.4) | collective-permute-done | bytes 21536 | tf_op jit(solution)/shard_map/ppermute | solution.py:30
  18.6 2.9 %shard_map.48 = (f32[12,4224]{1,0:T(8,128)S(1)}, f32[12,3584]{1,0:T(8,128)S(1)}, f32[6,4224]{1,0:T(8,128)S(1)}, f32[64,3584]{1,0:T(8,128)S(1)}) custom-call(bf16[3,304,128]{2,1,0:T(8,128)(2,1)S(1)} %get-tuple-element.35.tpl_ref, bf16[4,3,896]{2,1,0:T(4,128)(2,1)S(1)} %pad_maximum_fusion.refs_0_, bf16[4,3,896]{2,1,0:T(4,128)(2,1)S(1)} %collective-permute-done.4.refs_1_, ...), custom_call_target="tpu_custom_call" | custom-call | flops 1 | bytes 1 | tf_op jit(solution)/shard_map/pallas_call | solution.py:316
  21.5 0.1 collective-permute-start.6
  21.6 0.8 %collective-permute-done.10.tpl_ref = bf16[3,304,128]{2,1,0:T(8,128)(2,1)S(1)} collective-permute-done((bf16[3,304,128]{2,1,0:T(8,128)(2,1)S(1)}, bf16[3,304,128]{2,1,0:T(8,128)(2,1)S(1)}, u32[]{:S(2)}, u32[]{:S(2)}) %collective-permute-start.10) | collective-permute-done | bytes 233504 | tf_op jit(solution)/shard_map/ppermute | solution.py:30
  22.5 2.1 %shard_map.49.acc_ref = f32[64,3584]{1,0:T(8,128)S(1)} custom-call(bf16[3,304,128]{2,1,0:T(8,128)(2,1)S(1)} %collective-permute-done.10.tpl_ref, f32[12,4224]{1,0:T(8,128)S(1)} %get-tuple-element.43.ext_ref, f32[12,3584]{1,0:T(8,128)S(1)} %get-tuple-element.44.inv_ref, f32[64,3584]{1,0:T(8,128)S(1)} %get-tuple-element.47.acc_ref), custom_call_target="tpu_custom_call" | custom-call | flops 500000000 | bytes 1 | tf_op jit(solution)/shard_map/pallas_call | solution.py:335
  24.5 0.0 collective-permute-done.9.tpl_ref
  24.5 2.1 %shard_map.50 = (f32[32,3584]{1,0:T(8,128)S(1)}, bf16[32,1792]{1,0:T(8,128)(2,1)S(1)}, bf16[32,1792]{1,0:T(8,128)(2,1)S(1)}) custom-call(bf16[3,304,128]{2,1,0:T(8,128)(2,1)S(1)} %collective-permute-done.9.tpl_ref, f32[12,4224]{1,0:T(8,128)S(1)} %get-tuple-element.43.ext_ref, f32[12,3584]{1,0:T(8,128)S(1)} %get-tuple-element.44.inv_ref, ...), custom_call_target="tpu_custom_call" | custom-call | flops 1 | bytes 1 | tf_op jit(solution)/shard_map/pallas_call | solution.py:335
  26.6 0.8 %collective-permute-start.11 = (bf16[32,1792]{1,0:T(8,128)(2,1)S(1)}, bf16[32,1792]{1,0:T(8,128)(2,1)S(1)}, u32[]{:S(2)}, u32[]{:S(2)}) collective-permute-start(bf16[32,1792]{1,0:T(8,128)(2,1)S(1)} %get-tuple-element.49), channel_id=1, source_target_pairs={{0,1},{1,0},{2,3},{3,2},{4,5},{5,4},{6,7},{7,6},{8,9},{9,8},{10,11... | collective-permute-start | bytes 344072 | tf_op jit(solution)/shard_map/ppermute | solution.py:30
  27.4 0.1 collective-permute-start.12
  27.5 0.4 %collective-permute-start.7 = (f32[6,4224]{1,0:T(8,128)S(1)}, f32[6,4224]{1,0:T(8,128)S(1)}, u32[]{:S(2)}, u32[]{:S(2)}) collective-permute-start(f32[6,4224]{1,0:T(8,128)S(1)} %get-tuple-element.41), channel_id=1, source_target_pairs={{0,1},{1,0},{2,3},{3,2},{4,5},{5,4},{6,7},{7,6},{8,9},{9,8},{10,11... | collective-permute-start | bytes 304136 | tf_op jit(solution)/shard_map/ppermute | solution.py:30
  27.9 0.0 collective-permute-done.8.tpl_ref
  27.9 1.9 %shard_map.51.acc_ref = f32[32,3584]{1,0:T(8,128)S(1)} custom-call(bf16[3,152,128]{2,1,0:T(8,128)(2,1)S(1)} %collective-permute-done.8.tpl_ref, f32[12,4224]{1,0:T(8,128)S(1)} %get-tuple-element.43.ext_ref, f32[12,3584]{1,0:T(8,128)S(1)} %get-tuple-element.44.inv_ref, f32[32,3584]{1,0:T(8,128)S(1)} %get-tuple-element.48.acc_ref), custom_call_target="tpu_custom_call" | custom-call | flops 500000000 | bytes 1 | tf_op jit(solution)/shard_map/pallas_call | solution.py:335
  29.8 0.0 collective-permute-done.7.cross_ref
  29.8 0.8 %collective-permute-done.6.tpl_ref = bf16[3,152,128]{2,1,0:T(8,128)(2,1)S(1)} collective-permute-done((bf16[3,152,128]{2,1,0:T(8,128)(2,1)S(1)}, bf16[3,152,128]{2,1,0:T(8,128)(2,1)S(1)}, u32[]{:S(2)}, u32[]{:S(2)}) %collective-permute-start.6) | collective-permute-done | bytes 116768 | tf_op jit(solution)/shard_map/ppermute | solution.py:30
  30.6 0.0 collective-permute-done.11.early_ref
  30.6 0.0 collective-permute-done.12.late_ref
  30.6 2.0 %shard_map.52 = (f32[32,896]{1,0:T(8,128)S(1)}, bf16[32,896]{1,0:T(8,128)(2,1)S(1)}, bf16[32,896]{1,0:T(8,128)(2,1)S(1)}, bf16[32,1024]{1,0:T(8,128)(2,1)S(1)}) custom-call(bf16[3,152,128]{2,1,0:T(8,128)(2,1)S(1)} %collective-permute-done.6.tpl_ref, f32[6,4224]{1,0:T(8,128)S(1)} %collective-permute-done.7.cross_ref, f32[32,3584]{1,0:T(8,128)S(1)} %shard_map.51.acc_ref, ...), custom_call_target="tpu_custom_call" | custom-call | flops 1 | bytes 1 | tf_op jit(solution)/shard_map/pallas_call | solution.py:335
  32.6 2.8 %collective-permute-start.15 = (bf16[32,1024]{1,0:T(8,128)(2,1)S(1)}, bf16[32,1024]{1,0:T(8,128)(2,1)S(1)}, u32[]{:S(2)}, u32[]{:S(2)}) collective-permute-start(bf16[32,1024]{1,0:T(8,128)(2,1)S(1)} %get-tuple-element.54), channel_id=1, source_target_pairs={{0,24},{8,16},{16,8},{24,0},{1,25},{9,17},{17,9},{25,1},{2,26},{10... | collective-permute-start | bytes 196616 | tf_op jit(solution)/shard_map/ppermute | solution.py:30
  35.3 0.3 collective-permute-start.13
  35.6 0.5 %collective-permute-start.14 = (bf16[32,896]{1,0:T(8,128)(2,1)S(1)}, bf16[32,896]{1,0:T(8,128)(2,1)S(1)}, u32[]{:S(2)}, u32[]{:S(2)}) collective-permute-start(bf16[32,896]{1,0:T(8,128)(2,1)S(1)} %get-tuple-element.53), channel_id=1, source_target_pairs={{0,16},{8,24},{16,0},{24,8},{1,17},{9,25},{17,1},{25,9},{2,18},{10... | collective-permute-start | bytes 172040 | tf_op jit(solution)/shard_map/ppermute | solution.py:30
  36.1 3.4 %collective-permute-done.13.refs_1_ = bf16[32,896]{1,0:T(8,128)(2,1)S(1)} collective-permute-done((bf16[32,896]{1,0:T(8,128)(2,1)S(1)}, bf16[32,896]{1,0:T(8,128)(2,1)S(1)}, u32[]{:S(2)}, u32[]{:S(2)}) %collective-permute-start.13) | collective-permute-done | bytes 57376 | tf_op jit(solution)/shard_map/ppermute | solution.py:30
  39.5 0.3 collective-permute-done.14.refs_2_
  39.8 0.0 collective-permute-done.15.refs_3_
  39.8 0.8 %shard_map.53 = f32[4,32,896]{2,1,0:T(8,128)} custom-call(f32[32,896]{1,0:T(8,128)S(1)} %get-tuple-element.51.refs_0_, bf16[32,896]{1,0:T(8,128)(2,1)S(1)} %collective-permute-done.13.refs_1_, bf16[32,896]{1,0:T(8,128)(2,1)S(1)} %collective-permute-done.14.refs_2_, bf16[32,1024]{1,0:T(8,128)(2,1)S(1)} %collective-permute-done.15.refs_3_), custom_call_target="tpu_custom_call" | custom-call | tf_op jit(solution)/shard_map/pallas_call | solution.py:362
  (5 shorter events, 0.1 us)
Async XLA Ops:
  1.3 10.4 %collective-permute-start.2 = (bf16[3,1536]{1,0:T(4,128)(2,1)S(1)}, bf16[3,1536]{1,0:T(4,128)(2,1)S(1)}, u32[]{:S(2)}, u32[]{:S(2)}) collective-permute-start(bf16[3,1536]{1,0:T(4,128)(2,1)S(1)} %get-tuple-element.33.refs_4_), channel_id=1, source_target_pairs={{0,6},{1,7},{2,4},{3,5},{4,2},{5,3},{6,0},{7,1},{8,14},{9,15},{10,... | collective-permute-start | bytes 27656 | tf_op jit(solution)/shard_map/ppermute | solution.py:30
  6.4 5.3 %collective-permute-start.1 = (bf16[3,1536]{1,0:T(4,128)(2,1)S(1)}, bf16[3,1536]{1,0:T(4,128)(2,1)S(1)}, u32[]{:S(2)}, u32[]{:S(2)}) collective-permute-start(bf16[3,1536]{1,0:T(4,128)(2,1)S(1)} %get-tuple-element.33.refs_4_), channel_id=1, source_target_pairs={{0,4},{1,5},{2,6},{3,7},{4,0},{5,1},{6,2},{7,3},{8,12},{9,13},{10,... | collective-permute-start | bytes 27656 | tf_op jit(solution)/shard_map/ppermute | solution.py:30
  6.4 5.3 %collective-permute-start = (bf16[3,1536]{1,0:T(4,128)(2,1)S(1)}, bf16[3,1536]{1,0:T(4,128)(2,1)S(1)}, u32[]{:S(2)}, u32[]{:S(2)}) collective-permute-start(bf16[3,1536]{1,0:T(4,128)(2,1)S(1)} %get-tuple-element.33.refs_4_), channel_id=1, source_target_pairs={{0,2},{1,3},{2,0},{3,1},{4,6},{5,7},{6,4},{7,5},{8,10},{9,11},{10,... | collective-permute-start | bytes 27656 | tf_op jit(solution)/shard_map/ppermute | solution.py:30
  7.8 16.8 %collective-permute-start.9 = (bf16[3,304,128]{2,1,0:T(8,128)(2,1)S(1)}, bf16[3,304,128]{2,1,0:T(8,128)(2,1)S(1)}, u32[]{:S(2)}, u32[]{:S(2)}) collective-permute-start(bf16[3,304,128]{2,1,0:T(8,128)(2,1)S(1)} %get-tuple-element.45), channel_id=1, source_target_pairs={{0,6},{1,7},{2,4},{3,5},{4,2},{5,3},{6,0},{7,1},{8,14},{9,15},{10,... | collective-permute-start | bytes 700424 | tf_op jit(solution)/shard_map/ppermute | solution.py:30
  11.6 10.9 %collective-permute-start.10 = (bf16[3,304,128]{2,1,0:T(8,128)(2,1)S(1)}, bf16[3,304,128]{2,1,0:T(8,128)(2,1)S(1)}, u32[]{:S(2)}, u32[]{:S(2)}) collective-permute-start(bf16[3,304,128]{2,1,0:T(8,128)(2,1)S(1)} %get-tuple-element.46), channel_id=1, source_target_pairs={{0,2},{1,3},{2,0},{3,1},{4,6},{5,7},{6,4},{7,5},{8,10},{9,11},{10,... | collective-permute-start | bytes 700424 | tf_op jit(solution)/shard_map/ppermute | solution.py:30
  11.7 5.0 %collective-permute-start.5 = (bf16[4,3,896]{2,1,0:T(4,128)(2,1)S(1)}, bf16[4,3,896]{2,1,0:T(4,128)(2,1)S(1)}, u32[]{:S(2)}, u32[]{:S(2)}) collective-permute-start(bf16[4,3,896]{2,1,0:T(4,128)(2,1)S(1)} %pad_maximum_fusion.refs_0_), channel_id=1, source_target_pairs={{0,24},{8,16},{16,8},{24,0},{1,25},{9,17},{17,9},{25,1},{2,26},{10... | collective-permute-start | bytes 64520 | tf_op jit(solution)/shard_map/ppermute | solution.py:30
  14.2 3.9 %collective-permute-start.3 = (bf16[4,3,896]{2,1,0:T(4,128)(2,1)S(1)}, bf16[4,3,896]{2,1,0:T(4,128)(2,1)S(1)}, u32[]{:S(2)}, u32[]{:S(2)}) collective-permute-start(bf16[4,3,896]{2,1,0:T(4,128)(2,1)S(1)} %pad_maximum_fusion.refs_0_), channel_id=1, source_target_pairs={{0,16},{8,24},{16,0},{24,8},{1,17},{9,25},{17,1},{25,9},{2,18},{10... | collective-permute-start | bytes 64520 | tf_op jit(solution)/shard_map/ppermute | solution.py:30
  14.7 3.9 %collective-permute-start.4 = (bf16[4,3,896]{2,1,0:T(4,128)(2,1)S(1)}, bf16[4,3,896]{2,1,0:T(4,128)(2,1)S(1)}, u32[]{:S(2)}, u32[]{:S(2)}) collective-permute-start(bf16[4,3,896]{2,1,0:T(4,128)(2,1)S(1)} %pad_maximum_fusion.refs_0_), channel_id=1, source_target_pairs={{0,8},{8,0},{16,24},{24,16},{1,9},{9,1},{17,25},{25,17},{2,10},{10... | collective-permute-start | bytes 64520 | tf_op jit(solution)/shard_map/ppermute | solution.py:30
  16.7 11.2 %collective-permute-start.8 = (bf16[3,152,128]{2,1,0:T(8,128)(2,1)S(1)}, bf16[3,152,128]{2,1,0:T(8,128)(2,1)S(1)}, u32[]{:S(2)}, u32[]{:S(2)}) collective-permute-start(bf16[3,152,128]{2,1,0:T(8,128)(2,1)S(1)} %get-tuple-element.42), channel_id=1, source_target_pairs={{0,4},{1,5},{2,6},{3,7},{4,0},{5,1},{6,2},{7,3},{8,12},{9,13},{10,... | collective-permute-start | bytes 350216 | tf_op jit(solution)/shard_map/ppermute | solution.py:30
  21.5 9.0 %collective-permute-start.6 = (bf16[3,152,128]{2,1,0:T(8,128)(2,1)S(1)}, bf16[3,152,128]{2,1,0:T(8,128)(2,1)S(1)}, u32[]{:S(2)}, u32[]{:S(2)}) collective-permute-start(bf16[3,152,128]{2,1,0:T(8,128)(2,1)S(1)} %get-tuple-element.40), channel_id=1, source_target_pairs={{0,5},{1,4},{2,7},{3,6},{4,1},{5,0},{6,3},{7,2},{8,13},{9,12},{10,... | collective-permute-start | bytes 350216 | tf_op jit(solution)/shard_map/ppermute | solution.py:30
  26.6 4.0 %collective-permute-start.11 = (bf16[32,1792]{1,0:T(8,128)(2,1)S(1)}, bf16[32,1792]{1,0:T(8,128)(2,1)S(1)}, u32[]{:S(2)}, u32[]{:S(2)}) collective-permute-start(bf16[32,1792]{1,0:T(8,128)(2,1)S(1)} %get-tuple-element.49), channel_id=1, source_target_pairs={{0,1},{1,0},{2,3},{3,2},{4,5},{5,4},{6,7},{7,6},{8,9},{9,8},{10,11... | collective-permute-start | bytes 344072 | tf_op jit(solution)/shard_map/ppermute | solution.py:30
  27.4 3.2 %collective-permute-start.12 = (bf16[32,1792]{1,0:T(8,128)(2,1)S(1)}, bf16[32,1792]{1,0:T(8,128)(2,1)S(1)}, u32[]{:S(2)}, u32[]{:S(2)}) collective-permute-start(bf16[32,1792]{1,0:T(8,128)(2,1)S(1)} %get-tuple-element.50), channel_id=1, source_target_pairs={{0,1},{1,0},{2,3},{3,2},{4,5},{5,4},{6,7},{7,6},{8,9},{9,8},{10,11... | collective-permute-start | bytes 344072 | tf_op jit(solution)/shard_map/ppermute | solution.py:30
  27.5 2.3 %collective-permute-start.7 = (f32[6,4224]{1,0:T(8,128)S(1)}, f32[6,4224]{1,0:T(8,128)S(1)}, u32[]{:S(2)}, u32[]{:S(2)}) collective-permute-start(f32[6,4224]{1,0:T(8,128)S(1)} %get-tuple-element.41), channel_id=1, source_target_pairs={{0,1},{1,0},{2,3},{3,2},{4,5},{5,4},{6,7},{7,6},{8,9},{9,8},{10,11... | collective-permute-start | bytes 304136 | tf_op jit(solution)/shard_map/ppermute | solution.py:30
  32.6 7.2 %collective-permute-start.15 = (bf16[32,1024]{1,0:T(8,128)(2,1)S(1)}, bf16[32,1024]{1,0:T(8,128)(2,1)S(1)}, u32[]{:S(2)}, u32[]{:S(2)}) collective-permute-start(bf16[32,1024]{1,0:T(8,128)(2,1)S(1)} %get-tuple-element.54), channel_id=1, source_target_pairs={{0,24},{8,16},{16,8},{24,0},{1,25},{9,17},{17,9},{25,1},{2,26},{10... | collective-permute-start | bytes 196616 | tf_op jit(solution)/shard_map/ppermute | solution.py:30
  35.3 4.2 %collective-permute-start.13 = (bf16[32,896]{1,0:T(8,128)(2,1)S(1)}, bf16[32,896]{1,0:T(8,128)(2,1)S(1)}, u32[]{:S(2)}, u32[]{:S(2)}) collective-permute-start(bf16[32,896]{1,0:T(8,128)(2,1)S(1)} %get-tuple-element.52), channel_id=1, source_target_pairs={{0,8},{8,0},{16,24},{24,16},{1,9},{9,1},{17,25},{25,17},{2,10},{10... | collective-permute-start | bytes 172040 | tf_op jit(solution)/shard_map/ppermute | solution.py:30
  35.6 4.2 %collective-permute-start.14 = (bf16[32,896]{1,0:T(8,128)(2,1)S(1)}, bf16[32,896]{1,0:T(8,128)(2,1)S(1)}, u32[]{:S(2)}, u32[]{:S(2)}) collective-permute-start(bf16[32,896]{1,0:T(8,128)(2,1)S(1)} %get-tuple-element.53), channel_id=1, source_target_pairs={{0,16},{8,24},{16,0},{24,8},{1,17},{9,25},{17,1},{25,9},{2,18},{10... | collective-permute-start | bytes 172040 | tf_op jit(solution)/shard_map/ppermute | solution.py:30

commit v8 on v7

--- a/solution.py
+++ b/solution.py
@@ -388,7 +388,9 @@
     waves = [wave] + [swap_with(wave, "sta", 2 * offset) for offset in range(1, chips)]
     offsets = [0] + between
     targets = [(offset, None) for offset in offsets] + [(final, 0), (final, 1)]
-    messages = pack(targets, [rows] * len(offsets) + [own] * 2, tpl, mask)
+    messages = pack(targets[1:-2], [rows] * len(between), tpl, mask)
+    rest = pack(targets[:1] + targets[-2:], [rows, own, own], tpl, mask)
+    messages = [rest[0], *messages, *rest[1:]]
     pieces = {offset: swap_with(messages[1 + i], "sta", 2 * offset) for i, offset in enumerate(between)}
     stacked = jnp.stack([part[:, :samples] for part in waves])
     shards = [stacked] + [swap_with(stacked, "tm", offset) for offset in range(1, tm_count)]

time: 40.8 us -> 40.4 us (level)
  waiting for transfers between devices: 7.33 us -> 5.87 us
  starting transfers between devices: 19.3 us -> 20.3 us
    ppermute x16, waiting for transfers between devices: 7.33 us -> 5.87 us  [swap_with(): return lax.ppermute(x, axis, [(i, i ^ offset) for i in range(size)])]
    ppermute x16, starting transfers between devices: 19.3 us -> 20.3 us  [swap_with(): return lax.ppermute(x, axis, [(i, i ^ offset) for i in range(size)])]
  transfers between devices with their start and end apart: 16 -> 16, of which waited for: 7 -> 6; matrix products, arithmetic and copies ran while one was open for 0% -> 0% of each run, Pallas kernels for 24% -> 24%
where the time goes in v8:
time: 40.4 us; the launch traced here: 40.2 us
  starting transfers between devices  20.3 us (50%)
  Pallas kernels  13.8 us (34%)
  waiting for transfers between devices  5.87 us (15%)
    ppermute x16, starting transfers between devices, swap_with(): return lax.ppermute(x, axis, [(i, i ^ offset) for i in range(size)])  20.3 us
    pallas_call x4, Pallas kernels, later(): pl.pallas_call(kernel, out_shape=out_shape, in_specs=[VMEM] * len(inputs)...  8 us
    ppermute x16, waiting for transfers between devices, swap_with(): return lax.ppermute(x, axis, [(i, i ^ offset) for i in range(size)])  5.87 us
    pallas_call x1, Pallas kernels, first(): pl.pallas_call(functools.partial(first_kernel, len(shards), chips, rows,...  2.92 us
    pallas_call x1, Pallas kernels, join(): pl.pallas_call(join_kernel, out_shape=[jax.ShapeDtypeStruct((wave.shape[0...  1.25 us
  transfers between devices with their start and end apart: 16, of which 6 were waited for; matrix products, arithmetic and copies ran while one was open for 0% of the time, Pallas kernels for 24%

profile of v8, /device:TPU:0, one launch (start us, length us, event | category | flops | bytes accessed | tf_op | source)
XLA Modules:
  0.0 40.2 jit_solution(4208336028827480923)
XLA Ops:
  0.0 1.2 %shard_map.46 = (bf16[3,1536]{1,0:T(4,128)(2,1)S(1)}, bf16[3,600,256]{2,1,0:T(8,128)(2,1)S(1)}, s32[1,256]{1,0:T(1,128)S(1)}) custom-call(bf16[3,896]{1,0:T(4,128)(2,1)} %bitcast.15, bf16[3,599]{1,0:T(4,128)(2,1)} %bitcast.16, bf16[3,600,256]{2,1,0:T(8,128)(2,1)} %bitcast.14, s32[1,256]{1,0:T(1,128)} %bitcast.17), custom_call_target="tpu_custom_call" | custom-call | flops 1 | bytes 1 | tf_op jit(solution)/shard_map/pallas_call | solution.py:51
  1.3 5.1 %collective-permute-start.2 = (bf16[3,1536]{1,0:T(4,128)(2,1)S(1)}, bf16[3,1536]{1,0:T(4,128)(2,1)S(1)}, u32[]{:S(2)}, u32[]{:S(2)}) collective-permute-start(bf16[3,1536]{1,0:T(4,128)(2,1)S(1)} %get-tuple-element.33.refs_4_), channel_id=1, source_target_pairs={{0,6},{1,7},{2,4},{3,5},{4,2},{5,3},{6,0},{7,1},{8,14},{9,15},{10,... | collective-permute-start | bytes 27656 | tf_op jit(solution)/shard_map/ppermute | solution.py:30
  6.4 0.0 collective-permute-start.1
  6.4 0.6 %collective-permute-start = (bf16[3,1536]{1,0:T(4,128)(2,1)S(1)}, bf16[3,1536]{1,0:T(4,128)(2,1)S(1)}, u32[]{:S(2)}, u32[]{:S(2)}) collective-permute-start(bf16[3,1536]{1,0:T(4,128)(2,1)S(1)} %get-tuple-element.33.refs_4_), channel_id=1, source_target_pairs={{0,2},{1,3},{2,0},{3,1},{4,6},{5,7},{6,4},{7,5},{8,10},{9,11},{10,... | collective-permute-start | bytes 27656 | tf_op jit(solution)/shard_map/ppermute | solution.py:30
  7.0 0.3 shard_map.49
  7.3 3.8 %collective-permute-start.9 = (bf16[3,304,128]{2,1,0:T(8,128)(2,1)S(1)}, bf16[3,304,128]{2,1,0:T(8,128)(2,1)S(1)}, u32[]{:S(2)}, u32[]{:S(2)}) collective-permute-start(bf16[3,304,128]{2,1,0:T(8,128)(2,1)S(1)} %get-tuple-element.45), channel_id=1, source_target_pairs={{0,6},{1,7},{2,4},{3,5},{4,2},{5,3},{6,0},{7,1},{8,14},{9,15},{10,... | collective-permute-start | bytes 700424 | tf_op jit(solution)/shard_map/ppermute | solution.py:30
  11.2 0.0 collective-permute-start.10
  11.2 0.0 collective-permute-done.2.refs_7_
  11.2 0.0 collective-permute-done.1.refs_6_
  11.2 0.0 collective-permute-done.refs_5_
  11.3 2.5 %collective-permute-start.5 = (bf16[4,3,896]{2,1,0:T(4,128)(2,1)S(1)}, bf16[4,3,896]{2,1,0:T(4,128)(2,1)S(1)}, u32[]{:S(2)}, u32[]{:S(2)}) collective-permute-start(bf16[4,3,896]{2,1,0:T(4,128)(2,1)S(1)} %pad_maximum_fusion.refs_0_), channel_id=1, source_target_pairs={{0,24},{8,16},{16,8},{24,0},{1,25},{9,17},{17,9},{25,1},{2,26},{10... | collective-permute-start | bytes 64520 | tf_op jit(solution)/shard_map/ppermute | solution.py:30
  13.8 0.5 %collective-permute-start.3 = (bf16[4,3,896]{2,1,0:T(4,128)(2,1)S(1)}, bf16[4,3,896]{2,1,0:T(4,128)(2,1)S(1)}, u32[]{:S(2)}, u32[]{:S(2)}) collective-permute-start(bf16[4,3,896]{2,1,0:T(4,128)(2,1)S(1)} %pad_maximum_fusion.refs_0_), channel_id=1, source_target_pairs={{0,16},{8,24},{16,0},{24,8},{1,17},{9,25},{17,1},{25,9},{2,18},{10... | collective-permute-start | bytes 64520 | tf_op jit(solution)/shard_map/ppermute | solution.py:30
  14.3 0.5 %collective-permute-start.4 = (bf16[4,3,896]{2,1,0:T(4,128)(2,1)S(1)}, bf16[4,3,896]{2,1,0:T(4,128)(2,1)S(1)}, u32[]{:S(2)}, u32[]{:S(2)}) collective-permute-start(bf16[4,3,896]{2,1,0:T(4,128)(2,1)S(1)} %pad_maximum_fusion.refs_0_), channel_id=1, source_target_pairs={{0,8},{8,0},{16,24},{24,16},{1,9},{9,1},{17,25},{25,17},{2,10},{10... | collective-permute-start | bytes 64520 | tf_op jit(solution)/shard_map/ppermute | solution.py:30
  14.8 0.5 %shard_map.47 = (bf16[3,304,128]{2,1,0:T(8,128)(2,1)S(1)}, bf16[3,152,128]{2,1,0:T(8,128)(2,1)S(1)}, bf16[3,152,128]{2,1,0:T(8,128)(2,1)S(1)}) custom-call(bf16[3,600,256]{2,1,0:T(8,128)(2,1)S(1)} %get-tuple-element.30.tpl_ref, s32[1,256]{1,0:T(1,128)S(1)} %get-tuple-element.31.mask_ref), custom_call_target="tpu_custom_call" | custom-call | flops 1 | bytes 1 | tf_op jit(solution)/shard_map/pallas_call | solution.py:101
  15.3 0.9 %collective-permute-done.5.refs_3_ = bf16[4,3,896]{2,1,0:T(4,128)(2,1)S(1)} collective-permute-done((bf16[4,3,896]{2,1,0:T(4,128)(2,1)S(1)}, bf16[4,3,896]{2,1,0:T(4,128)(2,1)S(1)}, u32[]{:S(2)}, u32[]{:S(2)}) %collective-permute-start.5) | collective-permute-done | bytes 21536 | tf_op jit(solution)/shard_map/ppermute | solution.py:30
  16.2 1.8 %collective-permute-start.8 = (bf16[3,152,128]{2,1,0:T(8,128)(2,1)S(1)}, bf16[3,152,128]{2,1,0:T(8,128)(2,1)S(1)}, u32[]{:S(2)}, u32[]{:S(2)}) collective-permute-start(bf16[3,152,128]{2,1,0:T(8,128)(2,1)S(1)} %get-tuple-element.42), channel_id=1, source_target_pairs={{0,4},{1,5},{2,6},{3,7},{4,0},{5,1},{6,2},{7,3},{8,12},{9,13},{10,... | collective-permute-start | bytes 350216 | tf_op jit(solution)/shard_map/ppermute | solution.py:30
  18.0 0.0 collective-permute-done.3.refs_2_
  18.0 0.1 collective-permute-done.4.refs_1_
  18.2 2.9 %shard_map.48 = (f32[12,4224]{1,0:T(8,128)S(1)}, f32[12,3584]{1,0:T(8,128)S(1)}, f32[6,4224]{1,0:T(8,128)S(1)}, f32[64,3584]{1,0:T(8,128)S(1)}) custom-call(bf16[3,304,128]{2,1,0:T(8,128)(2,1)S(1)} %get-tuple-element.35.tpl_ref, bf16[4,3,896]{2,1,0:T(4,128)(2,1)S(1)} %pad_maximum_fusion.refs_0_, bf16[4,3,896]{2,1,0:T(4,128)(2,1)S(1)} %collective-permute-done.4.refs_1_, ...), custom_call_target="tpu_custom_call" | custom-call | flops 1 | bytes 1 | tf_op jit(solution)/shard_map/pallas_call | solution.py:316
  21.1 0.1 collective-permute-start.6
  21.2 0.8 %collective-permute-done.10.tpl_ref = bf16[3,304,128]{2,1,0:T(8,128)(2,1)S(1)} collective-permute-done((bf16[3,304,128]{2,1,0:T(8,128)(2,1)S(1)}, bf16[3,304,128]{2,1,0:T(8,128)(2,1)S(1)}, u32[]{:S(2)}, u32[]{:S(2)}) %collective-permute-start.10) | collective-permute-done | bytes 233504 | tf_op jit(solution)/shard_map/ppermute | solution.py:30
  22.0 2.1 %shard_map.50.acc_ref = f32[64,3584]{1,0:T(8,128)S(1)} custom-call(bf16[3,304,128]{2,1,0:T(8,128)(2,1)S(1)} %collective-permute-done.10.tpl_ref, f32[12,4224]{1,0:T(8,128)S(1)} %get-tuple-element.43.ext_ref, f32[12,3584]{1,0:T(8,128)S(1)} %get-tuple-element.44.inv_ref, f32[64,3584]{1,0:T(8,128)S(1)} %get-tuple-element.47.acc_ref), custom_call_target="tpu_custom_call" | custom-call | flops 500000000 | bytes 1 | tf_op jit(solution)/shard_map/pallas_call | solution.py:335
  24.1 0.0 collective-permute-done.9.tpl_ref
  24.1 2.1 %shard_map.51 = (f32[32,3584]{1,0:T(8,128)S(1)}, bf16[32,1792]{1,0:T(8,128)(2,1)S(1)}, bf16[32,1792]{1,0:T(8,128)(2,1)S(1)}) custom-call(bf16[3,304,128]{2,1,0:T(8,128)(2,1)S(1)} %collective-permute-done.9.tpl_ref, f32[12,4224]{1,0:T(8,128)S(1)} %get-tuple-element.43.ext_ref, f32[12,3584]{1,0:T(8,128)S(1)} %get-tuple-element.44.inv_ref, ...), custom_call_target="tpu_custom_call" | custom-call | flops 1 | bytes 1 | tf_op jit(solution)/shard_map/pallas_call | solution.py:335
  26.2 1.3 %collective-permute-start.11 = (bf16[32,1792]{1,0:T(8,128)(2,1)S(1)}, bf16[32,1792]{1,0:T(8,128)(2,1)S(1)}, u32[]{:S(2)}, u32[]{:S(2)}) collective-permute-start(bf16[32,1792]{1,0:T(8,128)(2,1)S(1)} %get-tuple-element.49), channel_id=1, source_target_pairs={{0,1},{1,0},{2,3},{3,2},{4,5},{5,4},{6,7},{7,6},{8,9},{9,8},{10,11... | collective-permute-start | bytes 344072 | tf_op jit(solution)/shard_map/ppermute | solution.py:30
  27.4 0.1 collective-permute-start.12
  27.5 0.4 %collective-permute-start.7 = (f32[6,4224]{1,0:T(8,128)S(1)}, f32[6,4224]{1,0:T(8,128)S(1)}, u32[]{:S(2)}, u32[]{:S(2)}) collective-permute-start(f32[6,4224]{1,0:T(8,128)S(1)} %get-tuple-element.41), channel_id=1, source_target_pairs={{0,1},{1,0},{2,3},{3,2},{4,5},{5,4},{6,7},{7,6},{8,9},{9,8},{10,11... | collective-permute-start | bytes 304136 | tf_op jit(solution)/shard_map/ppermute | solution.py:30
  27.9 0.0 collective-permute-done.8.tpl_ref
  27.9 1.9 %shard_map.52.acc_ref = f32[32,3584]{1,0:T(8,128)S(1)} custom-call(bf16[3,152,128]{2,1,0:T(8,128)(2,1)S(1)} %collective-permute-done.8.tpl_ref, f32[12,4224]{1,0:T(8,128)S(1)} %get-tuple-element.43.ext_ref, f32[12,3584]{1,0:T(8,128)S(1)} %get-tuple-element.44.inv_ref, f32[32,3584]{1,0:T(8,128)S(1)} %get-tuple-element.48.acc_ref), custom_call_target="tpu_custom_call" | custom-call | flops 500000000 | bytes 1 | tf_op jit(solution)/shard_map/pallas_call | solution.py:335
  29.8 0.0 collective-permute-done.7.cross_ref
  29.8 0.3 collective-permute-done.6.tpl_ref
  30.1 0.0 collective-permute-done.11.early_ref
  30.1 0.0 collective-permute-done.12.late_ref
  30.1 2.0 %shard_map.53 = (f32[32,896]{1,0:T(8,128)S(1)}, bf16[32,896]{1,0:T(8,128)(2,1)S(1)}, bf16[32,896]{1,0:T(8,128)(2,1)S(1)}, bf16[32,1024]{1,0:T(8,128)(2,1)S(1)}) custom-call(bf16[3,152,128]{2,1,0:T(8,128)(2,1)S(1)} %collective-permute-done.6.tpl_ref, f32[6,4224]{1,0:T(8,128)S(1)} %collective-permute-done.7.cross_ref, f32[32,3584]{1,0:T(8,128)S(1)} %shard_map.52.acc_ref, ...), custom_call_target="tpu_custom_call" | custom-call | flops 1 | bytes 1 | tf_op jit(solution)/shard_map/pallas_call | solution.py:335
  32.1 2.4 %collective-permute-start.15 = (bf16[32,1024]{1,0:T(8,128)(2,1)S(1)}, bf16[32,1024]{1,0:T(8,128)(2,1)S(1)}, u32[]{:S(2)}, u32[]{:S(2)}) collective-permute-start(bf16[32,1024]{1,0:T(8,128)(2,1)S(1)} %get-tuple-element.54), channel_id=1, source_target_pairs={{0,24},{8,16},{16,8},{24,0},{1,25},{9,17},{17,9},{25,1},{2,26},{10... | collective-permute-start | bytes 196616 | tf_op jit(solution)/shard_map/ppermute | solution.py:30
  34.5 0.7 %collective-permute-start.13 = (bf16[32,896]{1,0:T(8,128)(2,1)S(1)}, bf16[32,896]{1,0:T(8,128)(2,1)S(1)}, u32[]{:S(2)}, u32[]{:S(2)}) collective-permute-start(bf16[32,896]{1,0:T(8,128)(2,1)S(1)} %get-tuple-element.52), channel_id=1, source_target_pairs={{0,8},{8,0},{16,24},{24,16},{1,9},{9,1},{17,25},{25,17},{2,10},{10... | collective-permute-start | bytes 172040 | tf_op jit(solution)/shard_map/ppermute | solution.py:30
  35.2 0.5 %collective-permute-start.14 = (bf16[32,896]{1,0:T(8,128)(2,1)S(1)}, bf16[32,896]{1,0:T(8,128)(2,1)S(1)}, u32[]{:S(2)}, u32[]{:S(2)}) collective-permute-start(bf16[32,896]{1,0:T(8,128)(2,1)S(1)} %get-tuple-element.53), channel_id=1, source_target_pairs={{0,16},{8,24},{16,0},{24,8},{1,17},{9,25},{17,1},{25,9},{2,18},{10... | collective-permute-start | bytes 172040 | tf_op jit(solution)/shard_map/ppermute | solution.py:30
  35.7 3.0 %collective-permute-done.13.refs_1_ = bf16[32,896]{1,0:T(8,128)(2,1)S(1)} collective-permute-done((bf16[32,896]{1,0:T(8,128)(2,1)S(1)}, bf16[32,896]{1,0:T(8,128)(2,1)S(1)}, u32[]{:S(2)}, u32[]{:S(2)}) %collective-permute-start.13) | collective-permute-done | bytes 57376 | tf_op jit(solution)/shard_map/ppermute | solution.py:30
  38.7 0.7 %collective-permute-done.14.refs_2_ = bf16[32,896]{1,0:T(8,128)(2,1)S(1)} collective-permute-done((bf16[32,896]{1,0:T(8,128)(2,1)S(1)}, bf16[32,896]{1,0:T(8,128)(2,1)S(1)}, u32[]{:S(2)}, u32[]{:S(2)}) %collective-permute-start.14) | collective-permute-done | bytes 57376 | tf_op jit(solution)/shard_map/ppermute | solution.py:30
  39.4 0.0 collective-permute-done.15.refs_3_
  39.4 0.8 %shard_map.54 = f32[4,32,896]{2,1,0:T(8,128)} custom-call(f32[32,896]{1,0:T(8,128)S(1)} %get-tuple-element.51.refs_0_, bf16[32,896]{1,0:T(8,128)(2,1)S(1)} %collective-permute-done.13.refs_1_, bf16[32,896]{1,0:T(8,128)(2,1)S(1)} %collective-permute-done.14.refs_2_, bf16[32,1024]{1,0:T(8,128)(2,1)S(1)} %collective-permute-done.15.refs_3_), custom_call_target="tpu_custom_call" | custom-call | tf_op jit(solution)/shard_map/pallas_call | solution.py:362
  (5 shorter events, 0.1 us)
Async XLA Ops:
  1.3 9.9 %collective-permute-start.2 = (bf16[3,1536]{1,0:T(4,128)(2,1)S(1)}, bf16[3,1536]{1,0:T(4,128)(2,1)S(1)}, u32[]{:S(2)}, u32[]{:S(2)}) collective-permute-start(bf16[3,1536]{1,0:T(4,128)(2,1)S(1)} %get-tuple-element.33.refs_4_), channel_id=1, source_target_pairs={{0,6},{1,7},{2,4},{3,5},{4,2},{5,3},{6,0},{7,1},{8,14},{9,15},{10,... | collective-permute-start | bytes 27656 | tf_op jit(solution)/shard_map/ppermute | solution.py:30
  6.4 4.8 %collective-permute-start.1 = (bf16[3,1536]{1,0:T(4,128)(2,1)S(1)}, bf16[3,1536]{1,0:T(4,128)(2,1)S(1)}, u32[]{:S(2)}, u32[]{:S(2)}) collective-permute-start(bf16[3,1536]{1,0:T(4,128)(2,1)S(1)} %get-tuple-element.33.refs_4_), channel_id=1, source_target_pairs={{0,4},{1,5},{2,6},{3,7},{4,0},{5,1},{6,2},{7,3},{8,12},{9,13},{10,... | collective-permute-start | bytes 27656 | tf_op jit(solution)/shard_map/ppermute | solution.py:30
  6.4 4.8 %collective-permute-start = (bf16[3,1536]{1,0:T(4,128)(2,1)S(1)}, bf16[3,1536]{1,0:T(4,128)(2,1)S(1)}, u32[]{:S(2)}, u32[]{:S(2)}) collective-permute-start(bf16[3,1536]{1,0:T(4,128)(2,1)S(1)} %get-tuple-element.33.refs_4_), channel_id=1, source_target_pairs={{0,2},{1,3},{2,0},{3,1},{4,6},{5,7},{6,4},{7,5},{8,10},{9,11},{10,... | collective-permute-start | bytes 27656 | tf_op jit(solution)/shard_map/ppermute | solution.py:30
  7.3 16.7 %collective-permute-start.9 = (bf16[3,304,128]{2,1,0:T(8,128)(2,1)S(1)}, bf16[3,304,128]{2,1,0:T(8,128)(2,1)S(1)}, u32[]{:S(2)}, u32[]{:S(2)}) collective-permute-start(bf16[3,304,128]{2,1,0:T(8,128)(2,1)S(1)} %get-tuple-element.45), channel_id=1, source_target_pairs={{0,6},{1,7},{2,4},{3,5},{4,2},{5,3},{6,0},{7,1},{8,14},{9,15},{10,... | collective-permute-start | bytes 700424 | tf_op jit(solution)/shard_map/ppermute | solution.py:30
  11.2 10.8 %collective-permute-start.10 = (bf16[3,304,128]{2,1,0:T(8,128)(2,1)S(1)}, bf16[3,304,128]{2,1,0:T(8,128)(2,1)S(1)}, u32[]{:S(2)}, u32[]{:S(2)}) collective-permute-start(bf16[3,304,128]{2,1,0:T(8,128)(2,1)S(1)} %get-tuple-element.46), channel_id=1, source_target_pairs={{0,2},{1,3},{2,0},{3,1},{4,6},{5,7},{6,4},{7,5},{8,10},{9,11},{10,... | collective-permute-start | bytes 700424 | tf_op jit(solution)/shard_map/ppermute | solution.py:30
  11.3 4.9 %collective-permute-start.5 = (bf16[4,3,896]{2,1,0:T(4,128)(2,1)S(1)}, bf16[4,3,896]{2,1,0:T(4,128)(2,1)S(1)}, u32[]{:S(2)}, u32[]{:S(2)}) collective-permute-start(bf16[4,3,896]{2,1,0:T(4,128)(2,1)S(1)} %pad_maximum_fusion.refs_0_), channel_id=1, source_target_pairs={{0,24},{8,16},{16,8},{24,0},{1,25},{9,17},{17,9},{25,1},{2,26},{10... | collective-permute-start | bytes 64520 | tf_op jit(solution)/shard_map/ppermute | solution.py:30
  13.8 4.2 %collective-permute-start.3 = (bf16[4,3,896]{2,1,0:T(4,128)(2,1)S(1)}, bf16[4,3,896]{2,1,0:T(4,128)(2,1)S(1)}, u32[]{:S(2)}, u32[]{:S(2)}) collective-permute-start(bf16[4,3,896]{2,1,0:T(4,128)(2,1)S(1)} %pad_maximum_fusion.refs_0_), channel_id=1, source_target_pairs={{0,16},{8,24},{16,0},{24,8},{1,17},{9,25},{17,1},{25,9},{2,18},{10... | collective-permute-start | bytes 64520 | tf_op jit(solution)/shard_map/ppermute | solution.py:30
  14.3 3.9 %collective-permute-start.4 = (bf16[4,3,896]{2,1,0:T(4,128)(2,1)S(1)}, bf16[4,3,896]{2,1,0:T(4,128)(2,1)S(1)}, u32[]{:S(2)}, u32[]{:S(2)}) collective-permute-start(bf16[4,3,896]{2,1,0:T(4,128)(2,1)S(1)} %pad_maximum_fusion.refs_0_), channel_id=1, source_target_pairs={{0,8},{8,0},{16,24},{24,16},{1,9},{9,1},{17,25},{25,17},{2,10},{10... | collective-permute-start | bytes 64520 | tf_op jit(solution)/shard_map/ppermute | solution.py:30
  16.2 11.7 %collective-permute-start.8 = (bf16[3,152,128]{2,1,0:T(8,128)(2,1)S(1)}, bf16[3,152,128]{2,1,0:T(8,128)(2,1)S(1)}, u32[]{:S(2)}, u32[]{:S(2)}) collective-permute-start(bf16[3,152,128]{2,1,0:T(8,128)(2,1)S(1)} %get-tuple-element.42), channel_id=1, source_target_pairs={{0,4},{1,5},{2,6},{3,7},{4,0},{5,1},{6,2},{7,3},{8,12},{9,13},{10,... | collective-permute-start | bytes 350216 | tf_op jit(solution)/shard_map/ppermute | solution.py:30
  21.1 9.0 %collective-permute-start.6 = (bf16[3,152,128]{2,1,0:T(8,128)(2,1)S(1)}, bf16[3,152,128]{2,1,0:T(8,128)(2,1)S(1)}, u32[]{:S(2)}, u32[]{:S(2)}) collective-permute-start(bf16[3,152,128]{2,1,0:T(8,128)(2,1)S(1)} %get-tuple-element.40), channel_id=1, source_target_pairs={{0,5},{1,4},{2,7},{3,6},{4,1},{5,0},{6,3},{7,2},{8,13},{9,12},{10,... | collective-permute-start | bytes 350216 | tf_op jit(solution)/shard_map/ppermute | solution.py:30
  26.2 4.0 %collective-permute-start.11 = (bf16[32,1792]{1,0:T(8,128)(2,1)S(1)}, bf16[32,1792]{1,0:T(8,128)(2,1)S(1)}, u32[]{:S(2)}, u32[]{:S(2)}) collective-permute-start(bf16[32,1792]{1,0:T(8,128)(2,1)S(1)} %get-tuple-element.49), channel_id=1, source_target_pairs={{0,1},{1,0},{2,3},{3,2},{4,5},{5,4},{6,7},{7,6},{8,9},{9,8},{10,11... | collective-permute-start | bytes 344072 | tf_op jit(solution)/shard_map/ppermute | solution.py:30
  27.4 2.7 %collective-permute-start.12 = (bf16[32,1792]{1,0:T(8,128)(2,1)S(1)}, bf16[32,1792]{1,0:T(8,128)(2,1)S(1)}, u32[]{:S(2)}, u32[]{:S(2)}) collective-permute-start(bf16[32,1792]{1,0:T(8,128)(2,1)S(1)} %get-tuple-element.50), channel_id=1, source_target_pairs={{0,1},{1,0},{2,3},{3,2},{4,5},{5,4},{6,7},{7,6},{8,9},{9,8},{10,11... | collective-permute-start | bytes 344072 | tf_op jit(solution)/shard_map/ppermute | solution.py:30
  27.5 2.3 %collective-permute-start.7 = (f32[6,4224]{1,0:T(8,128)S(1)}, f32[6,4224]{1,0:T(8,128)S(1)}, u32[]{:S(2)}, u32[]{:S(2)}) collective-permute-start(f32[6,4224]{1,0:T(8,128)S(1)} %get-tuple-element.41), channel_id=1, source_target_pairs={{0,1},{1,0},{2,3},{3,2},{4,5},{5,4},{6,7},{7,6},{8,9},{9,8},{10,11... | collective-permute-start | bytes 304136 | tf_op jit(solution)/shard_map/ppermute | solution.py:30
  32.1 7.2 %collective-permute-start.15 = (bf16[32,1024]{1,0:T(8,128)(2,1)S(1)}, bf16[32,1024]{1,0:T(8,128)(2,1)S(1)}, u32[]{:S(2)}, u32[]{:S(2)}) collective-permute-start(bf16[32,1024]{1,0:T(8,128)(2,1)S(1)} %get-tuple-element.54), channel_id=1, source_target_pairs={{0,24},{8,16},{16,8},{24,0},{1,25},{9,17},{17,9},{25,1},{2,26},{10... | collective-permute-start | bytes 196616 | tf_op jit(solution)/shard_map/ppermute | solution.py:30
  34.5 4.2 %collective-permute-start.13 = (bf16[32,896]{1,0:T(8,128)(2,1)S(1)}, bf16[32,896]{1,0:T(8,128)(2,1)S(1)}, u32[]{:S(2)}, u32[]{:S(2)}) collective-permute-start(bf16[32,896]{1,0:T(8,128)(2,1)S(1)} %get-tuple-element.52), channel_id=1, source_target_pairs={{0,8},{8,0},{16,24},{24,16},{1,9},{9,1},{17,25},{25,17},{2,10},{10... | collective-permute-start | bytes 172040 | tf_op jit(solution)/shard_map/ppermute | solution.py:30
  35.2 4.2 %collective-permute-start.14 = (bf16[32,896]{1,0:T(8,128)(2,1)S(1)}, bf16[32,896]{1,0:T(8,128)(2,1)S(1)}, u32[]{:S(2)}, u32[]{:S(2)}) collective-permute-start(bf16[32,896]{1,0:T(8,128)(2,1)S(1)} %get-tuple-element.53), channel_id=1, source_target_pairs={{0,16},{8,24},{16,0},{24,8},{1,17},{9,25},{17,1},{25,9},{2,18},{10... | collective-permute-start | bytes 172040 | tf_op jit(solution)/shard_map/ppermute | solution.py:30
